TPU v7x, 32 devices: a whole 2x2x4 slice. The times are simulated.
32 devices in a mesh: shot: 4 (over y, x), slab: 8 (over z, core).
Axes of the slice: x: 2, y: 2, z: 4, core: 2. Of those that a mesh axis runs over, the one named last changes fastest.
Arguments:
- source_field: bfloat16 [4, 2, 1024, 2, 1024], P('shot', None, 'slab'), may hold values from -6 to 6
- residual_data: bfloat16 [4, 2, 1024, 2, 1024], P('shot', None, 'slab'), may hold values from -6 to 6
- receiver_lines: int32 [4, 1024], P('shot'), may hold values 0 or 1
- shot_positions: int32 [4, 2], P('shot'), may hold values from 0 to 1023
- slowness: float32 [2, 1024, 1024], P(None, 'slab'), may hold values from 0.5 to 2
- frequency: float32 [2], replicated, may hold values from 0.5 to 4
- line_inverse: bfloat16 [2, 2, 2, 512, 512], replicated, may hold values from -0.4 to 1.2
- coupling: float32 [2, 2], replicated, may hold values from -0.6 to 0.6
Outputs:
- gradient: float32 [2, 1024, 1024], P(None, 'slab', 'shot')
All inputs are finite; a program needn't handle non-finite values. No bound on the sum of `receiver_lines` on one device may be relied on, other than what follows from the above.
Results may differ from a plain program's by a relative error of at most 0.0082.
Values may be sent and summed in bfloat16 or wider, within the bound.
No kernel may reach another device: no remote copies, remote signals or barrier semaphores. Data moves between devices by JAX's collectives and lax.ppermute only.
A program may use at most 64 MiB of HBM per device.

v0:
```python
from functools import partial

import jax
import jax.numpy as jnp
from jax import lax
from jax.experimental import pallas as pl
from jax.experimental.pallas import tpu as pltpu
from jax.sharding import PartitionSpec as P

NX = 1024
STEPS = 2


def pick_index(values, position, axis_number, keep=False):
    return lax.index_in_dim(values, position, axis_number, keepdims=keep)


def line_solve(wavefield, line_inverse, coupling, line_dim):
    in_shape = wavefield.shape
    freq_count = line_inverse.shape[0]
    blocks = line_inverse.shape[2]
    block_len = line_inverse.shape[3]
    real_blocks = line_inverse[:, 0]
    imag_blocks = line_inverse[:, 1]
    if line_dim == 5:
        pieces = wavefield.reshape(in_shape[:5] + (blocks, block_len))
        formula = "shfxcgj,fgij->shfxcgi"
    else:
        pieces = wavefield.reshape(in_shape[:3] + (blocks, block_len, in_shape[4] * in_shape[5]))
        formula = "shfgjz,fgij->shfgiz"
    with_real = jnp.einsum(formula, pieces, real_blocks, preferred_element_type=jnp.float32)
    with_imag = jnp.einsum(formula, pieces, imag_blocks, preferred_element_type=jnp.float32)
    if line_dim == 5:
        comp_axis, block_axis, cell_axis = (4, 4, 4)
        col_shape = (1, 1, freq_count, 1, block_len)
    else:
        with_real = with_real.reshape(in_shape[:3] + (blocks, block_len, in_shape[4], in_shape[5]))
        with_imag = with_imag.reshape(in_shape[:3] + (blocks, block_len, in_shape[4], in_shape[5]))
        comp_axis, block_axis, cell_axis = (5, 3, 3)
        col_shape = (1, 1, freq_count, block_len, 1)
    signs_six = jnp.array([1.0, -1.0], jnp.float32).reshape(1, 2, 1, 1, 1, 1)
    signs_five = jnp.array([1.0, -1.0], jnp.float32).reshape(1, 2, 1, 1, 1)
    u_real = pick_index(with_real, 0, comp_axis) - signs_six * pick_index(with_imag, 1, comp_axis)
    u_imag = pick_index(with_real, 1, comp_axis) + signs_six * pick_index(with_imag, 0, comp_axis)
    coup_real = coupling[:, 0].reshape(1, 1, freq_count, 1, 1)
    coup_imag = coupling[:, 1].reshape(1, 1, freq_count, 1, 1)

    def factor(block_index, column):
        col_real = line_inverse[:, 0, block_index, :, column].astype(jnp.float32).reshape(col_shape)
        col_imag = line_inverse[:, 1, block_index, :, column].astype(jnp.float32).reshape(col_shape)
        return (
            coup_real * col_real - coup_imag * col_imag,
            signs_five * (coup_imag * col_real + coup_real * col_imag),
        )

    fwd_real = [pick_index(u_real, 0, block_axis)]
    fwd_imag = [pick_index(u_imag, 0, block_axis)]
    block_index = 1
    mult_real, mult_imag = factor(block_index, 0)
    prev_real = pick_index(fwd_real[-1], block_len - 1, cell_axis, True)
    prev_imag = pick_index(fwd_imag[-1], block_len - 1, cell_axis, True)
    fwd_real.append(
        pick_index(u_real, block_index, block_axis) + mult_real * prev_real - mult_imag * prev_imag
    )
    fwd_imag.append(
        pick_index(u_imag, block_index, block_axis) + mult_real * prev_imag + mult_imag * prev_real
    )
    out_real = list(fwd_real)
    out_imag = list(fwd_imag)
    block_index = 0
    mult_real, mult_imag = factor(block_index, block_len - 1)
    next_real = pick_index(out_real[block_index + 1], 0, cell_axis, True)
    next_imag = pick_index(out_imag[block_index + 1], 0, cell_axis, True)
    out_real[block_index] = fwd_real[block_index] + mult_real * next_real - mult_imag * next_imag
    out_imag[block_index] = fwd_imag[block_index] + mult_real * next_imag + mult_imag * next_real
    real_line = jnp.stack(out_real, axis=block_axis).reshape(in_shape[:4] + (in_shape[5],))
    imag_line = jnp.stack(out_imag, axis=block_axis).reshape(in_shape[:4] + (in_shape[5],))
    return jnp.stack([real_line, imag_line], axis=4).astype(jnp.bfloat16)


def phase_shift(wavefield, slow_field, frequency):
    angles = frequency[:, None, None] * slow_field[None]
    cosine = jnp.cos(angles)[None, None]
    sine_part = jnp.sin(angles)[None, None]
    signs_five = jnp.array([1.0, -1.0], jnp.float32).reshape(1, 2, 1, 1, 1)
    real_part = wavefield[:, :, :, :, 0].astype(jnp.float32)
    imag_part = wavefield[:, :, :, :, 1].astype(jnp.float32)
    new_real = real_part * cosine - signs_five * imag_part * sine_part
    new_imag = imag_part * cosine + signs_five * real_part * sine_part
    return jnp.stack([new_real, new_imag], axis=4).astype(jnp.bfloat16)


def image_term(wavefield, row_cells, col_cells, shot_positions, frequency):
    source = wavefield[:, 0].astype(jnp.float32)
    receiver = wavefield[:, 1].astype(jnp.float32)
    cross = source[:, :, :, 0] * receiver[:, :, :, 1] - source[:, :, :, 1] * receiver[:, :, :, 0]
    weighted = jnp.sum(cross * frequency[None, :, None, None], axis=1)
    row_gap = row_cells[None, :, None] - shot_positions[:, 0][:, None, None]
    col_gap = col_cells[None, None, :] - shot_positions[:, 1][:, None, None]
    spread = (row_gap * row_gap + col_gap * col_gap).astype(jnp.float32)
    taper = 1.0 / (1.0 + spread * (16.0 / (NX * NX)))
    return jnp.sum(weighted * taper, axis=0)


def general_shards(
    source_field,
    residual_data,
    receiver_lines,
    shot_positions,
    slowness,
    frequency,
    line_inverse,
    coupling,
):
    row_count = source_field.shape[2]
    line_len = source_field.shape[4]
    receiver = residual_data * receiver_lines.astype(jnp.bfloat16)[:, None, None, None, :]
    wavefield = jnp.stack([source_field, receiver], axis=1)
    slab_start = lax.axis_index("slab") * row_count
    own_cells = slab_start + jnp.arange(row_count, dtype=jnp.int32)
    all_cells = jnp.arange(line_len, dtype=jnp.int32)
    solve_first = partial(line_solve, line_inverse=line_inverse, coupling=coupling, line_dim=3)
    solve_second = partial(line_solve, line_inverse=line_inverse, coupling=coupling, line_dim=5)

    def forward(fields):
        return solve_first(lax.all_to_all(fields, "slab", split_axis=5, concat_axis=3, tiled=True))

    def backward(fields):
        return lax.all_to_all(fields, "slab", split_axis=3, concat_axis=5, tiled=True)

    images = []
    for depth_index in range(STEPS):
        shifted = phase_shift(wavefield, slowness[depth_index], frequency)
        if depth_index % 2 == 0:
            wavefield = backward(forward(solve_second(shifted)))
        else:
            wavefield = solve_second(backward(forward(shifted)))
        local_image = image_term(wavefield, own_cells, all_cells, shot_positions, frequency)
        images.append(lax.psum_scatter(local_image, "shot", scatter_dimension=1, tiled=True))
    return jnp.stack(images)


F32 = jnp.float32
BF16 = jnp.bfloat16
SMEM = pltpu.SMEM
VMEM = pltpu.VMEM
MIDDLE = 1.25


def params(mib):
    return pltpu.CompilerParams(vmem_limit_bytes=mib << 20)


def sincos(angle):
    turns = jnp.floor(angle * 0.15915494309189535 + 0.5)
    rest = (angle - turns * 6.28125) - turns * 1.9353071795864769e-3
    rest = rest * 0.25
    square = rest * rest
    sine = rest + rest * square * (
        -1.6666667e-1 + square * (8.3333333e-3 + square * (-1.9841270e-4 + square * 2.7557319e-6))
    )
    cosine = 1.0 + square * (
        -0.5 + square * (4.1666667e-2 + square * (-1.3888889e-3 + square * 2.4801587e-5))
    )
    sine, cosine = 2.0 * sine * cosine, 1.0 - 2.0 * sine * sine
    return 2.0 * sine * cosine, 1.0 - 2.0 * sine * sine


def dot_t(left, right):
    return lax.dot_general(left, right, (((1,), (1,)), ((), ())), preferred_element_type=F32)


def dot(left, right):
    return lax.dot_general(left, right, (((1,), (0,)), ((), ())), preferred_element_type=F32)


def dot_rows(left, right):
    return lax.dot_general(left, right, (((0,), (0,)), ((), ())), preferred_element_type=F32)


def shift_kernel(conjugate, other, meta, freq, mask, field, slowness, out):
    rows = slowness.shape[1]
    f = meta[0] ^ other
    sine, cosine = sincos(freq[f] * slowness[0])
    real = field[0, f, :, 0, :].astype(F32)
    imag = field[0, f, :, 1, :].astype(F32)
    if conjugate:
        keep = mask[...].astype(F32)
        real = real * keep
        imag = -(imag * keep)
    out[:rows] = (real * cosine - imag * sine).astype(BF16)
    out[rows:] = (imag * cosine + real * sine).astype(BF16)


def edge_rows(meta, blocks, block, lanes):
    start = pl.multiple_of((1 - block) * (blocks.shape[2] - 16), 16)
    return jnp.concatenate([blocks[part, block, pl.ds(start, 16), lanes] for part in range(2)], axis=0)


def pick_edge(block, values):
    first = block == 0
    return jnp.where(first, values[15:16], values[0:1]), jnp.where(first, values[31:32], values[16:17])


def edge_product(block, real, imag):
    rr, ir = pick_edge(block, real)
    ri, ii = pick_edge(block, imag)
    return rr - ii, ri + ir


def slab_kernel(meta, coupling, own, core, blocks, same, cross, partial_edge, ends):
    blocks = blocks.at[meta[0]]
    rows = own.shape[0] // 2
    half = blocks.shape[2]
    f, zz, xb, local = meta[0], meta[1], meta[2], meta[3]
    cr, ci = coupling[f, 0], coupling[f, 1]
    spot = lax.broadcasted_iota(jnp.int32, (16, half), 1)
    line = lax.broadcasted_iota(jnp.int32, (16, half), 0)
    solved, columns = [], []
    for k in range(2):
        cells = slice(k * half, (k + 1) * half)
        hot = jnp.where((spot == (half - 1 if k == 0 else 0)) & (line == 0), 1.0, 0.0).astype(BF16)
        left = jnp.concatenate(
            [own[:rows, cells], core[:rows, cells], own[rows:, cells], core[rows:, cells], hot], axis=0
        )
        by_real = dot_t(left, blocks[0, k])
        by_imag = dot_t(left, blocks[1, k])
        n = 2 * rows
        solved.append((by_real[:n] - by_imag[n : 2 * n], by_real[n : 2 * n] + by_imag[:n]))
        ar, ai = by_real[2 * n : 2 * n + 1], by_imag[2 * n : 2 * n + 1]
        columns.append((cr * ar - ci * ai, cr * ai + ci * ar))
        ends[2 * k : 2 * k + 1] = columns[k][0]
        ends[2 * k + 1 : 2 * k + 2] = columns[k][1]

    def couple(k, er, ei):
        qr, qi = columns[k]
        return solved[k][0] + er * qr - ei * qi, solved[k][1] + er * qi + ei * qr

    upper = couple(1, solved[0][0][:, half - 1 :], solved[0][1][:, half - 1 :])
    lower = couple(0, upper[0][:, 0:1], upper[1][:, 0:1])
    first = zz == 0
    pieces = []
    for part in range(2):
        low, high = lower[part].astype(BF16), upper[part].astype(BF16)
        mine, away = jnp.where(first, low, high), jnp.where(first, high, low)
        for n in range(2):
            at = slice((2 * n + part) * rows, (2 * n + part + 1) * rows)
            same[at] = mine[n * rows : (n + 1) * rows]
            cross[at] = away[n * rows : (n + 1) * rows]
        pieces.append(jnp.concatenate([mine, away], axis=1))
    edges = [0.0, 0.0]
    for n in range(2):
        lanes = pl.ds(pl.multiple_of((local ^ n) * rows, rows), rows)
        row = edge_rows(meta, blocks, xb, lanes)
        real = dot(row, pieces[0][n * rows : (n + 1) * rows])
        imag = dot(row, pieces[1][n * rows : (n + 1) * rows])
        er, ei = edge_product(xb, real, imag)
        edges = [edges[0] + er, edges[1] + ei]
    partial_edge[0:1] = edges[0][:, :half]
    partial_edge[1:2] = edges[1][:, :half]
    partial_edge[2:3] = edges[0][:, half:]
    partial_edge[3:4] = edges[1][:, half:]


def phase_kernel(meta, freq, place, own, core, far, far_core, sine, cosine, weight):
    rows, half = own.shape
    omega = freq[meta[0]]
    for k, piece in enumerate((own, core, far, far_core)):
        start = pl.multiple_of((meta[3] ^ k) * rows, rows)
        s, c = sincos(omega * (piece[...].astype(F32) + MIDDLE))
        sine[pl.ds(start, rows)] = s
        cosine[pl.ds(start, rows)] = c
    row = lax.broadcasted_iota(jnp.int32, (weight.shape[0], half), 0) + meta[2] * half - place[0, 0]
    col = lax.broadcasted_iota(jnp.int32, (weight.shape[0], half), 1) + meta[1] * half - place[0, 1]
    spread = (row * row + col * col).astype(F32)
    weight[...] = -omega / (1.0 + spread * (16.0 / (NX * NX)))


def turn_value(meta, coupling, blocks, block):
    cr, ci = coupling[meta[0], 0], coupling[meta[0], 1]
    ar = blocks[0, 1, 0:16, 0:128].astype(F32)[0:1, 0:1]
    ai = blocks[1, 1, 0:16, 0:128].astype(F32)[0:1, 0:1]
    first = block == 0
    return jnp.where(first, cr * ar - ci * ai, 0.0), jnp.where(first, cr * ai + ci * ar, 0.0)


def column_kernel(
    meta, coupling, near, far, blocks, edge_same, edge_cross, sine, cosine, solved, shifted, own_edge, real, imag
):
    blocks = blocks.at[meta[0]]
    rows = near.shape[0] // 4
    half = near.shape[1]
    xb = meta[2]
    for k, (piece, n) in enumerate(((near, 0), (near, 1), (far, 0), (far, 1))):
        start = pl.multiple_of((meta[3] ^ k) * rows, rows)
        real[pl.ds(start, rows)] = piece[2 * n * rows : (2 * n + 1) * rows]
        imag[pl.ds(start, rows)] = piece[(2 * n + 1) * rows : (2 * n + 2) * rows]
    cr, ci = coupling[meta[0], 0], coupling[meta[0], 1]
    ar, ai = turn_value(meta, coupling, blocks, xb)
    row = edge_rows(meta, blocks, xb, slice(0, half))
    own_real, own_imag = edge_product(xb, dot(row, real[...]), dot(row, imag[...]))
    hr = edge_same[0:1] + edge_cross[0:1] + ar * own_real - ai * own_imag
    hi = edge_same[1:2] + edge_cross[1:2] + ar * own_imag + ai * own_real
    add_real = cr * hr - ci * hi
    add_imag = cr * hi + ci * hr
    upper = xb == 1
    low = lax.broadcasted_iota(jnp.int32, (16, half), 0) == 0
    high = lax.broadcasted_iota(jnp.int32, (16, half), 0) == 15
    for ref, add in ((real, add_real), (imag, add_imag)):
        ref[0:16] = (ref[0:16].astype(F32) + jnp.where(low & upper, add, 0.0)).astype(BF16)
        ref[half - 16 :] = (
            ref[half - 16 :].astype(F32) + jnp.where(high & jnp.logical_not(upper), add, 0.0)
        ).astype(BF16)
    left = jnp.concatenate([blocks[0, xb], blocks[1, xb]], axis=0)
    for n in range(0, half, 256):
        cols = slice(n, n + 256)
        by_real = dot(left, real[:, cols])
        by_imag = dot(left, imag[:, cols])
        xr = (by_real[:half] - by_imag[half:]).astype(BF16)
        xi = (by_imag[:half] + by_real[half:]).astype(BF16)
        solved[:half, cols] = xr
        solved[half:, cols] = xi
        xr, xi = xr.astype(F32), xi.astype(F32)
        s, c = sine[:, cols], cosine[:, cols]
        shifted[:half, cols] = (xr * c - xi * s).astype(BF16)
        shifted[half:, cols] = (xi * c + xr * s).astype(BF16)
    own_real, own_imag = edge_product(xb, dot(row, shifted[:half]), dot(row, shifted[half:]))
    own_edge[0:1] = own_real
    own_edge[1:2] = own_imag


def both_kernel(meta, shifted, blocks, solved, edge):
    blocks = blocks.at[meta[0]]
    half = shifted.shape[1]
    xb, zz = meta[2], meta[1]
    left = jnp.concatenate([blocks[0, xb], blocks[1, xb]], axis=0)
    by_real = dot(left, shifted[:half])
    by_imag = dot(left, shifted[half:])
    u = jnp.concatenate(
        [(by_real[:half] - by_imag[half:]).astype(BF16), (by_imag[:half] + by_real[half:]).astype(BF16)], axis=0
    )
    row = dot_t(edge_rows(meta, blocks, zz, slice(0, half)), u)
    edge_real, edge_imag = edge_product(zz, row[:, :half], row[:, half:])
    edge[0:1] = edge_real
    edge[1:2] = edge_imag
    by_real = dot_t(u, blocks[0, zz])
    by_imag = dot_t(u, blocks[1, zz])
    solved[:half] = (by_real[:half] - by_imag[half:]).astype(BF16)
    solved[half:] = (by_real[half:] + by_imag[:half]).astype(BF16)


def image_pieces(meta, image, keep, send):
    rows, cols = keep.shape[1:]
    for kz in range(2):
        for kx in range(2):
            col = pl.multiple_of((meta[5] ^ kx) * cols, cols)
            for other, ref in ((0, keep), (1, send)):
                row = pl.multiple_of(((meta[4] ^ kz) * 2 + (meta[0] ^ other)) * rows, rows)
                ref[kz * 2 + kx] = image[pl.ds(row, rows), pl.ds(col, cols)].astype(BF16)


def pick_end(ends, block):
    first = block == 0
    return jnp.where(first, ends[0:1], ends[2:3]), jnp.where(first, ends[1:2], ends[3:4])


def turn_kernel(meta, coupling, edge_x, near_x, edge_y0, edge_y1, ends, blocks, whole, edge):
    blocks = blocks.at[meta[0]]
    ar, ai = turn_value(meta, coupling, blocks, meta[2])
    zz = meta[1]
    yr, yi = pick_edge(zz, edge_rows(meta, blocks, zz, slice(0, ends.shape[1])).astype(F32))
    pr, pi = pick_end(ends, meta[2])
    for n in range(2):
        r, i = slice(2 * n, 2 * n + 1), slice(2 * n + 1, 2 * n + 2)
        hr = near_x[r] + ar * edge_x[r] - ai * edge_x[i]
        hi = near_x[i] + ar * edge_x[i] + ai * edge_x[r]
        whole[r] = hr
        whole[i] = hi
        sr = jnp.sum(hr * yr - hi * yi, axis=1, keepdims=True)
        si = jnp.sum(hr * yi + hi * yr, axis=1, keepdims=True)
        edge_y = (edge_y0, edge_y1)[n]
        edge[r] = edge_y[0:1] + sr * pr - si * pi
        edge[i] = edge_y[1:2] + sr * pi + si * pr


def split(value):
    high = value.astype(BF16)
    return high.astype(F32), (value - high.astype(F32))


def between_kernel(meta, whole, inverse, source, receiver, weight, out, keep, send, image):
    blocks = inverse.at[meta[0]]
    high, low = split(whole[...])
    left = jnp.concatenate([high, low, high, low], axis=0).astype(BF16)
    by_real = dot_t(left, blocks[0, meta[1]])
    by_imag = dot_t(left, blocks[1, meta[1]])
    by_real = by_real[0:4] + by_real[4:8]
    by_imag = by_imag[0:4] + by_imag[4:8]
    for n in range(2):
        r, i = slice(2 * n, 2 * n + 1), slice(2 * n + 1, 2 * n + 2)
        out[r] = by_real[r] - by_imag[i]
        out[i] = by_real[i] + by_imag[r]
    half = source.shape[1]
    sr, si = source[:half].astype(F32), source[half:].astype(F32)
    rr, ri = receiver[:half].astype(F32), receiver[half:].astype(F32)
    image[...] = (sr * ri + si * rr) * weight[...]
    image_pieces(meta, image, keep, send)


def second_image_kernel(
    meta, coupling, source, receiver, weight, rows_y, edge, near, ends, blocks, keep, send, image
):
    half = source.shape[1]
    blocks = blocks.at[meta[0]]
    ar, ai = turn_value(meta, coupling, blocks, meta[1])
    pr, pi = pick_end(ends, meta[2])
    qr, qi = pick_end(ends, meta[1])

    def triple(value, order):
        high, low = split(value)
        return [high, high, low] if order == 0 else [high, low, high]

    fields = []
    for n, ref in enumerate((source, receiver)):
        r, i = slice(2 * n, 2 * n + 1), slice(2 * n + 1, 2 * n + 2)
        gr = near[r] + ar * edge[r] - ai * edge[i]
        gi = near[i] + ar * edge[i] + ai * edge[r]
        tr, ti = rows_y[r], rows_y[i]
        left, right_real, right_imag = [], [], []
        for a, b, c in ((pr, tr, ti), (pi, -ti, tr), (gr, qr, qi), (gi, -qi, qr)):
            left += triple(a, 0)
            right_real += triple(b, 1)
            right_imag += triple(c, 1)
        pad = [jnp.zeros((4, half), F32)]
        left = jnp.concatenate(left + pad, axis=0).astype(BF16)
        right_real = jnp.concatenate(right_real + pad, axis=0).astype(BF16)
        right_imag = jnp.concatenate(right_imag + pad, axis=0).astype(BF16)
        fields.append(
            (
                ref[:half].astype(F32) + dot_rows(left, right_real),
                ref[half:].astype(F32) + dot_rows(left, right_imag),
            )
        )
    (sr, si), (rr, ri) = fields
    image[...] = (sr * ri + si * rr) * weight[...]
    image_pieces(meta, image, keep, send)


def block_shards(
    source_field, residual_data, receiver_lines, shot_positions, slowness, frequency, line_inverse, coupling
):
    rows, length = slowness.shape[1:]
    half = line_inverse.shape[-1]
    slab = lax.axis_index("slab")
    shot = lax.axis_index("shot")
    meta = jnp.stack(
        [slab & 1, (slab >> 1) & 1, slab >> 2, slab & 3, shot >> 1, shot & 1]
    ).astype(jnp.int32)
    smem = pl.BlockSpec(memory_space=SMEM)
    vmem = pl.BlockSpec(memory_space=VMEM)

    def shape(dtype, *sizes):
        return jax.ShapeDtypeStruct(sizes, dtype)

    def call(body, name, specs, outs, scratch, mib, *args):
        return pl.pallas_call(
            body,
            in_specs=specs,
            out_specs=[vmem] * len(outs),
            out_shape=outs,
            scratch_shapes=scratch,
            compiler_params=params(mib),
            name=name,
        )(*args)

    def move(array, k):
        return lax.ppermute(array, "slab", [(i, i ^ k) for i in range(8)])

    same, far, edges = [], [], []
    for n, field in enumerate((source_field, residual_data)):
        mask = receiver_lines
        if n == 1:
            mask, edges[0] = lax.optimization_barrier((mask, edges[0]))
        halves = []
        for other in (1, 0):
            halves.append(
                call(
                    partial(shift_kernel, n == 1, other),
                    "shift",
                    [smem, smem, vmem, vmem, vmem],
                    [shape(BF16, 2 * rows, length)],
                    [],
                    12,
                    meta,
                    frequency,
                    mask,
                    field,
                    slowness,
                )
            )
        own, core = halves[1][0], move(halves[0][0], 1)
        if n == 0:
            layer = (slowness[1] - MIDDLE).astype(jnp.float16)
            low, high = layer[:, :half], layer[:, half:]
            first = meta[1] == 0
            own_slow = jnp.where(first, low, high)
            far_slow = move(jnp.where(first, high, low), 2)
            core, far_slow = lax.optimization_barrier((core, far_slow))
        mine, cross, edge, ends = call(
            slab_kernel,
            "slab",
            [smem, smem, vmem, vmem, vmem],
            [shape(BF16, 4 * rows, half)] * 2 + [shape(F32, 4, half)] * 2,
            [],
            16,
            meta,
            coupling,
            own,
            core,
            line_inverse,
        )
        same.append(mine)
        edges.append(edge)
        if n == 0:
            far.append(move(cross, 2))
    own_slow, far_slow, edges[1] = lax.optimization_barrier((own_slow, far_slow, edges[1]))
    edges = jnp.stack(edges)
    edge_same = move(edges[:, :2], 4)
    edge_cross = move(edges[:, 2:], 6)
    cross, edge_same, edge_cross, far[0] = lax.optimization_barrier((cross, edge_same, edge_cross, far[0]))
    far.append(move(cross, 2))
    pair = shape(BF16, 2 * half, half)
    line = shape(F32, 2, half)
    four = shape(F32, 4, half)
    core_slow = move(jnp.stack([own_slow, far_slow]), 1)
    block = shape(F32, half, half)
    sine, cosine, weight = call(
        phase_kernel,
        "phase",
        [smem] * 3 + [vmem] * 4,
        [block] * 3,
        [],
        8,
        meta,
        frequency,
        shot_positions,
        own_slow.astype(F32),
        core_slow[0].astype(F32),
        far_slow.astype(F32),
        core_slow[1].astype(F32),
    )
    solved, finals, edge_x, edge_y = [], [], [], []
    for n in range(2):
        if n == 1:
            same[1], finals[0] = lax.optimization_barrier((same[1], finals[0]))
        x0, turned, edge = call(
            column_kernel,
            "column",
            [smem, smem] + [vmem] * 7,
            [pair, pair, line],
            [VMEM((half, half), BF16)] * 2,
            16,
            meta,
            coupling,
            same[n],
            far[n],
            line_inverse,
            edge_same[n],
            edge_cross[n],
            sine,
            cosine,
        )
        v, across = call(both_kernel, "both", [smem] + [vmem] * 2, [pair, line], [], 20, meta, turned, line_inverse)
        solved.append(x0)
        finals.append(v)
        edge_x.append(edge)
        edge_y.append(across)
    edge_x = jnp.concatenate(edge_x)
    near_x = move(edge_x, 4)
    coupled, edge = call(
        turn_kernel,
        "turn",
        [smem, smem] + [vmem] * 6,
        [four, four],
        [],
        4,
        meta,
        coupling,
        edge_x,
        near_x,
        *edge_y,
        ends,
        line_inverse,
    )
    near_y = move(edge, 2)
    cut = shape(BF16, 4, rows, half // 2)
    scratch = [VMEM((half, half), F32)]
    rows_y, keep0, send0 = call(
        between_kernel,
        "between",
        [smem] + [vmem] * 5,
        [four, cut, cut],
        scratch,
        12,
        meta,
        coupled,
        line_inverse,
        solved[0],
        solved[1],
        weight,
    )
    keep1, send1 = call(
        second_image_kernel,
        "second_image",
        [smem] * 2 + [vmem] * 8,
        [cut] * 2,
        scratch,
        12,
        meta,
        coupling,
        finals[0],
        finals[1],
        weight,
        rows_y,
        edge,
        near_y,
        ends,
        line_inverse,
    )
    part0 = keep0.astype(F32) + move(send0, 1).astype(F32)
    part1 = keep1.astype(F32) + move(send1, 1).astype(F32)
    both = jnp.stack([part0, part1], axis=1).astype(BF16)
    total = 0.0
    for kz in range(2):
        for kx in range(2):
            route = []
            for s in range(4):
                for b in range(8):
                    sy, sx, bx, by, bc = s // 2, s % 2, b // 4, (b // 2) % 2, b % 2
                    target = (by * 2 + (sx ^ kx)) * 8 + bx * 4 + (sy ^ kz) * 2 + bc
                    route.append((s * 8 + b, target))
            total = total + lax.ppermute(both[kz * 2 + kx], ("shot", "slab"), route).astype(F32)
    return total


def solution(mesh):
    placed = (
        P("shot", None, "slab", None, None),
        P("shot", None, "slab", None, None),
        P("shot", None),
        P("shot", None),
        P(None, "slab", None),
        P(),
        P(),
        P(),
    )
    fits = mesh.shape["slab"] == 8 and mesh.shape["shot"] == 4

    def run(*args):
        line_inverse = args[6]
        blocks = fits and line_inverse.shape[0] == 2 and line_inverse.shape[2] == 2
        body = block_shards if blocks else general_shards
        return jax.shard_map(
            body, mesh=mesh, in_specs=placed, out_specs=P(None, "slab", "shot"), check_vma=False
        )(*args)

    return run
```

profile of v0, /device:TPU:4, one launch (start us, length us, event | category | flops | bytes accessed | tf_op | source)
XLA Modules:
  0.0 80.9 jit_solution(6221610760179247201)
XLA Ops:
  0.0 0.1 stack.57.meta
  0.1 1.2 %copy-done.2 = f32[2,128,1024]{2,1,0:T(8,128)S(1)} copy-done((f32[2,128,1024]{2,1,0:T(8,128)S(1)}, f32[2,128,1024]{2,1,0:T(8,128)}, u32[]{:S(2)}) %copy-start.2) | copy-done | bytes 1048600
  1.3 1.2 %copy-done.4 = bf16[1,2,128,2,1024]{4,3,2,1,0:T(2,128)(2,1)S(1)} copy-done((bf16[1,2,128,2,1024]{4,3,2,1,0:T(2,128)(2,1)S(1)}, bf16[1,2,128,2,1024]{4,3,2,1,0:T(2,128)(2,1)}, u32[]{:S(2)}) %copy-start.4) | copy-done | bytes 1048600
  2.5 0.7 copy-done.7
  3.2 0.7 copy-done.11
  3.9 1.6 %shift.5 = bf16[256,1024]{1,0:T(8,128)(2,1)S(1)} custom-call(s32[6]{0:T(128)S(1)} %stack.57.meta, f32[2]{0:T(128)S(1)} %copy-done.11, s32[1,1024]{1,0:T(1,128)S(1)} %copy-done.7, bf16[1,2,128,2,1024]{4,3,2,1,0:T(2,128)(2,1)S(1)} %copy-done.4, f32[2,128,1024]{2,1,0:T(8,128)S(1)} %copy-done.2), custom_call_target="tpu_custom_call" | custom-call | tf_op jit(solution)/shard_map/shift/pallas_call | solution.py:466
  5.5 0.1 collective-permute-start
  5.6 0.0 copy-start.9
  5.6 1.1 %fusion = f16[128,1024]{1,0:T(8,128)(2,1)S(1)} fusion(f32[2,128,1024]{2,1,0:T(8,128)} %slowness.7), kind=kLoop, calls=%fused_computation.9 | loop fusion | flops 262144 | bytes 786432 | tf_op jit(solution)/shard_map/convert_element_type | solution.py:503
  6.7 0.0 copy-start.6
  6.7 0.1 broadcast_select_fusion
  6.8 1.6 %collective-permute-start.1 = (f16[128,512]{1,0:T(8,128)(2,1)S(1)}, f16[128,512]{1,0:T(8,128)(2,1)S(1)}, u32[]{:S(2)}, u32[]{:S(2)}) collective-permute-start(f16[128,512]{1,0:T(8,128)(2,1)S(1)} %get-tuple-element.92), channel_id=1, source_target_pairs={{0,2},{1,3},{2,0},{3,1},{4,6},{5,7},{6,4},{7,5},{8,10},{9,11},{10,... | collective-permute-start | bytes 393224 | tf_op jit(solution)/shard_map/ppermute | solution.py:477
  8.5 0.7 copy-done.8
  9.1 0.7 copy-done.12
  9.8 1.6 %shift.4.own = bf16[256,1024]{1,0:T(8,128)(2,1)S(1)} custom-call(s32[6]{0:T(128)S(1)} %stack.57.meta, f32[2]{0:T(128)S(1)} %copy-done.12, s32[1,1024]{1,0:T(1,128)S(1)} %copy-done.8, bf16[1,2,128,2,1024]{4,3,2,1,0:T(2,128)(2,1)S(1)} %copy-done.5, f32[2,128,1024]{2,1,0:T(8,128)S(1)} %copy-done.3), custom_call_target="tpu_custom_call" | custom-call | tf_op jit(solution)/shard_map/shift/pallas_call | solution.py:466
  11.4 1.3 %collective-permute-done.1 = f16[128,512]{1,0:T(8,128)(2,1)S(1)} collective-permute-done((f16[128,512]{1,0:T(8,128)(2,1)S(1)}, f16[128,512]{1,0:T(8,128)(2,1)S(1)}, u32[]{:S(2)}, u32[]{:S(2)}) %collective-permute-start.1) | collective-permute-done | bytes 131104 | tf_op jit(solution)/shard_map/ppermute | solution.py:477
  12.8 0.0 collective-permute-done.core
  12.8 2.2 %copy-done = bf16[2,2,2,512,512]{4,3,2,1,0:T(8,128)(2,1)S(1)} copy-done((bf16[2,2,2,512,512]{4,3,2,1,0:T(8,128)(2,1)S(1)}, bf16[2,2,2,512,512]{4,3,2,1,0:T(8,128)(2,1)}, u32[]{:S(2)}) %copy-start) | copy-done | bytes 4194328
  15.0 3.1 %slab.2 = (bf16[512,512]{1,0:T(8,128)(2,1)S(1)}, bf16[512,512]{1,0:T(8,128)(2,1)S(1)}, f32[4,512]{1,0:T(4,128)S(1)}, f32[4,512]{1,0:T(4,128)}) custom-call(s32[6]{0:T(128)S(1)} %stack.57.meta, f32[2,2]{1,0:T(2,128)S(1)} %copy-done.10, bf16[256,1024]{1,0:T(8,128)(2,1)S(1)} %shift.4.own, bf16[256,1024]{1,0:T(8,128)(2,1)S(1)} %collective-permute-done.core, ...), custom_call_target="tpu_custom_call" | custom-call | tf_op jit(solution)/shard_map/slab/pallas_call | solution.py:466
  18.0 1.7 %shift.7 = bf16[256,1024]{1,0:T(8,128)(2,1)S(1)} custom-call(s32[6]{0:T(128)S(1)} %stack.57.meta, f32[2]{0:T(128)S(1)} %copy-done.12, s32[1,1024]{1,0:T(1,128)S(1)} %copy-done.9, bf16[1,2,128,2,1024]{4,3,2,1,0:T(2,128)(2,1)S(1)} %copy-done.6, f32[2,128,1024]{2,1,0:T(8,128)S(1)} %copy-done.3), custom_call_target="tpu_custom_call" | custom-call | tf_op jit(solution)/shard_map/shift/pallas_call | solution.py:466
  19.7 0.1 collective-permute-start.2
  19.8 1.6 %collective-permute-start.5 = (bf16[512,512]{1,0:T(8,128)(2,1)S(1)}, bf16[512,512]{1,0:T(8,128)(2,1)S(1)}, u32[]{:S(2)}, u32[]{:S(2)}) collective-permute-start(bf16[512,512]{1,0:T(8,128)(2,1)S(1)} %get-tuple-element.54), channel_id=1, source_target_pairs={{0,2},{1,3},{2,0},{3,1},{4,6},{5,7},{6,4},{7,5},{8,10},{9,11},{10,... | collective-permute-start | bytes 1572872 | tf_op jit(solution)/shard_map/ppermute | solution.py:477
  21.5 1.7 %shift.6.own = bf16[256,1024]{1,0:T(8,128)(2,1)S(1)} custom-call(s32[6]{0:T(128)S(1)} %stack.57.meta, f32[2]{0:T(128)S(1)} %copy-done.12, s32[1,1024]{1,0:T(1,128)S(1)} %copy-done.9, bf16[1,2,128,2,1024]{4,3,2,1,0:T(2,128)(2,1)S(1)} %copy-done.6, f32[2,128,1024]{2,1,0:T(8,128)S(1)} %copy-done.3), custom_call_target="tpu_custom_call" | custom-call | tf_op jit(solution)/shard_map/shift/pallas_call | solution.py:466
  23.2 0.0 copy-start.13
  23.2 0.0 copy-start.14
  23.2 0.0 collective-permute-done.2.core
  23.2 2.6 %slab.3 = (bf16[512,512]{1,0:T(8,128)(2,1)S(1)}, bf16[512,512]{1,0:T(8,128)(2,1)S(1)}, f32[4,512]{1,0:T(4,128)S(1)}, f32[4,512]{1,0:T(4,128)S(1)}) custom-call(s32[6]{0:T(128)S(1)} %stack.57.meta, f32[2,2]{1,0:T(2,128)S(1)} %copy-done.10, bf16[256,1024]{1,0:T(8,128)(2,1)S(1)} %shift.6.own, bf16[256,1024]{1,0:T(8,128)(2,1)S(1)} %collective-permute-done.2.core, ...), custom_call_target="tpu_custom_call" | custom-call | tf_op jit(solution)/shard_map/slab/pallas_call | solution.py:466
  25.8 2.5 %collective-permute-start.4 = (f32[2,2,512]{2,1,0:T(2,128)S(1)}, f32[2,2,512]{2,1,0:T(2,128)S(1)}, u32[]{:S(2)}, u32[]{:S(2)}) collective-permute-start(f32[2,2,512]{2,1,0:T(2,128)S(1)} %get-tuple-element.93), channel_id=1, source_target_pairs={{0,6},{1,7},{2,4},{3,5},{4,2},{5,3},{6,0},{7,1},{8,14},{9,15},{10,... | collective-permute-start | bytes 24584 | tf_op jit(solution)/shard_map/ppermute | solution.py:477
  28.4 0.2 collective-permute-start.3
  28.6 5.8 %collective-permute-done.5.far = bf16[512,512]{1,0:T(8,128)(2,1)S(1)} collective-permute-done((bf16[512,512]{1,0:T(8,128)(2,1)S(1)}, bf16[512,512]{1,0:T(8,128)(2,1)S(1)}, u32[]{:S(2)}, u32[]{:S(2)}) %collective-permute-start.5) | collective-permute-done | bytes 524320 | tf_op jit(solution)/shard_map/ppermute | solution.py:477
  34.3 2.1 %collective-permute-done.4 = f32[2,2,512]{2,1,0:T(2,128)S(1)} collective-permute-done((f32[2,2,512]{2,1,0:T(2,128)S(1)}, f32[2,2,512]{2,1,0:T(2,128)S(1)}, u32[]{:S(2)}, u32[]{:S(2)}) %collective-permute-start.4) | collective-permute-done | bytes 8224 | tf_op jit(solution)/shard_map/ppermute | solution.py:477
  36.5 0.6 collective-permute-start.7
  37.1 0.1 pad_maximum_fusion
  37.2 0.1 collective-permute-start.6
  37.3 1.5 %collective-permute-done.6 = f16[2,128,512]{2,1,0:T(8,128)(2,1)S(1)} collective-permute-done((f16[2,128,512]{2,1,0:T(8,128)(2,1)S(1)}, f16[2,128,512]{2,1,0:T(8,128)(2,1)S(1)}, u32[]{:S(2)}, u32[]{:S(2)}) %collective-permute-start.6) | collective-permute-done | bytes 262176 | tf_op jit(solution)/shard_map/ppermute | solution.py:477
  38.8 0.1 fusion.10
  38.9 2.1 %phase.1 = (f32[512,512]{1,0:T(8,128)S(1)}, f32[512,512]{1,0:T(8,128)S(1)}, f32[512,512]{1,0:T(8,128)S(1)}) custom-call(s32[6]{0:T(128)S(1)} %stack.57.meta, f32[2]{0:T(128)S(1)} %copy-done.13, s32[1,2]{1,0:T(1,128)S(1)} %copy-done.14, f32[128,512]{1,0:T(8,128)S(1)} %convert_element_type.49.own, f32[128,512]{1,0:T(8,128)S(1)} %get-tuple-element.90.core, ...), custom_call_target="tpu_custom_call" | custom-call | tf_op jit(solution)/shard_map/phase/pallas_call | solution.py:466
  40.9 2.9 %column.2 = (bf16[1024,512]{1,0:T(8,128)(2,1)S(1)}, bf16[1024,512]{1,0:T(8,128)(2,1)S(1)}, f32[2,512]{1,0:T(2,128)S(1)}) custom-call(s32[6]{0:T(128)S(1)} %stack.57.meta, f32[2,2]{1,0:T(2,128)S(1)} %copy-done.10, bf16[512,512]{1,0:T(8,128)(2,1)S(1)} %get-tuple-element.46.near, bf16[512,512]{1,0:T(8,128)(2,1)S(1)} %collective-permute-done.5.far, ...), custom_call_target="tpu_custom_call" | custom-call | tf_op jit(solution)/shard_map/column/pallas_call | solution.py:466
  43.8 3.3 %both.2 = (bf16[1024,512]{1,0:T(8,128)(2,1)S(1)}, f32[2,512]{1,0:T(2,128)S(1)}) custom-call(s32[6]{0:T(128)S(1)} %stack.57.meta, bf16[1024,512]{1,0:T(8,128)(2,1)S(1)} %get-tuple-element.64.shifted, bf16[2,2,2,512,512]{4,3,2,1,0:T(8,128)(2,1)S(1)} %copy-done.1), custom_call_target="tpu_custom_call" | custom-call | tf_op jit(solution)/shard_map/both/pallas_call | solution.py:466
  47.1 2.5 %collective-permute-done.7.far = bf16[512,512]{1,0:T(8,128)(2,1)S(1)} collective-permute-done((bf16[512,512]{1,0:T(8,128)(2,1)S(1)}, bf16[512,512]{1,0:T(8,128)(2,1)S(1)}, u32[]{:S(2)}, u32[]{:S(2)}) %collective-permute-start.7) | collective-permute-done | bytes 524320 | tf_op jit(solution)/shard_map/ppermute | solution.py:477
  49.6 2.7 %column.3 = (bf16[1024,512]{1,0:T(8,128)(2,1)S(1)}, bf16[1024,512]{1,0:T(8,128)(2,1)S(1)}, f32[2,512]{1,0:T(2,128)S(1)}) custom-call(s32[6]{0:T(128)S(1)} %stack.57.meta, f32[2,2]{1,0:T(2,128)S(1)} %copy-done.10, bf16[512,512]{1,0:T(8,128)(2,1)S(1)} %get-tuple-element.66.near, bf16[512,512]{1,0:T(8,128)(2,1)S(1)} %collective-permute-done.7.far, ...), custom_call_target="tpu_custom_call" | custom-call | tf_op jit(solution)/shard_map/column/pallas_call | solution.py:466
  52.3 0.9 %collective-permute-start.8 = (f32[4,512]{1,0:T(4,128)S(1)}, f32[4,512]{1,0:T(4,128)S(1)}, u32[]{:S(2)}, u32[]{:S(2)}) collective-permute-start(f32[4,512]{1,0:T(4,128)S(1)} %pad_maximum_fusion.3.edge_x), channel_id=1, source_target_pairs={{0,4},{1,5},{2,6},{3,7},{4,0},{5,1},{6,2},{7,3},{8,12},{9,13},{10,... | collective-permute-start | bytes 24584 | tf_op jit(solution)/shard_map/ppermute | solution.py:477
  53.1 3.3 %both.3 = (bf16[1024,512]{1,0:T(8,128)(2,1)S(1)}, f32[2,512]{1,0:T(2,128)S(1)}) custom-call(s32[6]{0:T(128)S(1)} %stack.57.meta, bf16[1024,512]{1,0:T(8,128)(2,1)S(1)} %get-tuple-element.70.shifted, bf16[2,2,2,512,512]{4,3,2,1,0:T(8,128)(2,1)S(1)} %copy-done.1), custom_call_target="tpu_custom_call" | custom-call | tf_op jit(solution)/shard_map/both/pallas_call | solution.py:466
  56.4 0.5 collective-permute-done.8.near_x
  56.9 0.7 turn.1
  57.6 1.6 %between.1 = (f32[4,512]{1,0:T(4,128)S(1)}, bf16[4,128,256]{2,1,0:T(8,128)(2,1)S(1)}, bf16[4,128,256]{2,1,0:T(8,128)(2,1)S(1)}) custom-call(s32[6]{0:T(128)S(1)} %stack.57.meta, f32[4,512]{1,0:T(4,128)S(1)} %get-tuple-element.73.whole, bf16[2,2,2,512,512]{4,3,2,1,0:T(8,128)(2,1)S(1)} %copy-done.1, bf16[1024,512]{1,0:T(8,128)(2,1)S(1)} %get-tuple-element.74.source, ...), custom_call_target="tpu_custom_call" | custom-call | tf_op jit(solution)/shard_map/between/pallas_call | solution.py:466
  59.2 0.1 collective-permute-start.9
  59.3 1.3 %collective-permute-start.10 = (f32[4,512]{1,0:T(4,128)S(1)}, f32[4,512]{1,0:T(4,128)S(1)}, u32[]{:S(2)}, u32[]{:S(2)}) collective-permute-start(f32[4,512]{1,0:T(4,128)S(1)} %get-tuple-element.82.edge), channel_id=1, source_target_pairs={{0,2},{1,3},{2,0},{3,1},{4,6},{5,7},{6,4},{7,5},{8,10},{9,11},{10,... | collective-permute-start | bytes 24584 | tf_op jit(solution)/shard_map/ppermute | solution.py:477
  60.7 2.4 %collective-permute-done.10.near = f32[4,512]{1,0:T(4,128)S(1)} collective-permute-done((f32[4,512]{1,0:T(4,128)S(1)}, f32[4,512]{1,0:T(4,128)S(1)}, u32[]{:S(2)}, u32[]{:S(2)}) %collective-permute-start.10) | collective-permute-done | bytes 8224 | tf_op jit(solution)/shard_map/ppermute | solution.py:477
  63.0 1.7 %second_image.1 = (bf16[4,128,256]{2,1,0:T(8,128)(2,1)S(1)}, bf16[4,128,256]{2,1,0:T(8,128)(2,1)S(1)}) custom-call(s32[6]{0:T(128)S(1)} %stack.57.meta, f32[2,2]{1,0:T(2,128)S(1)} %copy-done.10, bf16[1024,512]{1,0:T(8,128)(2,1)S(1)} %get-tuple-element.79.source, bf16[1024,512]{1,0:T(8,128)(2,1)S(1)} %get-tuple-element.80.receiver, ...), custom_call_target="tpu_custom_call" | custom-call | tf_op jit(solution)/shard_map/second_image/pallas_call | solution.py:466
  64.8 0.1 collective-permute-start.11
  64.9 0.1 fusion.1
  64.9 1.4 %collective-permute-done.11 = bf16[4,128,256]{2,1,0:T(8,128)(2,1)S(1)} collective-permute-done((bf16[4,128,256]{2,1,0:T(8,128)(2,1)S(1)}, bf16[4,128,256]{2,1,0:T(8,128)(2,1)S(1)}, u32[]{:S(2)}, u32[]{:S(2)}) %collective-permute-start.11) | collective-permute-done | bytes 262176 | tf_op jit(solution)/shard_map/ppermute | solution.py:477
  66.4 0.1 fusion.2
  66.4 0.1 fusion.6
  66.5 3.1 %collective-permute-start.12 = (bf16[2,128,256]{2,1,0:T(8,128)(2,1)S(1)}, bf16[2,128,256]{2,1,0:T(8,128)(2,1)S(1)}, u32[]{:S(2)}, u32[]{:S(2)}) collective-permute-start(bf16[2,128,256]{2,1,0:T(8,128)(2,1)S(1)} %get-tuple-element.85), channel_id=1, source_target_pairs={{0,0},{1,1},{2,16},{3,17},{4,4},{5,5},{6,20},{7,21},{8,8},{9,9},{1... | collective-permute-start | bytes 393224 | tf_op jit(solution)/shard_map/ppermute | solution.py:642
  69.6 2.7 %collective-permute-start.13 = (bf16[2,128,256]{2,1,0:T(8,128)(2,1)S(1)}, bf16[2,128,256]{2,1,0:T(8,128)(2,1)S(1)}, u32[]{:S(2)}, u32[]{:S(2)}) collective-permute-start(bf16[2,128,256]{2,1,0:T(8,128)(2,1)S(1)} %get-tuple-element.86), channel_id=1, source_target_pairs={{0,8},{1,9},{2,24},{3,25},{4,12},{5,13},{6,28},{7,29},{8,0},{9,1},... | collective-permute-start | bytes 393224 | tf_op jit(solution)/shard_map/ppermute | solution.py:642
  72.3 0.0 collective-permute-start.15
  72.3 1.8 %collective-permute-start.14 = (bf16[2,128,256]{2,1,0:T(8,128)(2,1)S(1)}, bf16[2,128,256]{2,1,0:T(8,128)(2,1)S(1)}, u32[]{:S(2)}, u32[]{:S(2)}) collective-permute-start(bf16[2,128,256]{2,1,0:T(8,128)(2,1)S(1)} %get-tuple-element.88), channel_id=1, source_target_pairs={{0,2},{1,3},{2,18},{3,19},{4,6},{5,7},{6,22},{7,23},{8,10},{9,11},... | collective-permute-start | bytes 393224 | tf_op jit(solution)/shard_map/ppermute | solution.py:642
  74.1 1.5 %collective-permute-done.12 = bf16[2,128,256]{2,1,0:T(8,128)(2,1)S(1)} collective-permute-done((bf16[2,128,256]{2,1,0:T(8,128)(2,1)S(1)}, bf16[2,128,256]{2,1,0:T(8,128)(2,1)S(1)}, u32[]{:S(2)}, u32[]{:S(2)}) %collective-permute-start.12) | collective-permute-done | bytes 131104 | tf_op jit(solution)/shard_map/ppermute | solution.py:642
  75.6 2.9 %collective-permute-done.13 = bf16[2,128,256]{2,1,0:T(8,128)(2,1)S(1)} collective-permute-done((bf16[2,128,256]{2,1,0:T(8,128)(2,1)S(1)}, bf16[2,128,256]{2,1,0:T(8,128)(2,1)S(1)}, u32[]{:S(2)}, u32[]{:S(2)}) %collective-permute-start.13) | collective-permute-done | bytes 131104 | tf_op jit(solution)/shard_map/ppermute | solution.py:642
  78.6 1.1 %collective-permute-done.15 = bf16[2,128,256]{2,1,0:T(8,128)(2,1)S(1)} collective-permute-done((bf16[2,128,256]{2,1,0:T(8,128)(2,1)S(1)}, bf16[2,128,256]{2,1,0:T(8,128)(2,1)S(1)}, u32[]{:S(2)}, u32[]{:S(2)}) %collective-permute-start.15) | collective-permute-done | bytes 131104 | tf_op jit(solution)/shard_map/ppermute | solution.py:642
  79.7 0.5 collective-permute-done.14
  80.1 0.8 convert_add_fusion
  (26 shorter events, 0.1 us)
Async XLA Ops:
  0.0 12.8 %copy-start.10 = (f32[2,2]{1,0:T(2,128)S(1)}, f32[2,2]{1,0:T(2,128)}, u32[]{:S(2)}) copy-start(f32[2,2]{1,0:T(2,128)} %coupling.11) | copy-start | bytes 52
  0.1 1.2 %copy-start.2 = (f32[2,128,1024]{2,1,0:T(8,128)S(1)}, f32[2,128,1024]{2,1,0:T(8,128)}, u32[]{:S(2)}) copy-start(f32[2,128,1024]{2,1,0:T(8,128)} %slowness.7) | copy-start | bytes 3145732
  1.3 1.2 %copy-start.4 = (bf16[1,2,128,2,1024]{4,3,2,1,0:T(2,128)(2,1)S(1)}, bf16[1,2,128,2,1024]{4,3,2,1,0:T(2,128)(2,1)}, u32[]{:S(2)}) copy-start(bf16[1,2,128,2,1024]{4,3,2,1,0:T(2,128)(2,1)} %field.5) | copy-start | bytes 3145732
  2.5 0.7 copy-start.7
  3.2 0.7 copy-start.11
  3.9 4.6 %copy-start.3 = (f32[2,128,1024]{2,1,0:T(8,128)S(1)}, f32[2,128,1024]{2,1,0:T(8,128)}, u32[]{:S(2)}) copy-start(f32[2,128,1024]{2,1,0:T(8,128)} %slowness.7) | copy-start | bytes 3145732
  3.9 4.6 %copy-start.5 = (bf16[1,2,128,2,1024]{4,3,2,1,0:T(2,128)(2,1)S(1)}, bf16[1,2,128,2,1024]{4,3,2,1,0:T(2,128)(2,1)}, u32[]{:S(2)}) copy-start(bf16[1,2,128,2,1024]{4,3,2,1,0:T(2,128)(2,1)} %field.5) | copy-start | bytes 3145732
  5.5 7.2 %collective-permute-start = (bf16[256,1024]{1,0:T(8,128)(2,1)S(1)}, bf16[256,1024]{1,0:T(8,128)(2,1)S(1)}, u32[]{:S(2)}, u32[]{:S(2)}) collective-permute-start(bf16[256,1024]{1,0:T(8,128)(2,1)S(1)} %shift.5), channel_id=1, source_target_pairs={{0,1},{1,0},{2,3},{3,2},{4,5},{5,4},{6,7},{7,6},{8,9},{9,8},{10,11... | collective-permute-start | bytes 1572872 | tf_op jit(solution)/shard_map/ppermute | solution.py:477
  5.6 12.4 %copy-start.9 = (s32[1,1024]{1,0:T(1,128)S(1)}, s32[1,1024]{1,0:T(1,128)}, u32[]{:S(2)}) copy-start(s32[1,1024]{1,0:T(1,128)} %mask.5) | copy-start | bytes 12292
  6.7 11.3 %copy-start.6 = (bf16[1,2,128,2,1024]{4,3,2,1,0:T(2,128)(2,1)S(1)}, bf16[1,2,128,2,1024]{4,3,2,1,0:T(2,128)(2,1)}, u32[]{:S(2)}) copy-start(bf16[1,2,128,2,1024]{4,3,2,1,0:T(2,128)(2,1)} %field.7) | copy-start | bytes 3145732
  6.8 6.0 %collective-permute-start.1 = (f16[128,512]{1,0:T(8,128)(2,1)S(1)}, f16[128,512]{1,0:T(8,128)(2,1)S(1)}, u32[]{:S(2)}, u32[]{:S(2)}) collective-permute-start(f16[128,512]{1,0:T(8,128)(2,1)S(1)} %get-tuple-element.92), channel_id=1, source_target_pairs={{0,2},{1,3},{2,0},{3,1},{4,6},{5,7},{6,4},{7,5},{8,10},{9,11},{10,... | collective-permute-start | bytes 393224 | tf_op jit(solution)/shard_map/ppermute | solution.py:477
  8.5 0.7 copy-start.8
  9.1 0.7 copy-start.12
  12.8 2.2 %copy-start = (bf16[2,2,2,512,512]{4,3,2,1,0:T(8,128)(2,1)S(1)}, bf16[2,2,2,512,512]{4,3,2,1,0:T(8,128)(2,1)}, u32[]{:S(2)}) copy-start(bf16[2,2,2,512,512]{4,3,2,1,0:T(8,128)(2,1)} %blocks.15) | copy-start | bytes 12582916
  15.0 8.2 %copy-start.1 = (bf16[2,2,2,512,512]{4,3,2,1,0:T(8,128)(2,1)S(1)}, bf16[2,2,2,512,512]{4,3,2,1,0:T(8,128)(2,1)}, u32[]{:S(2)}) copy-start(bf16[2,2,2,512,512]{4,3,2,1,0:T(8,128)(2,1)} %blocks.15) | copy-start | bytes 12582916
  19.7 3.5 %collective-permute-start.2 = (bf16[256,1024]{1,0:T(8,128)(2,1)S(1)}, bf16[256,1024]{1,0:T(8,128)(2,1)S(1)}, u32[]{:S(2)}, u32[]{:S(2)}) collective-permute-start(bf16[256,1024]{1,0:T(8,128)(2,1)S(1)} %shift.7), channel_id=1, source_target_pairs={{0,1},{1,0},{2,3},{3,2},{4,5},{5,4},{6,7},{7,6},{8,9},{9,8},{10,11... | collective-permute-start | bytes 1572872 | tf_op jit(solution)/shard_map/ppermute | solution.py:477
  19.8 14.5 %collective-permute-start.5 = (bf16[512,512]{1,0:T(8,128)(2,1)S(1)}, bf16[512,512]{1,0:T(8,128)(2,1)S(1)}, u32[]{:S(2)}, u32[]{:S(2)}) collective-permute-start(bf16[512,512]{1,0:T(8,128)(2,1)S(1)} %get-tuple-element.54), channel_id=1, source_target_pairs={{0,2},{1,3},{2,0},{3,1},{4,6},{5,7},{6,4},{7,5},{8,10},{9,11},{10,... | collective-permute-start | bytes 1572872 | tf_op jit(solution)/shard_map/ppermute | solution.py:477
  23.2 15.7 %copy-start.13 = (f32[2]{0:T(128)S(1)}, f32[2]{0:T(128)}, u32[]{:S(2)}) copy-start(f32[2]{0:T(128)} %freq.9) | copy-start | bytes 28
  23.2 15.7 %copy-start.14 = (s32[1,2]{1,0:T(1,128)S(1)}, s32[1,2]{1,0:T(1,128)}, u32[]{:S(2)}) copy-start(s32[1,2]{1,0:T(1,128)} %place.1) | copy-start | bytes 28
  25.8 10.6 %collective-permute-start.4 = (f32[2,2,512]{2,1,0:T(2,128)S(1)}, f32[2,2,512]{2,1,0:T(2,128)S(1)}, u32[]{:S(2)}, u32[]{:S(2)}) collective-permute-start(f32[2,2,512]{2,1,0:T(2,128)S(1)} %get-tuple-element.93), channel_id=1, source_target_pairs={{0,6},{1,7},{2,4},{3,5},{4,2},{5,3},{6,0},{7,1},{8,14},{9,15},{10,... | collective-permute-start | bytes 24584 | tf_op jit(solution)/shard_map/ppermute | solution.py:477
  28.4 8.1 %collective-permute-start.3 = (f32[2,2,512]{2,1,0:T(2,128)S(1)}, f32[2,2,512]{2,1,0:T(2,128)S(1)}, u32[]{:S(2)}, u32[]{:S(2)}) collective-permute-start(f32[2,2,512]{2,1,0:T(2,128)S(1)} %get-tuple-element.94), channel_id=1, source_target_pairs={{0,4},{1,5},{2,6},{3,7},{4,0},{5,1},{6,2},{7,3},{8,12},{9,13},{10,... | collective-permute-start | bytes 24584 | tf_op jit(solution)/shard_map/ppermute | solution.py:477
  36.5 13.1 %collective-permute-start.7 = (bf16[512,512]{1,0:T(8,128)(2,1)S(1)}, bf16[512,512]{1,0:T(8,128)(2,1)S(1)}, u32[]{:S(2)}, u32[]{:S(2)}) collective-permute-start(bf16[512,512]{1,0:T(8,128)(2,1)S(1)} %get-tuple-element.67), channel_id=1, source_target_pairs={{0,2},{1,3},{2,0},{3,1},{4,6},{5,7},{6,4},{7,5},{8,10},{9,11},{10,... | collective-permute-start | bytes 1572872 | tf_op jit(solution)/shard_map/ppermute | solution.py:477
  37.2 1.6 %collective-permute-start.6 = (f16[2,128,512]{2,1,0:T(8,128)(2,1)S(1)}, f16[2,128,512]{2,1,0:T(8,128)(2,1)S(1)}, u32[]{:S(2)}, u32[]{:S(2)}) collective-permute-start(f16[2,128,512]{2,1,0:T(8,128)(2,1)S(1)} %pad_maximum_fusion), channel_id=1, source_target_pairs={{0,1},{1,0},{2,3},{3,2},{4,5},{5,4},{6,7},{7,6},{8,9},{9,8},{10,11... | collective-permute-start | bytes 786440 | tf_op jit(solution)/shard_map/ppermute | solution.py:477
  52.3 4.6 %collective-permute-start.8 = (f32[4,512]{1,0:T(4,128)S(1)}, f32[4,512]{1,0:T(4,128)S(1)}, u32[]{:S(2)}, u32[]{:S(2)}) collective-permute-start(f32[4,512]{1,0:T(4,128)S(1)} %pad_maximum_fusion.3.edge_x), channel_id=1, source_target_pairs={{0,4},{1,5},{2,6},{3,7},{4,0},{5,1},{6,2},{7,3},{8,12},{9,13},{10,... | collective-permute-start | bytes 24584 | tf_op jit(solution)/shard_map/ppermute | solution.py:477
  59.2 5.6 %collective-permute-start.9 = (bf16[4,128,256]{2,1,0:T(8,128)(2,1)S(1)}, bf16[4,128,256]{2,1,0:T(8,128)(2,1)S(1)}, u32[]{:S(2)}, u32[]{:S(2)}) collective-permute-start(bf16[4,128,256]{2,1,0:T(8,128)(2,1)S(1)} %get-tuple-element.78), channel_id=1, source_target_pairs={{0,1},{1,0},{2,3},{3,2},{4,5},{5,4},{6,7},{7,6},{8,9},{9,8},{10,11... | collective-permute-start | bytes 786440 | tf_op jit(solution)/shard_map/ppermute | solution.py:477
  59.3 3.7 %collective-permute-start.10 = (f32[4,512]{1,0:T(4,128)S(1)}, f32[4,512]{1,0:T(4,128)S(1)}, u32[]{:S(2)}, u32[]{:S(2)}) collective-permute-start(f32[4,512]{1,0:T(4,128)S(1)} %get-tuple-element.82.edge), channel_id=1, source_target_pairs={{0,2},{1,3},{2,0},{3,1},{4,6},{5,7},{6,4},{7,5},{8,10},{9,11},{10,... | collective-permute-start | bytes 24584 | tf_op jit(solution)/shard_map/ppermute | solution.py:477
  64.8 1.6 %collective-permute-start.11 = (bf16[4,128,256]{2,1,0:T(8,128)(2,1)S(1)}, bf16[4,128,256]{2,1,0:T(8,128)(2,1)S(1)}, u32[]{:S(2)}, u32[]{:S(2)}) collective-permute-start(bf16[4,128,256]{2,1,0:T(8,128)(2,1)S(1)} %get-tuple-element.84), channel_id=1, source_target_pairs={{0,1},{1,0},{2,3},{3,2},{4,5},{5,4},{6,7},{7,6},{8,9},{9,8},{10,11... | collective-permute-start | bytes 786440 | tf_op jit(solution)/shard_map/ppermute | solution.py:477
  66.5 9.1 %collective-permute-start.12 = (bf16[2,128,256]{2,1,0:T(8,128)(2,1)S(1)}, bf16[2,128,256]{2,1,0:T(8,128)(2,1)S(1)}, u32[]{:S(2)}, u32[]{:S(2)}) collective-permute-start(bf16[2,128,256]{2,1,0:T(8,128)(2,1)S(1)} %get-tuple-element.85), channel_id=1, source_target_pairs={{0,0},{1,1},{2,16},{3,17},{4,4},{5,5},{6,20},{7,21},{8,8},{9,9},{1... | collective-permute-start | bytes 393224 | tf_op jit(solution)/shard_map/ppermute | solution.py:642
  69.6 8.9 %collective-permute-start.13 = (bf16[2,128,256]{2,1,0:T(8,128)(2,1)S(1)}, bf16[2,128,256]{2,1,0:T(8,128)(2,1)S(1)}, u32[]{:S(2)}, u32[]{:S(2)}) collective-permute-start(bf16[2,128,256]{2,1,0:T(8,128)(2,1)S(1)} %get-tuple-element.86), channel_id=1, source_target_pairs={{0,8},{1,9},{2,24},{3,25},{4,12},{5,13},{6,28},{7,29},{8,0},{9,1},... | collective-permute-start | bytes 393224 | tf_op jit(solution)/shard_map/ppermute | solution.py:642
  72.3 7.3 %collective-permute-start.15 = (bf16[2,128,256]{2,1,0:T(8,128)(2,1)S(1)}, bf16[2,128,256]{2,1,0:T(8,128)(2,1)S(1)}, u32[]{:S(2)}, u32[]{:S(2)}) collective-permute-start(bf16[2,128,256]{2,1,0:T(8,128)(2,1)S(1)} %get-tuple-element.87), channel_id=1, source_target_pairs={{0,10},{1,11},{2,26},{3,27},{4,14},{5,15},{6,30},{7,31},{8,2},{9,3... | collective-permute-start | bytes 393224 | tf_op jit(solution)/shard_map/ppermute | solution.py:642
  72.3 7.8 %collective-permute-start.14 = (bf16[2,128,256]{2,1,0:T(8,128)(2,1)S(1)}, bf16[2,128,256]{2,1,0:T(8,128)(2,1)S(1)}, u32[]{:S(2)}, u32[]{:S(2)}) collective-permute-start(bf16[2,128,256]{2,1,0:T(8,128)(2,1)S(1)} %get-tuple-element.88), channel_id=1, source_target_pairs={{0,2},{1,3},{2,18},{3,19},{4,6},{5,7},{6,22},{7,23},{8,10},{9,11},... | collective-permute-start | bytes 393224 | tf_op jit(solution)/shard_map/ppermute | solution.py:642
where the time goes:
time: 82.4 us; the launch traced here: 80.9 us
  Pallas kernels  30.6 us (37%)
  waiting for transfers between devices  23.5 us (29%)
  starting transfers between devices  16.8 us (20%)
  local copies, waits for them, and re-layouts  7.45 us (9%)
  other arithmetic  2.29 us (3%)
    pallas_call x14, Pallas kernels, call(): pl.pallas_call(body, in_specs=specs, out_specs=[vmem] * len(outs), out_sh...  30.6 us
    ppermute x12, waiting for transfers between devices, move(): return lax.ppermute(array, 'slab', [(i, i ^ k) for i in range(8)])  17.4 us
    ppermute x12, starting transfers between devices, move(): return lax.ppermute(array, 'slab', [(i, i ^ k) for i in range(8)])  9.22 us
    ppermute x4, starting transfers between devices, block_shards(): lax.ppermute(both[kz * 2 + kx], ('shot', 'slab'), route).astype(F32)  7.58 us
    unnamed x30, local copies, waits for them, and re-layouts  7.36 us
    ppermute x4, waiting for transfers between devices, block_shards(): lax.ppermute(both[kz * 2 + kx], ('shot', 'slab'), route).astype(F32)  6.05 us
  transfers between devices with their start and end apart: 16, of which 12 were waited for; matrix products, arithmetic and copies ran while one was open for 2% of the time, Pallas kernels for 24%

commit v1 on v0

--- a/solution.py
+++ b/solution.py
@@ -178,18 +178,34 @@
     return lax.dot_general(left, right, (((0,), (0,)), ((), ())), preferred_element_type=F32)
 
 
-def shift_kernel(conjugate, other, meta, freq, mask, field, slowness, out):
-    rows = slowness.shape[1]
-    f = meta[0] ^ other
-    sine, cosine = sincos(freq[f] * slowness[0])
-    real = field[0, f, :, 0, :].astype(F32)
-    imag = field[0, f, :, 1, :].astype(F32)
-    if conjugate:
-        keep = mask[...].astype(F32)
-        real = real * keep
-        imag = -(imag * keep)
+def rotate(omega, slow, real, imag, out):
+    rows = slow.shape[0]
+    sine, cosine = sincos(omega * slow)
     out[:rows] = (real * cosine - imag * sine).astype(BF16)
     out[rows:] = (imag * cosine + real * sine).astype(BF16)
+
+
+def receiver_kernel(meta, scalars, mask, field, slowness, own, other):
+    keep = mask[...].astype(F32)
+    for k, out in ((1, other), (0, own)):
+        f = meta[0] ^ k
+        real = field[0, f, :, 0, :].astype(F32) * keep
+        imag = -(field[0, f, :, 1, :].astype(F32) * keep)
+        rotate(scalars[f], slowness[0], real, imag, out)
+
+
+def other_kernel(meta, scalars, field, slowness, out, raw, slow):
+    f = meta[0] ^ 1
+    rotate(scalars[f], slowness[0], field[0, f, :, 0, :].astype(F32), field[0, f, :, 1, :].astype(F32), out)
+    raw[...] = field[0, meta[0]]
+    slow[...] = slowness[0]
+
+
+def own_kernel(meta, scalars, raw, slow, inverse, out, blocks, sem):
+    fetch = pltpu.make_async_copy(inverse.at[meta[0]], blocks, sem)
+    fetch.start()
+    rotate(scalars[meta[0]], slow[...], raw[:, 0, :].astype(F32), raw[:, 1, :].astype(F32), out)
+    fetch.wait()
 
 
 def edge_rows(meta, blocks, block, lanes):
@@ -208,12 +224,11 @@
     return rr - ii, ri + ir
 
 
-def slab_kernel(meta, coupling, own, core, blocks, same, cross, partial_edge, ends):
-    blocks = blocks.at[meta[0]]
+def slab_kernel(meta, scalars, own, core, blocks, same, cross, ends):
     rows = own.shape[0] // 2
     half = blocks.shape[2]
-    f, zz, xb, local = meta[0], meta[1], meta[2], meta[3]
-    cr, ci = coupling[f, 0], coupling[f, 1]
+    f, zz = meta[0], meta[1]
+    cr, ci = scalars[2 + 2 * f], scalars[3 + 2 * f]
     spot = lax.broadcasted_iota(jnp.int32, (16, half), 1)
     line = lax.broadcasted_iota(jnp.int32, (16, half), 0)
     solved, columns = [], []
@@ -239,7 +254,6 @@
     upper = couple(1, solved[0][0][:, half - 1 :], solved[0][1][:, half - 1 :])
     lower = couple(0, upper[0][:, 0:1], upper[1][:, 0:1])
     first = zz == 0
-    pieces = []
     for part in range(2):
         low, high = lower[part].astype(BF16), upper[part].astype(BF16)
         mine, away = jnp.where(first, low, high), jnp.where(first, high, low)
@@ -247,24 +261,31 @@
             at = slice((2 * n + part) * rows, (2 * n + part + 1) * rows)
             same[at] = mine[n * rows : (n + 1) * rows]
             cross[at] = away[n * rows : (n + 1) * rows]
-        pieces.append(jnp.concatenate([mine, away], axis=1))
-    edges = [0.0, 0.0]
-    for n in range(2):
-        lanes = pl.ds(pl.multiple_of((local ^ n) * rows, rows), rows)
-        row = edge_rows(meta, blocks, xb, lanes)
-        real = dot(row, pieces[0][n * rows : (n + 1) * rows])
-        imag = dot(row, pieces[1][n * rows : (n + 1) * rows])
-        er, ei = edge_product(xb, real, imag)
-        edges = [edges[0] + er, edges[1] + ei]
-    partial_edge[0:1] = edges[0][:, :half]
-    partial_edge[1:2] = edges[1][:, :half]
-    partial_edge[2:3] = edges[0][:, half:]
-    partial_edge[3:4] = edges[1][:, half:]
-
-
-def phase_kernel(meta, freq, place, own, core, far, far_core, sine, cosine, weight):
+
+
+def edge_kernel(meta, blocks, same0, cross0, same1, cross1, edge_same, edge_cross):
+    rows = same0.shape[0] // 4
+    xb, local = meta[2], meta[3]
+    for refs, out in (((same0, same1), edge_same), ((cross0, cross1), edge_cross)):
+        for part in range(2):
+            total = 0.0
+            for n in range(2):
+                lanes = pl.ds(pl.multiple_of((local ^ n) * rows, rows), rows)
+                row = edge_rows(meta, blocks, xb, lanes)
+                at = slice((2 * n + part) * rows, (2 * n + part + 1) * rows)
+                total = total + dot(row, jnp.concatenate([ref[at] for ref in refs], axis=1))
+            if part == 0:
+                real = total
+        er, ei = edge_product(xb, real, total)
+        half = same0.shape[1]
+        for k in range(2):
+            out[2 * k : 2 * k + 1] = er[:, k * half : (k + 1) * half]
+            out[2 * k + 1 : 2 * k + 2] = ei[:, k * half : (k + 1) * half]
+
+
+def phase_kernel(meta, scalars, place, own, core, far, far_core, sine, cosine, weight):
     rows, half = own.shape
-    omega = freq[meta[0]]
+    omega = scalars[meta[0]]
     for k, piece in enumerate((own, core, far, far_core)):
         start = pl.multiple_of((meta[3] ^ k) * rows, rows)
         s, c = sincos(omega * (piece[...].astype(F32) + MIDDLE))
@@ -276,8 +297,8 @@
     weight[...] = -omega / (1.0 + spread * (16.0 / (NX * NX)))
 
 
-def turn_value(meta, coupling, blocks, block):
-    cr, ci = coupling[meta[0], 0], coupling[meta[0], 1]
+def turn_value(meta, scalars, blocks, block):
+    cr, ci = scalars[2 + 2 * meta[0]], scalars[3 + 2 * meta[0]]
     ar = blocks[0, 1, 0:16, 0:128].astype(F32)[0:1, 0:1]
     ai = blocks[1, 1, 0:16, 0:128].astype(F32)[0:1, 0:1]
     first = block == 0
@@ -285,9 +306,8 @@
 
 
 def column_kernel(
-    meta, coupling, near, far, blocks, edge_same, edge_cross, sine, cosine, solved, shifted, own_edge, real, imag
+    meta, scalars, near, far, blocks, edge_same, edge_cross, sine, cosine, solved, shifted, own_edge, real, imag
 ):
-    blocks = blocks.at[meta[0]]
     rows = near.shape[0] // 4
     half = near.shape[1]
     xb = meta[2]
@@ -295,8 +315,8 @@
         start = pl.multiple_of((meta[3] ^ k) * rows, rows)
         real[pl.ds(start, rows)] = piece[2 * n * rows : (2 * n + 1) * rows]
         imag[pl.ds(start, rows)] = piece[(2 * n + 1) * rows : (2 * n + 2) * rows]
-    cr, ci = coupling[meta[0], 0], coupling[meta[0], 1]
-    ar, ai = turn_value(meta, coupling, blocks, xb)
+    cr, ci = scalars[2 + 2 * meta[0]], scalars[3 + 2 * meta[0]]
+    ar, ai = turn_value(meta, scalars, blocks, xb)
     row = edge_rows(meta, blocks, xb, slice(0, half))
     own_real, own_imag = edge_product(xb, dot(row, real[...]), dot(row, imag[...]))
     hr = edge_same[0:1] + edge_cross[0:1] + ar * own_real - ai * own_imag
@@ -330,7 +350,6 @@
 
 
 def both_kernel(meta, shifted, blocks, solved, edge):
-    blocks = blocks.at[meta[0]]
     half = shifted.shape[1]
     xb, zz = meta[2], meta[1]
     left = jnp.concatenate([blocks[0, xb], blocks[1, xb]], axis=0)
@@ -364,9 +383,8 @@
     return jnp.where(first, ends[0:1], ends[2:3]), jnp.where(first, ends[1:2], ends[3:4])
 
 
-def turn_kernel(meta, coupling, edge_x, near_x, edge_y0, edge_y1, ends, blocks, whole, edge):
-    blocks = blocks.at[meta[0]]
-    ar, ai = turn_value(meta, coupling, blocks, meta[2])
+def turn_kernel(meta, scalars, edge_x, near_x, edge_y0, edge_y1, ends, blocks, whole, edge):
+    ar, ai = turn_value(meta, scalars, blocks, meta[2])
     zz = meta[1]
     yr, yi = pick_edge(zz, edge_rows(meta, blocks, zz, slice(0, ends.shape[1])).astype(F32))
     pr, pi = pick_end(ends, meta[2])
@@ -388,8 +406,7 @@
     return high.astype(F32), (value - high.astype(F32))
 
 
-def between_kernel(meta, whole, inverse, source, receiver, weight, out, keep, send, image):
-    blocks = inverse.at[meta[0]]
+def between_kernel(meta, whole, blocks, source, receiver, weight, out, keep, send, image):
     high, low = split(whole[...])
     left = jnp.concatenate([high, low, high, low], axis=0).astype(BF16)
     by_real = dot_t(left, blocks[0, meta[1]])
@@ -408,11 +425,10 @@
 
 
 def second_image_kernel(
-    meta, coupling, source, receiver, weight, rows_y, edge, near, ends, blocks, keep, send, image
+    meta, scalars, source, receiver, weight, rows_y, edge, near, ends, blocks, keep, send, image
 ):
     half = source.shape[1]
-    blocks = blocks.at[meta[0]]
-    ar, ai = turn_value(meta, coupling, blocks, meta[1])
+    ar, ai = turn_value(meta, scalars, blocks, meta[1])
     pr, pi = pick_end(ends, meta[2])
     qr, qi = pick_end(ends, meta[1])
 
@@ -456,8 +472,10 @@
     meta = jnp.stack(
         [slab & 1, (slab >> 1) & 1, slab >> 2, slab & 3, shot >> 1, shot & 1]
     ).astype(jnp.int32)
+    scalars = jnp.concatenate([frequency, coupling.reshape(-1)])
     smem = pl.BlockSpec(memory_space=SMEM)
     vmem = pl.BlockSpec(memory_space=VMEM)
+    hbm = pl.BlockSpec(memory_space=pltpu.HBM)
 
     def shape(dtype, *sizes):
         return jax.ShapeDtypeStruct(sizes, dtype)
@@ -478,60 +496,95 @@
 
     same, far, edges = [], [], []
     for n, field in enumerate((source_field, residual_data)):
-        mask = receiver_lines
-        if n == 1:
-            mask, edges[0] = lax.optimization_barrier((mask, edges[0]))
-        halves = []
-        for other in (1, 0):
-            halves.append(
-                call(
-                    partial(shift_kernel, n == 1, other),
-                    "shift",
-                    [smem, smem, vmem, vmem, vmem],
-                    [shape(BF16, 2 * rows, length)],
-                    [],
-                    12,
-                    meta,
-                    frequency,
-                    mask,
-                    field,
-                    slowness,
-                )
+        cut = shape(BF16, 2 * rows, length)
+        if n == 0:
+            core, raw, slow = call(
+                other_kernel,
+                "other",
+                [smem, smem, vmem, vmem],
+                [cut, shape(BF16, rows, 2, length), shape(F32, rows, length)],
+                [],
+                12,
+                meta,
+                scalars,
+                field,
+                slowness,
             )
-        own, core = halves[1][0], move(halves[0][0], 1)
+            own, blocks = call(
+                own_kernel,
+                "own",
+                [smem, smem, vmem, vmem, hbm],
+                [cut, shape(BF16, *line_inverse.shape[1:])],
+                [pltpu.SemaphoreType.DMA],
+                48,
+                meta,
+                scalars,
+                raw,
+                slow,
+                line_inverse,
+            )
+        else:
+            mask, near_slow = lax.optimization_barrier((receiver_lines, near_slow))
+            own, core = call(
+                receiver_kernel,
+                "receiver",
+                [smem, smem, vmem, vmem, vmem],
+                [cut] * 2,
+                [],
+                12,
+                meta,
+                scalars,
+                mask,
+                field,
+                slowness,
+            )
+            far_slow = move(near_slow, 2)
+        core = move(core, 1)
+        mine, cross, ends = call(
+            slab_kernel,
+            "slab",
+            [smem, smem, vmem, vmem, vmem],
+            [shape(BF16, 4 * rows, half)] * 2 + [shape(F32, 4, half)],
+            [],
+            16,
+            meta,
+            scalars,
+            own,
+            core,
+            blocks,
+        )
+        same.append(mine)
+        edges.append(cross)
         if n == 0:
-            layer = (slowness[1] - MIDDLE).astype(jnp.float16)
+            far.append(move(cross, 2))
+            layer, same[0] = lax.optimization_barrier((slowness[1], same[0]))
+            layer = (layer - MIDDLE).astype(jnp.float16)
             low, high = layer[:, :half], layer[:, half:]
             first = meta[1] == 0
             own_slow = jnp.where(first, low, high)
-            far_slow = move(jnp.where(first, high, low), 2)
-            core, far_slow = lax.optimization_barrier((core, far_slow))
-        mine, cross, edge, ends = call(
-            slab_kernel,
-            "slab",
-            [smem, smem, vmem, vmem, vmem],
-            [shape(BF16, 4 * rows, half)] * 2 + [shape(F32, 4, half)] * 2,
-            [],
-            16,
-            meta,
-            coupling,
-            own,
-            core,
-            line_inverse,
-        )
-        same.append(mine)
-        edges.append(edge)
-        if n == 0:
-            far.append(move(cross, 2))
-    own_slow, far_slow, edges[1] = lax.optimization_barrier((own_slow, far_slow, edges[1]))
-    edges = jnp.stack(edges)
-    edge_same = move(edges[:, :2], 4)
-    edge_cross = move(edges[:, 2:], 6)
-    cross, edge_same, edge_cross, far[0] = lax.optimization_barrier((cross, edge_same, edge_cross, far[0]))
+            near_slow = jnp.where(first, high, low)
+    edges = call(
+        edge_kernel,
+        "edge",
+        [smem] + [vmem] * 5,
+        [shape(F32, 4, half)] * 2,
+        [],
+        8,
+        meta,
+        blocks,
+        same[0],
+        edges[0],
+        same[1],
+        edges[1],
+    )
+    edge_same = move(edges[0], 4)
+    edge_cross = move(edges[1], 6)
+    cross, far[0] = lax.optimization_barrier((cross, far[0]))
     far.append(move(cross, 2))
     pair = shape(BF16, 2 * half, half)
     line = shape(F32, 2, half)
     four = shape(F32, 4, half)
+    far_slow, edge_same, edge_cross = lax.optimization_barrier((far_slow, edge_same, edge_cross))
     core_slow = move(jnp.stack([own_slow, far_slow]), 1)
     block = shape(F32, half, half)
     sine, cosine, weight = call(
@@ -542,7 +595,7 @@
         [],
         8,
         meta,
-        frequency,
+        scalars,
         shot_positions,
         own_slow.astype(F32),
         core_slow[0].astype(F32),
@@ -561,16 +614,16 @@
             [VMEM((half, half), BF16)] * 2,
             16,
             meta,
-            coupling,
+            scalars,
             same[n],
             far[n],
-            line_inverse,
-            edge_same[n],
-            edge_cross[n],
+            blocks,
+            edge_same[2 * n : 2 * n + 2],
+            edge_cross[2 * n : 2 * n + 2],
             sine,
             cosine,
         )
-        v, across = call(both_kernel, "both", [smem] + [vmem] * 2, [pair, line], [], 20, meta, turned, line_inverse)
+        v, across = call(both_kernel, "both", [smem] + [vmem] * 2, [pair, line], [], 20, meta, turned, blocks)
         solved.append(x0)
         finals.append(v)
         edge_x.append(edge)
@@ -585,12 +638,12 @@
         [],
         4,
         meta,
-        coupling,
+        scalars,
         edge_x,
         near_x,
         *edge_y,
         ends,
-        line_inverse,
+        blocks,
     )
     near_y = move(edge, 2)
     cut = shape(BF16, 4, rows, half // 2)
@@ -604,11 +657,12 @@
         12,
         meta,
         coupled,
-        line_inverse,
+        blocks,
         solved[0],
         solved[1],
         weight,
     )
+    near_y, rows_y, send0 = lax.optimization_barrier((near_y, rows_y, send0))
     keep1, send1 = call(
         second_image_kernel,
         "second_image",
@@ -617,7 +671,7 @@
         scratch,
         12,
         meta,
-        coupling,
+        scalars,
         finals[0],
         finals[1],
         weight,
@@ -625,18 +679,19 @@
         edge,
         near_y,
         ends,
-        line_inverse,
+        blocks,
     )
     part0 = keep0.astype(F32) + move(send0, 1).astype(F32)
     part1 = keep1.astype(F32) + move(send1, 1).astype(F32)
     both = jnp.stack([part0, part1], axis=1).astype(BF16)
     total = 0.0
-    for kz in range(2):
-        for kx in range(2):
+    for kz in (1, 0):
+        for kx in (1, 0):
             route = []
             for s in range(4):
                 for b in range(8):
-                    sy, sx, bx, by, bc = s // 2, s % 2, b // 4, (b // 2) % 2, b % 2
+                    sy, sx, bx, bc = s // 2, s % 2, b // 4, b % 2
+                    by = (b // 2) % 2
                     target = (by * 2 + (sx ^ kx)) * 8 + bx * 4 + (sy ^ kz) * 2 + bc
                     route.append((s * 8 + b, target))
             total = total + lax.ppermute(both[kz * 2 + kx], ("shot", "slab"), route).astype(F32)

time: 82.4 us -> 75 us (0.910); the launches traced: 80.9 us -> 74.7 us
  waiting for transfers between devices: 23.5 us -> 19.2 us
  local copies, waits for them, and re-layouts: 7.45 us -> 3.36 us
  starting transfers between devices: 16.8 us -> 18.9 us
    unnamed x30 -> x12, local copies, waits for them, and re-layouts: 7.36 us -> 2.47 us
    ppermute x12, waiting for transfers between devices: 17.4 us -> 13 us  [move(): return lax.ppermute(array, 'slab', [(i, i ^ k) for i in range(8)])]
    ppermute x12, starting transfers between devices: 9.22 us -> 11.2 us  [move(): return lax.ppermute(array, 'slab', [(i, i ^ k) for i in range(8)])]
    convert_element_type x2 -> x1, other arithmetic: 1.11 us -> 0.05 us  [block_shards(): layer = (layer - MIDDLE).astype(jnp.float16)]
  transfers between devices with their start and end apart: 16 -> 16, of which waited for: 12 -> 11; matrix products, arithmetic and copies ran while one was open for 2% -> 0% of each run, Pallas kernels for 24% -> 25%
where the time goes in v1:
time: 75 us; the launch traced here: 74.7 us
  Pallas kernels  31.1 us (41%)
  waiting for transfers between devices  19.2 us (26%)
  starting transfers between devices  18.9 us (25%)
  local copies, waits for them, and re-layouts  3.36 us (4%)
  other arithmetic  1.94 us (3%)
    pallas_call x14, Pallas kernels, call(): pl.pallas_call(body, in_specs=specs, out_specs=[vmem] * len(outs), out_sh...  31.1 us
    ppermute x12, waiting for transfers between devices, move(): return lax.ppermute(array, 'slab', [(i, i ^ k) for i in range(8)])  13 us
    ppermute x12, starting transfers between devices, move(): return lax.ppermute(array, 'slab', [(i, i ^ k) for i in range(8)])  11.2 us
    ppermute x4, starting transfers between devices, block_shards(): lax.ppermute(both[kz * 2 + kx], ('shot', 'slab'), route).astype(F32)  7.7 us
    ppermute x4, waiting for transfers between devices, block_shards(): lax.ppermute(both[kz * 2 + kx], ('shot', 'slab'), route).astype(F32)  6.19 us
    unnamed x12, local copies, waits for them, and re-layouts  2.47 us
  transfers between devices with their start and end apart: 16, of which 11 were waited for; matrix products, arithmetic and copies ran while one was open for 0% of the time, Pallas kernels for 25%

profile of v1, /device:TPU:4, one launch (start us, length us, event | category | flops | bytes accessed | tf_op | source)
XLA Modules:
  0.0 74.7 jit_solution(4165870500843566006)
XLA Ops:
  0.0 0.8 %reshape.7 = f32[4]{0:T(128)S(1)} reshape(f32[2,2]{1,0:T(2,128)} %param.15) | data formatting | bytes 32 | tf_op jit(solution)/shard_map/reshape | solution.py:475
  0.8 0.7 pad_maximum_fusion.3.scalars
  1.5 0.1 stack.48.meta
  1.6 0.0 copy-start
  1.6 1.2 %copy-done = f32[2,128,1024]{2,1,0:T(8,128)S(1)} copy-done((f32[2,128,1024]{2,1,0:T(8,128)S(1)}, f32[2,128,1024]{2,1,0:T(8,128)}, u32[]{:S(2)}) %copy-start) | copy-done | bytes 1048600
  2.8 1.2 %copy-done.2 = bf16[1,2,128,2,1024]{4,3,2,1,0:T(2,128)(2,1)S(1)} copy-done((bf16[1,2,128,2,1024]{4,3,2,1,0:T(2,128)(2,1)S(1)}, bf16[1,2,128,2,1024]{4,3,2,1,0:T(2,128)(2,1)}, u32[]{:S(2)}) %copy-start.2) | copy-done | bytes 1048600
  4.0 1.7 %other.1 = (bf16[256,1024]{1,0:T(8,128)(2,1)S(1)}, bf16[128,2,1024]{2,1,0:T(2,128)(2,1)S(1)}, f32[128,1024]{1,0:T(8,128)S(1)}) custom-call(s32[6]{0:T(128)S(1)} %stack.48.meta, f32[6]{0:T(128)S(1)} %pad_maximum_fusion.3.scalars, bf16[1,2,128,2,1024]{4,3,2,1,0:T(2,128)(2,1)S(1)} %copy-done.2, f32[2,128,1024]{2,1,0:T(8,128)S(1)} %copy-done), custom_call_target="tpu_custom_call" | custom-call | tf_op jit(solution)/shard_map/other/pallas_call | solution.py:484
  5.7 0.1 collective-permute-start
  5.8 2.1 %own.1 = (bf16[256,1024]{1,0:T(8,128)(2,1)S(1)}, bf16[2,2,512,512]{3,2,1,0:T(8,128)(2,1)S(1)}) custom-call(s32[6]{0:T(128)S(1)} %stack.48.meta, f32[6]{0:T(128)S(1)} %pad_maximum_fusion.3.scalars, bf16[128,2,1024]{2,1,0:T(2,128)(2,1)S(1)} %get-tuple-element.53.raw, f32[128,1024]{1,0:T(8,128)S(1)} %get-tuple-element.54.slow, bf16[2,2,2,512,512]{4,3,2,1,0:T(8,128)(2,1)} %inverse.1), custom_call_target="tpu_custom_call" | custom-call | tf_op jit(solution)/shard_map/own/pallas_call | solution.py:484
  8.0 0.0 copy-done.1
  8.0 0.0 copy-start.3
  8.0 0.0 copy-start.4
  8.1 0.0 collective-permute-done.core
  8.1 2.9 %slab.2 = (bf16[512,512]{1,0:T(8,128)(2,1)S(1)}, bf16[512,512]{1,0:T(8,128)(2,1)S(1)}, f32[4,512]{1,0:T(4,128)}) custom-call(s32[6]{0:T(128)S(1)} %stack.48.meta, f32[6]{0:T(128)S(1)} %pad_maximum_fusion.3.scalars, bf16[256,1024]{1,0:T(8,128)(2,1)S(1)} %get-tuple-element.55.own, bf16[256,1024]{1,0:T(8,128)(2,1)S(1)} %collective-permute-done.core, ...), custom_call_target="tpu_custom_call" | custom-call | tf_op jit(solution)/shard_map/slab/pallas_call | solution.py:484
  11.1 0.1 fusion.11
  11.1 0.0 copy-done.3
  11.1 0.0 copy-done.4
  11.1 2.9 %receiver.1 = (bf16[256,1024]{1,0:T(8,128)(2,1)S(1)}, bf16[256,1024]{1,0:T(8,128)(2,1)S(1)}) custom-call(s32[6]{0:T(128)S(1)} %stack.48.meta, f32[6]{0:T(128)S(1)} %pad_maximum_fusion.3.scalars, s32[1,1024]{1,0:T(1,128)S(1)} %copy-done.4, bf16[1,2,128,2,1024]{4,3,2,1,0:T(2,128)(2,1)S(1)} %copy-done.3, f32[2,128,1024]{2,1,0:T(8,128)S(1)} %copy-done.1), custom_call_target="tpu_custom_call" | custom-call | tf_op jit(solution)/shard_map/receiver/pallas_call | solution.py:484
  14.0 0.6 collective-permute-start.1
  14.6 1.6 %collective-permute-start.2 = (bf16[512,512]{1,0:T(8,128)(2,1)S(1)}, bf16[512,512]{1,0:T(8,128)(2,1)S(1)}, u32[]{:S(2)}, u32[]{:S(2)}) collective-permute-start(bf16[512,512]{1,0:T(8,128)(2,1)S(1)} %get-tuple-element.65.cross0), channel_id=1, source_target_pairs={{0,2},{1,3},{2,0},{3,1},{4,6},{5,7},{6,4},{7,5},{8,10},{9,11},{10,... | collective-permute-start | bytes 1572872 | tf_op jit(solution)/shard_map/ppermute | solution.py:495
  16.1 0.4 collective-permute-start.3
  16.6 0.0 collective-permute-done.1.core
  16.6 2.3 %slab.3 = (bf16[512,512]{1,0:T(8,128)(2,1)S(1)}, bf16[512,512]{1,0:T(8,128)(2,1)S(1)}, f32[4,512]{1,0:T(4,128)S(1)}) custom-call(s32[6]{0:T(128)S(1)} %stack.48.meta, f32[6]{0:T(128)S(1)} %pad_maximum_fusion.3.scalars, bf16[256,1024]{1,0:T(8,128)(2,1)S(1)} %get-tuple-element.62.own, bf16[256,1024]{1,0:T(8,128)(2,1)S(1)} %collective-permute-done.1.core, ...), custom_call_target="tpu_custom_call" | custom-call | tf_op jit(solution)/shard_map/slab/pallas_call | solution.py:484
  18.9 0.9 %edge.1 = (f32[4,512]{1,0:T(4,128)S(1)}, f32[4,512]{1,0:T(4,128)S(1)}) custom-call(s32[6]{0:T(128)S(1)} %stack.48.meta, bf16[2,2,512,512]{3,2,1,0:T(8,128)(2,1)S(1)} %get-tuple-element.57.blocks, bf16[512,512]{1,0:T(8,128)(2,1)S(1)} %get-tuple-element.59.same0.near, bf16[512,512]{1,0:T(8,128)(2,1)S(1)} %get-tuple-element.65.cross0, ...), custom_call_target="tpu_custom_call" | custom-call | tf_op jit(solution)/shard_map/edge/pallas_call | solution.py:484
  19.9 2.6 %collective-permute-start.4 = (f32[4,512]{1,0:T(4,128)S(1)}, f32[4,512]{1,0:T(4,128)S(1)}, u32[]{:S(2)}, u32[]{:S(2)}) collective-permute-start(f32[4,512]{1,0:T(4,128)S(1)} %get-tuple-element.69), channel_id=1, source_target_pairs={{0,4},{1,5},{2,6},{3,7},{4,0},{5,1},{6,2},{7,3},{8,12},{9,13},{10,... | collective-permute-start | bytes 24584 | tf_op jit(solution)/shard_map/ppermute | solution.py:495
  22.6 1.4 %collective-permute-start.5 = (f32[4,512]{1,0:T(4,128)S(1)}, f32[4,512]{1,0:T(4,128)S(1)}, u32[]{:S(2)}, u32[]{:S(2)}) collective-permute-start(f32[4,512]{1,0:T(4,128)S(1)} %get-tuple-element.70), channel_id=1, source_target_pairs={{0,6},{1,7},{2,4},{3,5},{4,2},{5,3},{6,0},{7,1},{8,14},{9,15},{10,... | collective-permute-start | bytes 24584 | tf_op jit(solution)/shard_map/ppermute | solution.py:495
  23.9 5.6 %collective-permute-done.2.far = bf16[512,512]{1,0:T(8,128)(2,1)S(1)} collective-permute-done((bf16[512,512]{1,0:T(8,128)(2,1)S(1)}, bf16[512,512]{1,0:T(8,128)(2,1)S(1)}, u32[]{:S(2)}, u32[]{:S(2)}) %collective-permute-start.2) | collective-permute-done | bytes 524320 | tf_op jit(solution)/shard_map/ppermute | solution.py:495
  29.5 1.4 %collective-permute-start.7 = (bf16[512,512]{1,0:T(8,128)(2,1)S(1)}, bf16[512,512]{1,0:T(8,128)(2,1)S(1)}, u32[]{:S(2)}, u32[]{:S(2)}) collective-permute-start(bf16[512,512]{1,0:T(8,128)(2,1)S(1)} %get-tuple-element.80.cross1), channel_id=1, source_target_pairs={{0,2},{1,3},{2,0},{3,1},{4,6},{5,7},{6,4},{7,5},{8,10},{9,11},{10,... | collective-permute-start | bytes 1572872 | tf_op jit(solution)/shard_map/ppermute | solution.py:495
  30.9 1.4 %collective-permute-done.3 = f16[128,512]{1,0:T(8,128)(2,1)S(1)} collective-permute-done((f16[128,512]{1,0:T(8,128)(2,1)S(1)}, f16[128,512]{1,0:T(8,128)(2,1)S(1)}, u32[]{:S(2)}, u32[]{:S(2)}) %collective-permute-start.3) | collective-permute-done | bytes 131104 | tf_op jit(solution)/shard_map/ppermute | solution.py:495
  32.3 0.0 collective-permute-done.4
  32.3 2.2 %collective-permute-done.5 = f32[4,512]{1,0:T(4,128)S(1)} collective-permute-done((f32[4,512]{1,0:T(4,128)S(1)}, f32[4,512]{1,0:T(4,128)S(1)}, u32[]{:S(2)}, u32[]{:S(2)}) %collective-permute-start.5) | collective-permute-done | bytes 8224 | tf_op jit(solution)/shard_map/ppermute | solution.py:495
  34.5 0.1 pad_maximum_fusion
  34.6 0.1 collective-permute-start.6
  34.7 1.5 %collective-permute-done.6 = f16[2,128,512]{2,1,0:T(8,128)(2,1)S(1)} collective-permute-done((f16[2,128,512]{2,1,0:T(8,128)(2,1)S(1)}, f16[2,128,512]{2,1,0:T(8,128)(2,1)S(1)}, u32[]{:S(2)}, u32[]{:S(2)}) %collective-permute-start.6) | collective-permute-done | bytes 262176 | tf_op jit(solution)/shard_map/ppermute | solution.py:495
  36.2 0.1 fusion.9
  36.3 0.0 copy-done.5
  36.3 2.1 %phase.1 = (f32[512,512]{1,0:T(8,128)S(1)}, f32[512,512]{1,0:T(8,128)S(1)}, f32[512,512]{1,0:T(8,128)S(1)}) custom-call(s32[6]{0:T(128)S(1)} %stack.48.meta, f32[6]{0:T(128)S(1)} %pad_maximum_fusion.3.scalars, s32[1,2]{1,0:T(1,128)S(1)} %copy-done.5, f32[128,512]{1,0:T(8,128)S(1)} %get-tuple-element.109.own, f32[128,512]{1,0:T(8,128)S(1)} %get-tuple-element.106.core, ...), custom_call_target="tpu_custom_call" | custom-call | tf_op jit(solution)/shard_map/phase/pallas_call | solution.py:484
  38.4 2.8 %column.2 = (bf16[1024,512]{1,0:T(8,128)(2,1)S(1)}, bf16[1024,512]{1,0:T(8,128)(2,1)S(1)}, f32[2,512]{1,0:T(2,128)S(1)}) custom-call(s32[6]{0:T(128)S(1)} %stack.48.meta, f32[6]{0:T(128)S(1)} %pad_maximum_fusion.3.scalars, bf16[512,512]{1,0:T(8,128)(2,1)S(1)} %get-tuple-element.59.same0.near, bf16[512,512]{1,0:T(8,128)(2,1)S(1)} %collective-permute-done.2.far, ...), custom_call_target="tpu_custom_call" | custom-call | tf_op jit(solution)/shard_map/column/pallas_call | solution.py:484
  41.1 3.3 %both.2 = (bf16[1024,512]{1,0:T(8,128)(2,1)S(1)}, f32[2,512]{1,0:T(2,128)S(1)}) custom-call(s32[6]{0:T(128)S(1)} %stack.48.meta, bf16[1024,512]{1,0:T(8,128)(2,1)S(1)} %get-tuple-element.77.shifted, bf16[2,2,512,512]{3,2,1,0:T(8,128)(2,1)S(1)} %get-tuple-element.57.blocks), custom_call_target="tpu_custom_call" | custom-call | tf_op jit(solution)/shard_map/both/pallas_call | solution.py:484
  44.4 0.0 collective-permute-done.7.far
  44.4 2.7 %column.3 = (bf16[1024,512]{1,0:T(8,128)(2,1)S(1)}, bf16[1024,512]{1,0:T(8,128)(2,1)S(1)}, f32[2,512]{1,0:T(2,128)S(1)}) custom-call(s32[6]{0:T(128)S(1)} %stack.48.meta, f32[6]{0:T(128)S(1)} %pad_maximum_fusion.3.scalars, bf16[512,512]{1,0:T(8,128)(2,1)S(1)} %get-tuple-element.79.same1.near, bf16[512,512]{1,0:T(8,128)(2,1)S(1)} %collective-permute-done.7.far, ...), custom_call_target="tpu_custom_call" | custom-call | tf_op jit(solution)/shard_map/column/pallas_call | solution.py:484
  47.1 1.1 %collective-permute-start.8 = (f32[4,512]{1,0:T(4,128)S(1)}, f32[4,512]{1,0:T(4,128)S(1)}, u32[]{:S(2)}, u32[]{:S(2)}) collective-permute-start(f32[4,512]{1,0:T(4,128)S(1)} %pad_maximum_fusion.2.edge_x), channel_id=1, source_target_pairs={{0,4},{1,5},{2,6},{3,7},{4,0},{5,1},{6,2},{7,3},{8,12},{9,13},{10,... | collective-permute-start | bytes 24584 | tf_op jit(solution)/shard_map/ppermute | solution.py:495
  48.2 3.3 %both.3 = (bf16[1024,512]{1,0:T(8,128)(2,1)S(1)}, f32[2,512]{1,0:T(2,128)S(1)}) custom-call(s32[6]{0:T(128)S(1)} %stack.48.meta, bf16[1024,512]{1,0:T(8,128)(2,1)S(1)} %get-tuple-element.83.shifted, bf16[2,2,512,512]{3,2,1,0:T(8,128)(2,1)S(1)} %get-tuple-element.57.blocks), custom_call_target="tpu_custom_call" | custom-call | tf_op jit(solution)/shard_map/both/pallas_call | solution.py:484
  51.5 0.2 collective-permute-done.8.near_x
  51.8 0.7 turn.1
  52.5 1.4 %collective-permute-start.9 = (f32[4,512]{1,0:T(4,128)S(1)}, f32[4,512]{1,0:T(4,128)S(1)}, u32[]{:S(2)}, u32[]{:S(2)}) collective-permute-start(f32[4,512]{1,0:T(4,128)S(1)} %get-tuple-element.91.edge), channel_id=1, source_target_pairs={{0,2},{1,3},{2,0},{3,1},{4,6},{5,7},{6,4},{7,5},{8,10},{9,11},{10,... | collective-permute-start | bytes 24584 | tf_op jit(solution)/shard_map/ppermute | solution.py:495
  53.9 1.6 %between.1 = (f32[4,512]{1,0:T(4,128)S(1)}, bf16[4,128,256]{2,1,0:T(8,128)(2,1)S(1)}, bf16[4,128,256]{2,1,0:T(8,128)(2,1)S(1)}) custom-call(s32[6]{0:T(128)S(1)} %stack.48.meta, f32[4,512]{1,0:T(4,128)S(1)} %get-tuple-element.86.whole, bf16[2,2,512,512]{3,2,1,0:T(8,128)(2,1)S(1)} %get-tuple-element.57.blocks, ...), custom_call_target="tpu_custom_call" | custom-call | tf_op jit(solution)/shard_map/between/pallas_call | solution.py:484
  55.5 0.7 collective-permute-done.9.near
  56.2 1.7 %second_image.1 = (bf16[4,128,256]{2,1,0:T(8,128)(2,1)S(1)}, bf16[4,128,256]{2,1,0:T(8,128)(2,1)S(1)}) custom-call(s32[6]{0:T(128)S(1)} %stack.48.meta, f32[6]{0:T(128)S(1)} %pad_maximum_fusion.3.scalars, bf16[1024,512]{1,0:T(8,128)(2,1)S(1)} %get-tuple-element.95.source, bf16[1024,512]{1,0:T(8,128)(2,1)S(1)} %get-tuple-element.96.receiver, ...), custom_call_target="tpu_custom_call" | custom-call | tf_op jit(solution)/shard_map/second_image/pallas_call | solution.py:484
  58.0 0.1 collective-permute-start.11
  58.0 0.5 collective-permute-start.10
  58.5 1.0 %collective-permute-done.11 = bf16[4,128,256]{2,1,0:T(8,128)(2,1)S(1)} collective-permute-done((bf16[4,128,256]{2,1,0:T(8,128)(2,1)S(1)}, bf16[4,128,256]{2,1,0:T(8,128)(2,1)S(1)}, u32[]{:S(2)}, u32[]{:S(2)}) %collective-permute-start.11) | collective-permute-done | bytes 262176 | tf_op jit(solution)/shard_map/ppermute | solution.py:495
  59.6 0.1 fusion.1
  59.6 0.3 collective-permute-done.10
  59.9 0.1 fusion
  60.1 1.5 %collective-permute-start.12 = (bf16[2,128,256]{2,1,0:T(8,128)(2,1)S(1)}, bf16[2,128,256]{2,1,0:T(8,128)(2,1)S(1)}, u32[]{:S(2)}, u32[]{:S(2)}) collective-permute-start(bf16[2,128,256]{2,1,0:T(8,128)(2,1)S(1)} %get-tuple-element.101), channel_id=1, source_target_pairs={{0,10},{1,11},{2,26},{3,27},{4,14},{5,15},{6,30},{7,31},{8,2},{9,3... | collective-permute-start | bytes 393224 | tf_op jit(solution)/shard_map/ppermute | solution.py:697
  61.5 1.4 %collective-permute-start.13 = (bf16[2,128,256]{2,1,0:T(8,128)(2,1)S(1)}, bf16[2,128,256]{2,1,0:T(8,128)(2,1)S(1)}, u32[]{:S(2)}, u32[]{:S(2)}) collective-permute-start(bf16[2,128,256]{2,1,0:T(8,128)(2,1)S(1)} %get-tuple-element.102), channel_id=1, source_target_pairs={{0,2},{1,3},{2,18},{3,19},{4,6},{5,7},{6,22},{7,23},{8,10},{9,11},... | collective-permute-start | bytes 393224 | tf_op jit(solution)/shard_map/ppermute | solution.py:697
  62.9 3.5 %collective-permute-start.15 = (bf16[2,128,256]{2,1,0:T(8,128)(2,1)S(1)}, bf16[2,128,256]{2,1,0:T(8,128)(2,1)S(1)}, u32[]{:S(2)}, u32[]{:S(2)}) collective-permute-start(bf16[2,128,256]{2,1,0:T(8,128)(2,1)S(1)} %get-tuple-element.103), channel_id=1, source_target_pairs={{0,0},{1,1},{2,16},{3,17},{4,4},{5,5},{6,20},{7,21},{8,8},{9,9},{1... | collective-permute-start | bytes 393224 | tf_op jit(solution)/shard_map/ppermute | solution.py:697
  66.4 1.3 %collective-permute-start.14 = (bf16[2,128,256]{2,1,0:T(8,128)(2,1)S(1)}, bf16[2,128,256]{2,1,0:T(8,128)(2,1)S(1)}, u32[]{:S(2)}, u32[]{:S(2)}) collective-permute-start(bf16[2,128,256]{2,1,0:T(8,128)(2,1)S(1)} %get-tuple-element.104), channel_id=1, source_target_pairs={{0,8},{1,9},{2,24},{3,25},{4,12},{5,13},{6,28},{7,29},{8,0},{9,1},... | collective-permute-start | bytes 393224 | tf_op jit(solution)/shard_map/ppermute | solution.py:697
  67.8 0.0 collective-permute-done.12
  67.8 1.7 %collective-permute-done.13 = bf16[2,128,256]{2,1,0:T(8,128)(2,1)S(1)} collective-permute-done((bf16[2,128,256]{2,1,0:T(8,128)(2,1)S(1)}, bf16[2,128,256]{2,1,0:T(8,128)(2,1)S(1)}, u32[]{:S(2)}, u32[]{:S(2)}) %collective-permute-start.13) | collective-permute-done | bytes 131104 | tf_op jit(solution)/shard_map/ppermute | solution.py:697
  69.4 3.2 %collective-permute-done.15 = bf16[2,128,256]{2,1,0:T(8,128)(2,1)S(1)} collective-permute-done((bf16[2,128,256]{2,1,0:T(8,128)(2,1)S(1)}, bf16[2,128,256]{2,1,0:T(8,128)(2,1)S(1)}, u32[]{:S(2)}, u32[]{:S(2)}) %collective-permute-start.15) | collective-permute-done | bytes 131104 | tf_op jit(solution)/shard_map/ppermute | solution.py:697
  72.6 1.4 %collective-permute-done.14 = bf16[2,128,256]{2,1,0:T(8,128)(2,1)S(1)} collective-permute-done((bf16[2,128,256]{2,1,0:T(8,128)(2,1)S(1)}, bf16[2,128,256]{2,1,0:T(8,128)(2,1)S(1)}, u32[]{:S(2)}, u32[]{:S(2)}) %collective-permute-start.14) | collective-permute-done | bytes 131104 | tf_op jit(solution)/shard_map/ppermute | solution.py:697
  74.0 0.8 %convert_add_fusion = f32[2,128,256]{2,1,0:T(8,128)} fusion(bf16[2,128,256]{2,1,0:T(8,128)(2,1)S(1)} %collective-permute-done.15, bf16[2,128,256]{2,1,0:T(8,128)(2,1)S(1)} %collective-permute-done.14, bf16[2,128,256]{2,1,0:T(8,128)(2,1)S(1)} %collective-permute-done.13, bf16[2,128,256]{2,1,0:T(8,128)(2,1)S(1)} %collective-permute-done.12), kind=kLoop, calls=%fused_computation.13 | loop fusion | flops 458752 | bytes 786432 | tf_op jit(solution)/shard_map/add | solution.py:697
  (9 shorter events, 0.2 us)
Async XLA Ops:
  1.6 1.2 %copy-start = (f32[2,128,1024]{2,1,0:T(8,128)S(1)}, f32[2,128,1024]{2,1,0:T(8,128)}, u32[]{:S(2)}) copy-start(f32[2,128,1024]{2,1,0:T(8,128)} %slowness.3) | copy-start | bytes 3145732
  2.8 1.2 %copy-start.2 = (bf16[1,2,128,2,1024]{4,3,2,1,0:T(2,128)(2,1)S(1)}, bf16[1,2,128,2,1024]{4,3,2,1,0:T(2,128)(2,1)}, u32[]{:S(2)}) copy-start(bf16[1,2,128,2,1024]{4,3,2,1,0:T(2,128)(2,1)} %field.2) | copy-start | bytes 3145732
  4.0 4.0 %copy-start.1 = (f32[2,128,1024]{2,1,0:T(8,128)S(1)}, f32[2,128,1024]{2,1,0:T(8,128)}, u32[]{:S(2)}) copy-start(f32[2,128,1024]{2,1,0:T(8,128)} %slowness.3) | copy-start | bytes 3145732
  5.7 2.3 %collective-permute-start = (bf16[256,1024]{1,0:T(8,128)(2,1)S(1)}, bf16[256,1024]{1,0:T(8,128)(2,1)S(1)}, u32[]{:S(2)}, u32[]{:S(2)}) collective-permute-start(bf16[256,1024]{1,0:T(8,128)(2,1)S(1)} %get-tuple-element.56), channel_id=1, source_target_pairs={{0,1},{1,0},{2,3},{3,2},{4,5},{5,4},{6,7},{7,6},{8,9},{9,8},{10,11... | collective-permute-start | bytes 1572872 | tf_op jit(solution)/shard_map/ppermute | solution.py:495
  8.0 3.1 %copy-start.3 = (bf16[1,2,128,2,1024]{4,3,2,1,0:T(2,128)(2,1)S(1)}, bf16[1,2,128,2,1024]{4,3,2,1,0:T(2,128)(2,1)}, u32[]{:S(2)}) copy-start(bf16[1,2,128,2,1024]{4,3,2,1,0:T(2,128)(2,1)} %field.3) | copy-start | bytes 3145732
  8.0 3.1 %copy-start.4 = (s32[1,1024]{1,0:T(1,128)S(1)}, s32[1,1024]{1,0:T(1,128)}, u32[]{:S(2)}) copy-start(s32[1,1024]{1,0:T(1,128)} %mask) | copy-start | bytes 12292
  14.0 2.6 %collective-permute-start.1 = (bf16[256,1024]{1,0:T(8,128)(2,1)S(1)}, bf16[256,1024]{1,0:T(8,128)(2,1)S(1)}, u32[]{:S(2)}, u32[]{:S(2)}) collective-permute-start(bf16[256,1024]{1,0:T(8,128)(2,1)S(1)} %get-tuple-element.63), channel_id=1, source_target_pairs={{0,1},{1,0},{2,3},{3,2},{4,5},{5,4},{6,7},{7,6},{8,9},{9,8},{10,11... | collective-permute-start | bytes 1572872 | tf_op jit(solution)/shard_map/ppermute | solution.py:495
  14.6 15.0 %collective-permute-start.2 = (bf16[512,512]{1,0:T(8,128)(2,1)S(1)}, bf16[512,512]{1,0:T(8,128)(2,1)S(1)}, u32[]{:S(2)}, u32[]{:S(2)}) collective-permute-start(bf16[512,512]{1,0:T(8,128)(2,1)S(1)} %get-tuple-element.65.cross0), channel_id=1, source_target_pairs={{0,2},{1,3},{2,0},{3,1},{4,6},{5,7},{6,4},{7,5},{8,10},{9,11},{10,... | collective-permute-start | bytes 1572872 | tf_op jit(solution)/shard_map/ppermute | solution.py:495
  16.1 16.2 %collective-permute-start.3 = (f16[128,512]{1,0:T(8,128)(2,1)S(1)}, f16[128,512]{1,0:T(8,128)(2,1)S(1)}, u32[]{:S(2)}, u32[]{:S(2)}) collective-permute-start(f16[128,512]{1,0:T(8,128)(2,1)S(1)} %get-tuple-element.67), channel_id=1, source_target_pairs={{0,2},{1,3},{2,0},{3,1},{4,6},{5,7},{6,4},{7,5},{8,10},{9,11},{10,... | collective-permute-start | bytes 393224 | tf_op jit(solution)/shard_map/ppermute | solution.py:495
  16.6 19.7 %copy-start.5 = (s32[1,2]{1,0:T(1,128)S(1)}, s32[1,2]{1,0:T(1,128)}, u32[]{:S(2)}) copy-start(s32[1,2]{1,0:T(1,128)} %place.1) | copy-start | bytes 28
  19.9 12.4 %collective-permute-start.4 = (f32[4,512]{1,0:T(4,128)S(1)}, f32[4,512]{1,0:T(4,128)S(1)}, u32[]{:S(2)}, u32[]{:S(2)}) collective-permute-start(f32[4,512]{1,0:T(4,128)S(1)} %get-tuple-element.69), channel_id=1, source_target_pairs={{0,4},{1,5},{2,6},{3,7},{4,0},{5,1},{6,2},{7,3},{8,12},{9,13},{10,... | collective-permute-start | bytes 24584 | tf_op jit(solution)/shard_map/ppermute | solution.py:495
  22.6 12.0 %collective-permute-start.5 = (f32[4,512]{1,0:T(4,128)S(1)}, f32[4,512]{1,0:T(4,128)S(1)}, u32[]{:S(2)}, u32[]{:S(2)}) collective-permute-start(f32[4,512]{1,0:T(4,128)S(1)} %get-tuple-element.70), channel_id=1, source_target_pairs={{0,6},{1,7},{2,4},{3,5},{4,2},{5,3},{6,0},{7,1},{8,14},{9,15},{10,... | collective-permute-start | bytes 24584 | tf_op jit(solution)/shard_map/ppermute | solution.py:495
  29.5 14.9 %collective-permute-start.7 = (bf16[512,512]{1,0:T(8,128)(2,1)S(1)}, bf16[512,512]{1,0:T(8,128)(2,1)S(1)}, u32[]{:S(2)}, u32[]{:S(2)}) collective-permute-start(bf16[512,512]{1,0:T(8,128)(2,1)S(1)} %get-tuple-element.80.cross1), channel_id=1, source_target_pairs={{0,2},{1,3},{2,0},{3,1},{4,6},{5,7},{6,4},{7,5},{8,10},{9,11},{10,... | collective-permute-start | bytes 1572872 | tf_op jit(solution)/shard_map/ppermute | solution.py:495
  34.6 1.6 %collective-permute-start.6 = (f16[2,128,512]{2,1,0:T(8,128)(2,1)S(1)}, f16[2,128,512]{2,1,0:T(8,128)(2,1)S(1)}, u32[]{:S(2)}, u32[]{:S(2)}) collective-permute-start(f16[2,128,512]{2,1,0:T(8,128)(2,1)S(1)} %pad_maximum_fusion), channel_id=1, source_target_pairs={{0,1},{1,0},{2,3},{3,2},{4,5},{5,4},{6,7},{7,6},{8,9},{9,8},{10,11... | collective-permute-start | bytes 786440 | tf_op jit(solution)/shard_map/ppermute | solution.py:495
  47.1 4.6 %collective-permute-start.8 = (f32[4,512]{1,0:T(4,128)S(1)}, f32[4,512]{1,0:T(4,128)S(1)}, u32[]{:S(2)}, u32[]{:S(2)}) collective-permute-start(f32[4,512]{1,0:T(4,128)S(1)} %pad_maximum_fusion.2.edge_x), channel_id=1, source_target_pairs={{0,4},{1,5},{2,6},{3,7},{4,0},{5,1},{6,2},{7,3},{8,12},{9,13},{10,... | collective-permute-start | bytes 24584 | tf_op jit(solution)/shard_map/ppermute | solution.py:495
  52.5 3.7 %collective-permute-start.9 = (f32[4,512]{1,0:T(4,128)S(1)}, f32[4,512]{1,0:T(4,128)S(1)}, u32[]{:S(2)}, u32[]{:S(2)}) collective-permute-start(f32[4,512]{1,0:T(4,128)S(1)} %get-tuple-element.91.edge), channel_id=1, source_target_pairs={{0,2},{1,3},{2,0},{3,1},{4,6},{5,7},{6,4},{7,5},{8,10},{9,11},{10,... | collective-permute-start | bytes 24584 | tf_op jit(solution)/shard_map/ppermute | solution.py:495
  58.0 1.6 %collective-permute-start.11 = (bf16[4,128,256]{2,1,0:T(8,128)(2,1)S(1)}, bf16[4,128,256]{2,1,0:T(8,128)(2,1)S(1)}, u32[]{:S(2)}, u32[]{:S(2)}) collective-permute-start(bf16[4,128,256]{2,1,0:T(8,128)(2,1)S(1)} %get-tuple-element.100), channel_id=1, source_target_pairs={{0,1},{1,0},{2,3},{3,2},{4,5},{5,4},{6,7},{7,6},{8,9},{9,8},{10,11... | collective-permute-start | bytes 786440 | tf_op jit(solution)/shard_map/ppermute | solution.py:495
  58.0 1.9 %collective-permute-start.10 = (bf16[4,128,256]{2,1,0:T(8,128)(2,1)S(1)}, bf16[4,128,256]{2,1,0:T(8,128)(2,1)S(1)}, u32[]{:S(2)}, u32[]{:S(2)}) collective-permute-start(bf16[4,128,256]{2,1,0:T(8,128)(2,1)S(1)} %get-tuple-element.94), channel_id=1, source_target_pairs={{0,1},{1,0},{2,3},{3,2},{4,5},{5,4},{6,7},{7,6},{8,9},{9,8},{10,11... | collective-permute-start | bytes 786440 | tf_op jit(solution)/shard_map/ppermute | solution.py:495
  60.1 7.7 %collective-permute-start.12 = (bf16[2,128,256]{2,1,0:T(8,128)(2,1)S(1)}, bf16[2,128,256]{2,1,0:T(8,128)(2,1)S(1)}, u32[]{:S(2)}, u32[]{:S(2)}) collective-permute-start(bf16[2,128,256]{2,1,0:T(8,128)(2,1)S(1)} %get-tuple-element.101), channel_id=1, source_target_pairs={{0,10},{1,11},{2,26},{3,27},{4,14},{5,15},{6,30},{7,31},{8,2},{9,3... | collective-permute-start | bytes 393224 | tf_op jit(solution)/shard_map/ppermute | solution.py:697
  61.5 7.9 %collective-permute-start.13 = (bf16[2,128,256]{2,1,0:T(8,128)(2,1)S(1)}, bf16[2,128,256]{2,1,0:T(8,128)(2,1)S(1)}, u32[]{:S(2)}, u32[]{:S(2)}) collective-permute-start(bf16[2,128,256]{2,1,0:T(8,128)(2,1)S(1)} %get-tuple-element.102), channel_id=1, source_target_pairs={{0,2},{1,3},{2,18},{3,19},{4,6},{5,7},{6,22},{7,23},{8,10},{9,11},... | collective-permute-start | bytes 393224 | tf_op jit(solution)/shard_map/ppermute | solution.py:697
  62.9 9.7 %collective-permute-start.15 = (bf16[2,128,256]{2,1,0:T(8,128)(2,1)S(1)}, bf16[2,128,256]{2,1,0:T(8,128)(2,1)S(1)}, u32[]{:S(2)}, u32[]{:S(2)}) collective-permute-start(bf16[2,128,256]{2,1,0:T(8,128)(2,1)S(1)} %get-tuple-element.103), channel_id=1, source_target_pairs={{0,0},{1,1},{2,16},{3,17},{4,4},{5,5},{6,20},{7,21},{8,8},{9,9},{1... | collective-permute-start | bytes 393224 | tf_op jit(solution)/shard_map/ppermute | solution.py:697
  66.4 7.5 %collective-permute-start.14 = (bf16[2,128,256]{2,1,0:T(8,128)(2,1)S(1)}, bf16[2,128,256]{2,1,0:T(8,128)(2,1)S(1)}, u32[]{:S(2)}, u32[]{:S(2)}) collective-permute-start(bf16[2,128,256]{2,1,0:T(8,128)(2,1)S(1)} %get-tuple-element.104), channel_id=1, source_target_pairs={{0,8},{1,9},{2,24},{3,25},{4,12},{5,13},{6,28},{7,29},{8,0},{9,1},... | collective-permute-start | bytes 393224 | tf_op jit(solution)/shard_map/ppermute | solution.py:697

commit v2 on v1

--- a/solution.py
+++ b/solution.py
@@ -144,6 +144,7 @@
 BF16 = jnp.bfloat16
 SMEM = pltpu.SMEM
 VMEM = pltpu.VMEM
+OWN_MIB = 48
 MIDDLE = 1.25
 
 
@@ -185,27 +186,32 @@
     out[rows:] = (imag * cosine + real * sine).astype(BF16)
 
 
-def receiver_kernel(meta, scalars, mask, field, slowness, own, other):
-    keep = mask[...].astype(F32)
-    for k, out in ((1, other), (0, own)):
-        f = meta[0] ^ k
-        real = field[0, f, :, 0, :].astype(F32) * keep
-        imag = -(field[0, f, :, 1, :].astype(F32) * keep)
-        rotate(scalars[f], slowness[0], real, imag, out)
-
-
-def other_kernel(meta, scalars, field, slowness, out, raw, slow):
+def other_kernel(meta, freq, field, slowness, out, raw, slow, freq_out):
     f = meta[0] ^ 1
-    rotate(scalars[f], slowness[0], field[0, f, :, 0, :].astype(F32), field[0, f, :, 1, :].astype(F32), out)
     raw[...] = field[0, meta[0]]
     slow[...] = slowness[0]
-
-
-def own_kernel(meta, scalars, raw, slow, inverse, out, blocks, sem):
+    for k in range(2):
+        freq_out[k] = freq[k]
+    rotate(freq[f], slowness[0], field[0, f, :, 0, :].astype(F32), field[0, f, :, 1, :].astype(F32), out)
+
+
+def own_kernel(meta, freq, raw, slow, inverse, out, blocks, sem):
     fetch = pltpu.make_async_copy(inverse.at[meta[0]], blocks, sem)
     fetch.start()
-    rotate(scalars[meta[0]], slow[...], raw[:, 0, :].astype(F32), raw[:, 1, :].astype(F32), out)
+    rotate(freq[meta[0]], slow[...], raw[:, 0, :].astype(F32), raw[:, 1, :].astype(F32), out)
     fetch.wait()
+
+
+def source_kernel(meta, freq, coupling, own, core, blocks, same, cross, ends, scalars):
+    for k in range(2):
+        scalars[k] = freq[k]
+        scalars[2 + 2 * k] = coupling[k, 0]
+        scalars[3 + 2 * k] = coupling[k, 1]
+    slab_kernel(meta, scalars, own, core, blocks, same, cross, ends)
+
+
+def away_kernel(meta, residual, out):
+    out[...] = residual[0, 1 - meta[0]]
 
 
 def edge_rows(meta, blocks, block, lanes):
@@ -281,6 +287,19 @@
         for k in range(2):
             out[2 * k : 2 * k + 1] = er[:, k * half : (k + 1) * half]
             out[2 * k + 1 : 2 * k + 2] = ei[:, k * half : (k + 1) * half]
+
+
+def receiver_kernel(
+    meta, scalars, mask, field, core_raw, slow, core_slow, blocks, same0, cross0, same, cross, edge_same, edge_cross, own, core, ends
+):
+    keep = mask[...].astype(F32)
+    f = meta[0]
+    for raw, slowness, out in ((field.at[0, f], slow, own), (core_raw, core_slow, core)):
+        rotate(
+            scalars[f], slowness[...], raw[:, 0, :].astype(F32) * keep, -(raw[:, 1, :].astype(F32) * keep), out
+        )
+    slab_kernel(meta, scalars, own, core, blocks, same, cross, ends)
+    edge_kernel(meta, blocks, same0, cross0, same, cross, edge_same, edge_cross)
 
 
 def phase_kernel(meta, scalars, place, own, core, far, far_core, sine, cosine, weight):
@@ -472,7 +491,6 @@
     meta = jnp.stack(
         [slab & 1, (slab >> 1) & 1, slab >> 2, slab & 3, shot >> 1, shot & 1]
     ).astype(jnp.int32)
-    scalars = jnp.concatenate([frequency, coupling.reshape(-1)])
     smem = pl.BlockSpec(memory_space=SMEM)
     vmem = pl.BlockSpec(memory_space=VMEM)
     hbm = pl.BlockSpec(memory_space=pltpu.HBM)
@@ -494,89 +512,67 @@
     def move(array, k):
         return lax.ppermute(array, "slab", [(i, i ^ k) for i in range(8)])
 
-    same, far, edges = [], [], []
-    for n, field in enumerate((source_field, residual_data)):
-        cut = shape(BF16, 2 * rows, length)
-        if n == 0:
-            core, raw, slow = call(
-                other_kernel,
-                "other",
-                [smem, smem, vmem, vmem],
-                [cut, shape(BF16, rows, 2, length), shape(F32, rows, length)],
-                [],
-                12,
-                meta,
-                scalars,
-                field,
-                slowness,
-            )
-            own, blocks = call(
-                own_kernel,
-                "own",
-                [smem, smem, vmem, vmem, hbm],
-                [cut, shape(BF16, *line_inverse.shape[1:])],
-                [pltpu.SemaphoreType.DMA],
-                48,
-                meta,
-                scalars,
-                raw,
-                slow,
-                line_inverse,
-            )
-        else:
-            mask, near_slow = lax.optimization_barrier((receiver_lines, near_slow))
-            own, core = call(
-                receiver_kernel,
-                "receiver",
-                [smem, smem, vmem, vmem, vmem],
-                [cut] * 2,
-                [],
-                12,
-                meta,
-                scalars,
-                mask,
-                field,
-                slowness,
-            )
-            far_slow = move(near_slow, 2)
-        core = move(core, 1)
-        mine, cross, ends = call(
-            slab_kernel,
-            "slab",
-            [smem, smem, vmem, vmem, vmem],
-            [shape(BF16, 4 * rows, half)] * 2 + [shape(F32, 4, half)],
-            [],
-            16,
-            meta,
-            scalars,
-            own,
-            core,
-            blocks,
-        )
-        same.append(mine)
-        edges.append(cross)
-        if n == 0:
-            far.append(move(cross, 2))
-            layer, same[0] = lax.optimization_barrier((slowness[1], same[0]))
-            layer = (layer - MIDDLE).astype(jnp.float16)
-            low, high = layer[:, :half], layer[:, half:]
-            first = meta[1] == 0
-            own_slow = jnp.where(first, low, high)
-            near_slow = jnp.where(first, high, low)
-    edges = call(
-        edge_kernel,
-        "edge",
-        [smem] + [vmem] * 5,
-        [shape(F32, 4, half)] * 2,
-        [],
-        8,
+    cut = shape(BF16, 2 * rows, length)
+    block_shape = shape(BF16, *line_inverse.shape[1:])
+    core, raw, slow, freq = pl.pallas_call(
+        other_kernel,
+        in_specs=[smem, smem, vmem, vmem],
+        out_specs=[vmem] * 3 + [smem],
+        out_shape=[cut, shape(BF16, rows, 2, length), shape(F32, rows, length), shape(F32, 2)],
+        compiler_params=params(12),
+        name="other",
+    )(meta, frequency, source_field, slowness)
+    own, blocks = pl.pallas_call(
+        own_kernel,
+        in_specs=[smem, smem, vmem, vmem, hbm],
+        out_specs=[vmem, vmem],
+        out_shape=[cut, block_shape],
+        scratch_shapes=[pltpu.SemaphoreType.DMA],
+        compiler_params=params(OWN_MIB),
+        name="own",
+    )(meta, freq, raw, slow, line_inverse)
+    core = move(core, 1)
+    block_piece = shape(BF16, 4 * rows, half)
+    same0, cross0, ends, scalars = pl.pallas_call(
+        source_kernel,
+        in_specs=[smem] * 3 + [vmem] * 3,
+        out_specs=[vmem] * 3 + [smem],
+        out_shape=[block_piece] * 2 + [shape(F32, 4, half), shape(F32, 6)],
+        compiler_params=params(16),
+        name="slab",
+    )(meta, freq, coupling, own, core, blocks)
+    far = [move(cross0, 2)]
+    residual, same0, slow0 = lax.optimization_barrier((residual_data, same0, slow))
+    (away,) = call(
+        away_kernel, "away", [smem, vmem], [shape(BF16, rows, 2, length)], [], 12, meta, residual
+    )
+    core_raw = move(away, 1)
+    core_slow0 = move(slow0, 1)
+    layer, same0 = lax.optimization_barrier((slowness[1], same0))
+    layer = (layer - MIDDLE).astype(jnp.float16)
+    low, high = layer[:, :half], layer[:, half:]
+    first = meta[1] == 0
+    own_slow = jnp.where(first, low, high)
+    far_slow = move(jnp.where(first, high, low), 2)
+    same1, cross, *edges = call(
+        receiver_kernel,
+        "receiver",
+        [smem, smem] + [vmem] * 8,
+        [block_piece] * 2 + [shape(F32, 4, half)] * 2,
+        [VMEM((2 * rows, length), BF16)] * 2 + [VMEM((4, half), F32)],
+        20,
         meta,
+        scalars,
+        receiver_lines,
+        residual_data,
+        core_raw,
+        slow,
+        core_slow0,
         blocks,
-        same[0],
-        edges[0],
-        same[1],
-        edges[1],
-    )
+        same0,
+        cross0,
+    )
+    same = [same0, same1]
     edge_same = move(edges[0], 4)
     edge_cross = move(edges[1], 6)
     cross, far[0] = lax.optimization_barrier((cross, far[0]))

time: 75 us -> 71.9 us (0.959)
  waiting for transfers between devices: 19.2 us -> 16.9 us
  Pallas kernels: 31.1 us -> 30.2 us
  starting transfers between devices: 18.9 us -> 19.8 us
    pallas_call x14 -> x10, Pallas kernels: 31.1 us -> 23.6 us  [call(): pl.pallas_call(body, in_specs=specs, out_specs=[vmem] * len(outs), out_sh...]
    pallas_call x0 -> x3, Pallas kernels: none -> 6.67 us  [the longest x1 2.37 us: block_shards(): pl.pallas_call(source_kernel, in_specs=[smem] * 3 + [vmem] * 3, out_specs...]
    ppermute x12 -> x13, waiting for transfers between devices: 13 us -> 10.8 us  [move(): return lax.ppermute(array, 'slab', [(i, i ^ k) for i in range(8)])]
    reshape x1 -> x0, local copies, waits for them, and re-layouts: 0.76 us -> none  [block_shards(): scalars = jnp.concatenate([frequency, coupling.reshape(-1)])]
    ppermute x12 -> x13, starting transfers between devices: 11.2 us -> 11.9 us  [move(): return lax.ppermute(array, 'slab', [(i, i ^ k) for i in range(8)])]
    unnamed x12 -> x16, local copies, waits for them, and re-layouts: 2.47 us -> 3.13 us
  transfers between devices with their start and end apart: 16 -> 17, of which waited for: 11 -> 10; matrix products, arithmetic and copies ran while one was open for 0% -> 1% of each run, Pallas kernels for 25% -> 28%
where the time goes in v2:
time: 71.9 us; the launch traced here: 71.7 us
  Pallas kernels  30.2 us (42%)
  starting transfers between devices  19.8 us (28%)
  waiting for transfers between devices  16.9 us (24%)
  local copies, waits for them, and re-layouts  3.26 us (5%)
  other arithmetic  1.21 us (2%)
    pallas_call x10, Pallas kernels, call(): pl.pallas_call(body, in_specs=specs, out_specs=[vmem] * len(outs), out_sh...  23.6 us
    ppermute x13, starting transfers between devices, move(): return lax.ppermute(array, 'slab', [(i, i ^ k) for i in range(8)])  11.9 us
    ppermute x13, waiting for transfers between devices, move(): return lax.ppermute(array, 'slab', [(i, i ^ k) for i in range(8)])  10.8 us
    ppermute x4, starting transfers between devices, block_shards(): lax.ppermute(both[kz * 2 + kx], ('shot', 'slab'), route).astype(F32)  7.92 us
    ppermute x4, waiting for transfers between devices, block_shards(): lax.ppermute(both[kz * 2 + kx], ('shot', 'slab'), route).astype(F32)  6.07 us
    unnamed x16, local copies, waits for them, and re-layouts  3.13 us
    pallas_call x1, Pallas kernels, block_shards(): pl.pallas_call(source_kernel, in_specs=[smem] * 3 + [vmem] * 3, out_specs...  2.37 us
    pallas_call x1, Pallas kernels, block_shards(): pl.pallas_call(other_kernel, in_specs=[smem, smem, vmem, vmem], out_specs...  2.15 us
  transfers between devices with their start and end apart: 17, of which 10 were waited for; matrix products, arithmetic and copies ran while one was open for 1% of the time, Pallas kernels for 28%

profile of v2, /device:TPU:4, one launch (start us, length us, event | category | flops | bytes accessed | tf_op | source)
XLA Modules:
  0.0 71.7 jit_solution(16855704873578295384)
XLA Ops:
  0.0 0.1 stack.48.meta
  0.1 1.2 %copy-done.1 = f32[2,128,1024]{2,1,0:T(8,128)S(1)} copy-done((f32[2,128,1024]{2,1,0:T(8,128)S(1)}, f32[2,128,1024]{2,1,0:T(8,128)}, u32[]{:S(2)}) %copy-start.1) | copy-done | bytes 1048600
  1.3 1.2 %copy-done.3 = bf16[1,2,128,2,1024]{4,3,2,1,0:T(2,128)(2,1)S(1)} copy-done((bf16[1,2,128,2,1024]{4,3,2,1,0:T(2,128)(2,1)S(1)}, bf16[1,2,128,2,1024]{4,3,2,1,0:T(2,128)(2,1)}, u32[]{:S(2)}) %copy-start.3) | copy-done | bytes 1048600
  2.5 0.7 copy-done.7
  3.2 2.2 %other.1 = (bf16[256,1024]{1,0:T(8,128)(2,1)S(1)}, bf16[128,2,1024]{2,1,0:T(2,128)(2,1)S(1)}, f32[128,1024]{1,0:T(8,128)S(1)}, f32[2]{0:T(128)S(1)}) custom-call(s32[6]{0:T(128)S(1)} %stack.48.meta, f32[2]{0:T(128)S(1)} %copy-done.7, bf16[1,2,128,2,1024]{4,3,2,1,0:T(2,128)(2,1)S(1)} %copy-done.3, f32[2,128,1024]{2,1,0:T(8,128)S(1)} %copy-done.1), custom_call_target="tpu_custom_call" | custom-call | tf_op jit(solution)/shard_map/other/pallas_call | solution.py:517
  5.4 0.1 collective-permute-start
  5.4 0.0 copy-start
  5.5 2.1 %own.1 = (bf16[256,1024]{1,0:T(8,128)(2,1)S(1)}, bf16[2,2,512,512]{3,2,1,0:T(8,128)(2,1)S(1)}) custom-call(s32[6]{0:T(128)S(1)} %stack.48.meta, f32[2]{0:T(128)S(1)} %get-tuple-element.54.freq, bf16[128,2,1024]{2,1,0:T(2,128)(2,1)S(1)} %get-tuple-element.55.raw, f32[128,1024]{1,0:T(8,128)S(1)} %get-tuple-element.65.slow, bf16[2,2,2,512,512]{4,3,2,1,0:T(8,128)(2,1)} %inverse.1), custom_call_target="tpu_custom_call" | custom-call | tf_op jit(solution)/shard_map/own/pallas_call | solution.py:525
  7.6 0.0 copy-done.2
  7.6 0.0 copy-start.4
  7.7 0.0 collective-permute-done.core
  7.7 0.0 copy-done.5
  7.7 2.4 %slab.1 = (bf16[512,512]{1,0:T(8,128)(2,1)S(1)}, bf16[512,512]{1,0:T(8,128)(2,1)S(1)}, f32[4,512]{1,0:T(4,128)S(1)}, f32[6]{0:T(128)S(1)}) custom-call(s32[6]{0:T(128)S(1)} %stack.48.meta, f32[2]{0:T(128)S(1)} %get-tuple-element.54.freq, f32[2,2]{1,0:T(2,128)S(1)} %copy-done.5, bf16[256,1024]{1,0:T(8,128)(2,1)S(1)} %get-tuple-element.57.own, ...), custom_call_target="tpu_custom_call" | custom-call | tf_op jit(solution)/shard_map/slab/pallas_call | solution.py:536
  10.1 0.0 copy-done
  10.1 0.6 away.1
  10.7 0.5 collective-permute-start.1
  11.2 0.1 collective-permute-start.2
  11.3 1.6 %collective-permute-start.3 = (bf16[512,512]{1,0:T(8,128)(2,1)S(1)}, bf16[512,512]{1,0:T(8,128)(2,1)S(1)}, u32[]{:S(2)}, u32[]{:S(2)}) collective-permute-start(bf16[512,512]{1,0:T(8,128)(2,1)S(1)} %get-tuple-element.66.cross0), channel_id=1, source_target_pairs={{0,2},{1,3},{2,0},{3,1},{4,6},{5,7},{6,4},{7,5},{8,10},{9,11},{10,... | collective-permute-start | bytes 1572872 | tf_op jit(solution)/shard_map/ppermute | solution.py:513
  12.9 0.0 copy-start.6
  12.9 0.1 fusion.11
  13.0 0.5 collective-permute-start.4
  13.5 0.0 collective-permute-done.1.core_raw
  13.5 0.0 collective-permute-done.2.core_slow
  13.5 0.0 copy-done.4
  13.5 4.7 %receiver.1 = (bf16[512,512]{1,0:T(8,128)(2,1)S(1)}, bf16[512,512]{1,0:T(8,128)(2,1)S(1)}, f32[4,512]{1,0:T(4,128)S(1)}, f32[4,512]{1,0:T(4,128)S(1)}) custom-call(s32[6]{0:T(128)S(1)} %stack.48.meta, f32[6]{0:T(128)S(1)} %get-tuple-element.60.scalars, s32[1,1024]{1,0:T(1,128)S(1)} %copy-done.4, bf16[1,2,128,2,1024]{4,3,2,1,0:T(2,128)(2,1)S(1)} %copy-done, ...), custom_call_target="tpu_custom_call" | custom-call | tf_op jit(solution)/shard_map/receiver/pallas_call | solution.py:502
  18.3 2.7 %collective-permute-start.5 = (f32[4,512]{1,0:T(4,128)S(1)}, f32[4,512]{1,0:T(4,128)S(1)}, u32[]{:S(2)}, u32[]{:S(2)}) collective-permute-start(f32[4,512]{1,0:T(4,128)S(1)} %get-tuple-element.70), channel_id=1, source_target_pairs={{0,4},{1,5},{2,6},{3,7},{4,0},{5,1},{6,2},{7,3},{8,12},{9,13},{10,... | collective-permute-start | bytes 24584 | tf_op jit(solution)/shard_map/ppermute | solution.py:513
  20.9 1.4 %collective-permute-start.6 = (f32[4,512]{1,0:T(4,128)S(1)}, f32[4,512]{1,0:T(4,128)S(1)}, u32[]{:S(2)}, u32[]{:S(2)}) collective-permute-start(f32[4,512]{1,0:T(4,128)S(1)} %get-tuple-element.71), channel_id=1, source_target_pairs={{0,6},{1,7},{2,4},{3,5},{4,2},{5,3},{6,0},{7,1},{8,14},{9,15},{10,... | collective-permute-start | bytes 24584 | tf_op jit(solution)/shard_map/ppermute | solution.py:513
  22.3 3.9 %collective-permute-done.3.far = bf16[512,512]{1,0:T(8,128)(2,1)S(1)} collective-permute-done((bf16[512,512]{1,0:T(8,128)(2,1)S(1)}, bf16[512,512]{1,0:T(8,128)(2,1)S(1)}, u32[]{:S(2)}, u32[]{:S(2)}) %collective-permute-start.3) | collective-permute-done | bytes 524320 | tf_op jit(solution)/shard_map/ppermute | solution.py:513
  26.2 1.4 %collective-permute-start.8 = (bf16[512,512]{1,0:T(8,128)(2,1)S(1)}, bf16[512,512]{1,0:T(8,128)(2,1)S(1)}, u32[]{:S(2)}, u32[]{:S(2)}) collective-permute-start(bf16[512,512]{1,0:T(8,128)(2,1)S(1)} %get-tuple-element.82), channel_id=1, source_target_pairs={{0,2},{1,3},{2,0},{3,1},{4,6},{5,7},{6,4},{7,5},{8,10},{9,11},{10,... | collective-permute-start | bytes 1572872 | tf_op jit(solution)/shard_map/ppermute | solution.py:513
  27.6 1.4 %collective-permute-done.4 = f16[128,512]{1,0:T(8,128)(2,1)S(1)} collective-permute-done((f16[128,512]{1,0:T(8,128)(2,1)S(1)}, f16[128,512]{1,0:T(8,128)(2,1)S(1)}, u32[]{:S(2)}, u32[]{:S(2)}) %collective-permute-start.4) | collective-permute-done | bytes 131104 | tf_op jit(solution)/shard_map/ppermute | solution.py:513
  29.0 0.0 collective-permute-done.5
  29.0 2.2 %collective-permute-done.6 = f32[4,512]{1,0:T(4,128)S(1)} collective-permute-done((f32[4,512]{1,0:T(4,128)S(1)}, f32[4,512]{1,0:T(4,128)S(1)}, u32[]{:S(2)}, u32[]{:S(2)}) %collective-permute-start.6) | collective-permute-done | bytes 8224 | tf_op jit(solution)/shard_map/ppermute | solution.py:513
  31.2 0.1 pad_maximum_fusion
  31.3 0.1 collective-permute-start.7
  31.4 1.5 %collective-permute-done.7 = f16[2,128,512]{2,1,0:T(8,128)(2,1)S(1)} collective-permute-done((f16[2,128,512]{2,1,0:T(8,128)(2,1)S(1)}, f16[2,128,512]{2,1,0:T(8,128)(2,1)S(1)}, u32[]{:S(2)}, u32[]{:S(2)}) %collective-permute-start.7) | collective-permute-done | bytes 262176 | tf_op jit(solution)/shard_map/ppermute | solution.py:513
  32.9 0.1 fusion.9
  32.9 2.1 %phase.1 = (f32[512,512]{1,0:T(8,128)S(1)}, f32[512,512]{1,0:T(8,128)S(1)}, f32[512,512]{1,0:T(8,128)S(1)}) custom-call(s32[6]{0:T(128)S(1)} %stack.48.meta, f32[6]{0:T(128)S(1)} %get-tuple-element.60.scalars, s32[1,2]{1,0:T(1,128)S(1)} %copy-done.6, f32[128,512]{1,0:T(8,128)S(1)} %get-tuple-element.111.own, f32[128,512]{1,0:T(8,128)S(1)} %get-tuple-element.108.core, ...), custom_call_target="tpu_custom_call" | custom-call | tf_op jit(solution)/shard_map/phase/pallas_call | solution.py:502
  35.0 2.7 %column.2 = (bf16[1024,512]{1,0:T(8,128)(2,1)S(1)}, bf16[1024,512]{1,0:T(8,128)(2,1)S(1)}, f32[2,512]{1,0:T(2,128)S(1)}) custom-call(s32[6]{0:T(128)S(1)} %stack.48.meta, f32[6]{0:T(128)S(1)} %get-tuple-element.60.scalars, bf16[512,512]{1,0:T(8,128)(2,1)S(1)} %get-tuple-element.63.same0.near, bf16[512,512]{1,0:T(8,128)(2,1)S(1)} %collective-permute-done.3.far, ...), custom_call_target="tpu_custom_call" | custom-call | tf_op jit(solution)/shard_map/column/pallas_call | solution.py:502
  37.7 3.5 %both.2 = (bf16[1024,512]{1,0:T(8,128)(2,1)S(1)}, f32[2,512]{1,0:T(2,128)S(1)}) custom-call(s32[6]{0:T(128)S(1)} %stack.48.meta, bf16[1024,512]{1,0:T(8,128)(2,1)S(1)} %get-tuple-element.79.shifted, bf16[2,2,512,512]{3,2,1,0:T(8,128)(2,1)S(1)} %get-tuple-element.59.blocks), custom_call_target="tpu_custom_call" | custom-call | tf_op jit(solution)/shard_map/both/pallas_call | solution.py:502
  41.2 0.0 collective-permute-done.8.far
  41.2 2.7 %column.3 = (bf16[1024,512]{1,0:T(8,128)(2,1)S(1)}, bf16[1024,512]{1,0:T(8,128)(2,1)S(1)}, f32[2,512]{1,0:T(2,128)S(1)}) custom-call(s32[6]{0:T(128)S(1)} %stack.48.meta, f32[6]{0:T(128)S(1)} %get-tuple-element.60.scalars, bf16[512,512]{1,0:T(8,128)(2,1)S(1)} %get-tuple-element.81.near, bf16[512,512]{1,0:T(8,128)(2,1)S(1)} %collective-permute-done.8.far, ...), custom_call_target="tpu_custom_call" | custom-call | tf_op jit(solution)/shard_map/column/pallas_call | solution.py:502
  43.9 1.4 %collective-permute-start.9 = (f32[4,512]{1,0:T(4,128)S(1)}, f32[4,512]{1,0:T(4,128)S(1)}, u32[]{:S(2)}, u32[]{:S(2)}) collective-permute-start(f32[4,512]{1,0:T(4,128)S(1)} %pad_maximum_fusion.2.edge_x), channel_id=1, source_target_pairs={{0,4},{1,5},{2,6},{3,7},{4,0},{5,1},{6,2},{7,3},{8,12},{9,13},{10,... | collective-permute-start | bytes 24584 | tf_op jit(solution)/shard_map/ppermute | solution.py:513
  45.3 3.3 %both.3 = (bf16[1024,512]{1,0:T(8,128)(2,1)S(1)}, f32[2,512]{1,0:T(2,128)S(1)}) custom-call(s32[6]{0:T(128)S(1)} %stack.48.meta, bf16[1024,512]{1,0:T(8,128)(2,1)S(1)} %get-tuple-element.85.shifted, bf16[2,2,512,512]{3,2,1,0:T(8,128)(2,1)S(1)} %get-tuple-element.59.blocks), custom_call_target="tpu_custom_call" | custom-call | tf_op jit(solution)/shard_map/both/pallas_call | solution.py:502
  48.6 0.0 collective-permute-done.9.near_x
  48.6 0.7 %turn.1 = (f32[4,512]{1,0:T(4,128)S(1)}, f32[4,512]{1,0:T(4,128)S(1)}) custom-call(s32[6]{0:T(128)S(1)} %stack.48.meta, f32[6]{0:T(128)S(1)} %get-tuple-element.60.scalars, f32[4,512]{1,0:T(4,128)S(1)} %pad_maximum_fusion.2.edge_x, f32[4,512]{1,0:T(4,128)S(1)} %collective-permute-done.9.near_x, f32[2,512]{1,0:T(2,128)S(1)} %get-tuple-element.84.edge_y0, ...), custom_call_target="tpu_custom_call" | custom-call | tf_op jit(solution)/shard_map/turn/pallas_call | solution.py:502
  49.4 1.6 %collective-permute-start.10 = (f32[4,512]{1,0:T(4,128)S(1)}, f32[4,512]{1,0:T(4,128)S(1)}, u32[]{:S(2)}, u32[]{:S(2)}) collective-permute-start(f32[4,512]{1,0:T(4,128)S(1)} %get-tuple-element.93.edge), channel_id=1, source_target_pairs={{0,2},{1,3},{2,0},{3,1},{4,6},{5,7},{6,4},{7,5},{8,10},{9,11},{10,... | collective-permute-start | bytes 24584 | tf_op jit(solution)/shard_map/ppermute | solution.py:513
  51.0 1.6 %between.1 = (f32[4,512]{1,0:T(4,128)S(1)}, bf16[4,128,256]{2,1,0:T(8,128)(2,1)S(1)}, bf16[4,128,256]{2,1,0:T(8,128)(2,1)S(1)}) custom-call(s32[6]{0:T(128)S(1)} %stack.48.meta, f32[4,512]{1,0:T(4,128)S(1)} %get-tuple-element.88.whole, bf16[2,2,512,512]{3,2,1,0:T(8,128)(2,1)S(1)} %get-tuple-element.59.blocks, ...), custom_call_target="tpu_custom_call" | custom-call | tf_op jit(solution)/shard_map/between/pallas_call | solution.py:502
  52.6 0.5 collective-permute-done.10.near
  53.1 1.7 %second_image.1 = (bf16[4,128,256]{2,1,0:T(8,128)(2,1)S(1)}, bf16[4,128,256]{2,1,0:T(8,128)(2,1)S(1)}) custom-call(s32[6]{0:T(128)S(1)} %stack.48.meta, f32[6]{0:T(128)S(1)} %get-tuple-element.60.scalars, bf16[1024,512]{1,0:T(8,128)(2,1)S(1)} %get-tuple-element.97.source, bf16[1024,512]{1,0:T(8,128)(2,1)S(1)} %get-tuple-element.98.receiver, ...), custom_call_target="tpu_custom_call" | custom-call | tf_op jit(solution)/shard_map/second_image/pallas_call | solution.py:502
  54.8 0.1 collective-permute-start.12
  54.9 0.5 collective-permute-start.11
  55.4 1.0 %collective-permute-done.12 = bf16[4,128,256]{2,1,0:T(8,128)(2,1)S(1)} collective-permute-done((bf16[4,128,256]{2,1,0:T(8,128)(2,1)S(1)}, bf16[4,128,256]{2,1,0:T(8,128)(2,1)S(1)}, u32[]{:S(2)}, u32[]{:S(2)}) %collective-permute-start.12) | collective-permute-done | bytes 262176 | tf_op jit(solution)/shard_map/ppermute | solution.py:513
  56.4 0.1 fusion.1
  56.5 0.3 collective-permute-done.11
  56.8 0.1 fusion
  56.9 1.5 %collective-permute-start.13 = (bf16[2,128,256]{2,1,0:T(8,128)(2,1)S(1)}, bf16[2,128,256]{2,1,0:T(8,128)(2,1)S(1)}, u32[]{:S(2)}, u32[]{:S(2)}) collective-permute-start(bf16[2,128,256]{2,1,0:T(8,128)(2,1)S(1)} %get-tuple-element.103), channel_id=1, source_target_pairs={{0,10},{1,11},{2,26},{3,27},{4,14},{5,15},{6,30},{7,31},{8,2},{9,3... | collective-permute-start | bytes 393224 | tf_op jit(solution)/shard_map/ppermute | solution.py:693
  58.4 1.6 %collective-permute-start.14 = (bf16[2,128,256]{2,1,0:T(8,128)(2,1)S(1)}, bf16[2,128,256]{2,1,0:T(8,128)(2,1)S(1)}, u32[]{:S(2)}, u32[]{:S(2)}) collective-permute-start(bf16[2,128,256]{2,1,0:T(8,128)(2,1)S(1)} %get-tuple-element.104), channel_id=1, source_target_pairs={{0,2},{1,3},{2,18},{3,19},{4,6},{5,7},{6,22},{7,23},{8,10},{9,11},... | collective-permute-start | bytes 393224 | tf_op jit(solution)/shard_map/ppermute | solution.py:693
  60.0 3.3 %collective-permute-start.16 = (bf16[2,128,256]{2,1,0:T(8,128)(2,1)S(1)}, bf16[2,128,256]{2,1,0:T(8,128)(2,1)S(1)}, u32[]{:S(2)}, u32[]{:S(2)}) collective-permute-start(bf16[2,128,256]{2,1,0:T(8,128)(2,1)S(1)} %get-tuple-element.105), channel_id=1, source_target_pairs={{0,0},{1,1},{2,16},{3,17},{4,4},{5,5},{6,20},{7,21},{8,8},{9,9},{1... | collective-permute-start | bytes 393224 | tf_op jit(solution)/shard_map/ppermute | solution.py:693
  63.3 1.6 %collective-permute-start.15 = (bf16[2,128,256]{2,1,0:T(8,128)(2,1)S(1)}, bf16[2,128,256]{2,1,0:T(8,128)(2,1)S(1)}, u32[]{:S(2)}, u32[]{:S(2)}) collective-permute-start(bf16[2,128,256]{2,1,0:T(8,128)(2,1)S(1)} %get-tuple-element.106), channel_id=1, source_target_pairs={{0,8},{1,9},{2,24},{3,25},{4,12},{5,13},{6,28},{7,29},{8,0},{9,1},... | collective-permute-start | bytes 393224 | tf_op jit(solution)/shard_map/ppermute | solution.py:693
  64.8 0.0 collective-permute-done.13
  64.9 1.4 %collective-permute-done.14 = bf16[2,128,256]{2,1,0:T(8,128)(2,1)S(1)} collective-permute-done((bf16[2,128,256]{2,1,0:T(8,128)(2,1)S(1)}, bf16[2,128,256]{2,1,0:T(8,128)(2,1)S(1)}, u32[]{:S(2)}, u32[]{:S(2)}) %collective-permute-start.14) | collective-permute-done | bytes 131104 | tf_op jit(solution)/shard_map/ppermute | solution.py:693
  66.3 3.3 %collective-permute-done.16 = bf16[2,128,256]{2,1,0:T(8,128)(2,1)S(1)} collective-permute-done((bf16[2,128,256]{2,1,0:T(8,128)(2,1)S(1)}, bf16[2,128,256]{2,1,0:T(8,128)(2,1)S(1)}, u32[]{:S(2)}, u32[]{:S(2)}) %collective-permute-start.16) | collective-permute-done | bytes 131104 | tf_op jit(solution)/shard_map/ppermute | solution.py:693
  69.5 1.4 %collective-permute-done.15 = bf16[2,128,256]{2,1,0:T(8,128)(2,1)S(1)} collective-permute-done((bf16[2,128,256]{2,1,0:T(8,128)(2,1)S(1)}, bf16[2,128,256]{2,1,0:T(8,128)(2,1)S(1)}, u32[]{:S(2)}, u32[]{:S(2)}) %collective-permute-start.15) | collective-permute-done | bytes 131104 | tf_op jit(solution)/shard_map/ppermute | solution.py:693
  70.9 0.8 %convert_add_fusion = f32[2,128,256]{2,1,0:T(8,128)} fusion(bf16[2,128,256]{2,1,0:T(8,128)(2,1)S(1)} %collective-permute-done.16, bf16[2,128,256]{2,1,0:T(8,128)(2,1)S(1)} %collective-permute-done.15, bf16[2,128,256]{2,1,0:T(8,128)(2,1)S(1)} %collective-permute-done.14, bf16[2,128,256]{2,1,0:T(8,128)(2,1)S(1)} %collective-permute-done.13), kind=kLoop, calls=%fused_computation.13 | loop fusion | flops 458752 | bytes 786432 | tf_op jit(solution)/shard_map/add | solution.py:693
  (12 shorter events, 0.2 us)
Async XLA Ops:
  0.1 1.2 %copy-start.1 = (f32[2,128,1024]{2,1,0:T(8,128)S(1)}, f32[2,128,1024]{2,1,0:T(8,128)}, u32[]{:S(2)}) copy-start(f32[2,128,1024]{2,1,0:T(8,128)} %slowness.1) | copy-start | bytes 3145732
  1.3 1.2 %copy-start.3 = (bf16[1,2,128,2,1024]{4,3,2,1,0:T(2,128)(2,1)S(1)}, bf16[1,2,128,2,1024]{4,3,2,1,0:T(2,128)(2,1)}, u32[]{:S(2)}) copy-start(bf16[1,2,128,2,1024]{4,3,2,1,0:T(2,128)(2,1)} %field.2) | copy-start | bytes 3145732
  2.5 0.7 copy-start.7
  3.2 4.4 %copy-start.2 = (f32[2,128,1024]{2,1,0:T(8,128)S(1)}, f32[2,128,1024]{2,1,0:T(8,128)}, u32[]{:S(2)}) copy-start(f32[2,128,1024]{2,1,0:T(8,128)} %slowness.1) | copy-start | bytes 3145732
  3.2 4.5 %copy-start.5 = (f32[2,2]{1,0:T(2,128)S(1)}, f32[2,2]{1,0:T(2,128)}, u32[]{:S(2)}) copy-start(f32[2,2]{1,0:T(2,128)} %coupling.1) | copy-start | bytes 52
  5.4 2.3 %collective-permute-start = (bf16[256,1024]{1,0:T(8,128)(2,1)S(1)}, bf16[256,1024]{1,0:T(8,128)(2,1)S(1)}, u32[]{:S(2)}, u32[]{:S(2)}) collective-permute-start(bf16[256,1024]{1,0:T(8,128)(2,1)S(1)} %get-tuple-element.58), channel_id=1, source_target_pairs={{0,1},{1,0},{2,3},{3,2},{4,5},{5,4},{6,7},{7,6},{8,9},{9,8},{10,11... | collective-permute-start | bytes 1572872 | tf_op jit(solution)/shard_map/ppermute | solution.py:513
  5.4 4.6 %copy-start = (bf16[1,2,128,2,1024]{4,3,2,1,0:T(2,128)(2,1)S(1)}, bf16[1,2,128,2,1024]{4,3,2,1,0:T(2,128)(2,1)}, u32[]{:S(2)}) copy-start(bf16[1,2,128,2,1024]{4,3,2,1,0:T(2,128)(2,1)} %field.3) | copy-start | bytes 3145732
  7.6 5.9 %copy-start.4 = (s32[1,1024]{1,0:T(1,128)S(1)}, s32[1,1024]{1,0:T(1,128)}, u32[]{:S(2)}) copy-start(s32[1,1024]{1,0:T(1,128)} %mask.1) | copy-start | bytes 12292
  10.7 2.9 %collective-permute-start.1 = (bf16[128,2,1024]{2,1,0:T(2,128)(2,1)S(1)}, bf16[128,2,1024]{2,1,0:T(2,128)(2,1)S(1)}, u32[]{:S(2)}, u32[]{:S(2)}) collective-permute-start(bf16[128,2,1024]{2,1,0:T(2,128)(2,1)S(1)} %away.1), channel_id=1, source_target_pairs={{0,1},{1,0},{2,3},{3,2},{4,5},{5,4},{6,7},{7,6},{8,9},{9,8},{10,11... | collective-permute-start | bytes 1572872 | tf_op jit(solution)/shard_map/ppermute | solution.py:513
  11.2 2.3 %collective-permute-start.2 = (f32[128,1024]{1,0:T(8,128)S(1)}, f32[128,1024]{1,0:T(8,128)S(1)}, u32[]{:S(2)}, u32[]{:S(2)}) collective-permute-start(f32[128,1024]{1,0:T(8,128)S(1)} %get-tuple-element.65.slow), channel_id=1, source_target_pairs={{0,1},{1,0},{2,3},{3,2},{4,5},{5,4},{6,7},{7,6},{8,9},{9,8},{10,11... | collective-permute-start | bytes 1572872 | tf_op jit(solution)/shard_map/ppermute | solution.py:513
  11.3 14.9 %collective-permute-start.3 = (bf16[512,512]{1,0:T(8,128)(2,1)S(1)}, bf16[512,512]{1,0:T(8,128)(2,1)S(1)}, u32[]{:S(2)}, u32[]{:S(2)}) collective-permute-start(bf16[512,512]{1,0:T(8,128)(2,1)S(1)} %get-tuple-element.66.cross0), channel_id=1, source_target_pairs={{0,2},{1,3},{2,0},{3,1},{4,6},{5,7},{6,4},{7,5},{8,10},{9,11},{10,... | collective-permute-start | bytes 1572872 | tf_op jit(solution)/shard_map/ppermute | solution.py:513
  12.9 20.0 %copy-start.6 = (s32[1,2]{1,0:T(1,128)S(1)}, s32[1,2]{1,0:T(1,128)}, u32[]{:S(2)}) copy-start(s32[1,2]{1,0:T(1,128)} %place.1) | copy-start | bytes 28
  13.0 16.0 %collective-permute-start.4 = (f16[128,512]{1,0:T(8,128)(2,1)S(1)}, f16[128,512]{1,0:T(8,128)(2,1)S(1)}, u32[]{:S(2)}, u32[]{:S(2)}) collective-permute-start(f16[128,512]{1,0:T(8,128)(2,1)S(1)} %get-tuple-element.110), channel_id=1, source_target_pairs={{0,2},{1,3},{2,0},{3,1},{4,6},{5,7},{6,4},{7,5},{8,10},{9,11},{10,... | collective-permute-start | bytes 393224 | tf_op jit(solution)/shard_map/ppermute | solution.py:513
  18.3 10.7 %collective-permute-start.5 = (f32[4,512]{1,0:T(4,128)S(1)}, f32[4,512]{1,0:T(4,128)S(1)}, u32[]{:S(2)}, u32[]{:S(2)}) collective-permute-start(f32[4,512]{1,0:T(4,128)S(1)} %get-tuple-element.70), channel_id=1, source_target_pairs={{0,4},{1,5},{2,6},{3,7},{4,0},{5,1},{6,2},{7,3},{8,12},{9,13},{10,... | collective-permute-start | bytes 24584 | tf_op jit(solution)/shard_map/ppermute | solution.py:513
  20.9 10.3 %collective-permute-start.6 = (f32[4,512]{1,0:T(4,128)S(1)}, f32[4,512]{1,0:T(4,128)S(1)}, u32[]{:S(2)}, u32[]{:S(2)}) collective-permute-start(f32[4,512]{1,0:T(4,128)S(1)} %get-tuple-element.71), channel_id=1, source_target_pairs={{0,6},{1,7},{2,4},{3,5},{4,2},{5,3},{6,0},{7,1},{8,14},{9,15},{10,... | collective-permute-start | bytes 24584 | tf_op jit(solution)/shard_map/ppermute | solution.py:513
  26.2 15.0 %collective-permute-start.8 = (bf16[512,512]{1,0:T(8,128)(2,1)S(1)}, bf16[512,512]{1,0:T(8,128)(2,1)S(1)}, u32[]{:S(2)}, u32[]{:S(2)}) collective-permute-start(bf16[512,512]{1,0:T(8,128)(2,1)S(1)} %get-tuple-element.82), channel_id=1, source_target_pairs={{0,2},{1,3},{2,0},{3,1},{4,6},{5,7},{6,4},{7,5},{8,10},{9,11},{10,... | collective-permute-start | bytes 1572872 | tf_op jit(solution)/shard_map/ppermute | solution.py:513
  31.3 1.6 %collective-permute-start.7 = (f16[2,128,512]{2,1,0:T(8,128)(2,1)S(1)}, f16[2,128,512]{2,1,0:T(8,128)(2,1)S(1)}, u32[]{:S(2)}, u32[]{:S(2)}) collective-permute-start(f16[2,128,512]{2,1,0:T(8,128)(2,1)S(1)} %pad_maximum_fusion), channel_id=1, source_target_pairs={{0,1},{1,0},{2,3},{3,2},{4,5},{5,4},{6,7},{7,6},{8,9},{9,8},{10,11... | collective-permute-start | bytes 786440 | tf_op jit(solution)/shard_map/ppermute | solution.py:513
  43.9 4.7 %collective-permute-start.9 = (f32[4,512]{1,0:T(4,128)S(1)}, f32[4,512]{1,0:T(4,128)S(1)}, u32[]{:S(2)}, u32[]{:S(2)}) collective-permute-start(f32[4,512]{1,0:T(4,128)S(1)} %pad_maximum_fusion.2.edge_x), channel_id=1, source_target_pairs={{0,4},{1,5},{2,6},{3,7},{4,0},{5,1},{6,2},{7,3},{8,12},{9,13},{10,... | collective-permute-start | bytes 24584 | tf_op jit(solution)/shard_map/ppermute | solution.py:513
  49.4 3.7 %collective-permute-start.10 = (f32[4,512]{1,0:T(4,128)S(1)}, f32[4,512]{1,0:T(4,128)S(1)}, u32[]{:S(2)}, u32[]{:S(2)}) collective-permute-start(f32[4,512]{1,0:T(4,128)S(1)} %get-tuple-element.93.edge), channel_id=1, source_target_pairs={{0,2},{1,3},{2,0},{3,1},{4,6},{5,7},{6,4},{7,5},{8,10},{9,11},{10,... | collective-permute-start | bytes 24584 | tf_op jit(solution)/shard_map/ppermute | solution.py:513
  54.8 1.6 %collective-permute-start.12 = (bf16[4,128,256]{2,1,0:T(8,128)(2,1)S(1)}, bf16[4,128,256]{2,1,0:T(8,128)(2,1)S(1)}, u32[]{:S(2)}, u32[]{:S(2)}) collective-permute-start(bf16[4,128,256]{2,1,0:T(8,128)(2,1)S(1)} %get-tuple-element.102), channel_id=1, source_target_pairs={{0,1},{1,0},{2,3},{3,2},{4,5},{5,4},{6,7},{7,6},{8,9},{9,8},{10,11... | collective-permute-start | bytes 786440 | tf_op jit(solution)/shard_map/ppermute | solution.py:513
  54.9 1.9 %collective-permute-start.11 = (bf16[4,128,256]{2,1,0:T(8,128)(2,1)S(1)}, bf16[4,128,256]{2,1,0:T(8,128)(2,1)S(1)}, u32[]{:S(2)}, u32[]{:S(2)}) collective-permute-start(bf16[4,128,256]{2,1,0:T(8,128)(2,1)S(1)} %get-tuple-element.96), channel_id=1, source_target_pairs={{0,1},{1,0},{2,3},{3,2},{4,5},{5,4},{6,7},{7,6},{8,9},{9,8},{10,11... | collective-permute-start | bytes 786440 | tf_op jit(solution)/shard_map/ppermute | solution.py:513
  56.9 7.9 %collective-permute-start.13 = (bf16[2,128,256]{2,1,0:T(8,128)(2,1)S(1)}, bf16[2,128,256]{2,1,0:T(8,128)(2,1)S(1)}, u32[]{:S(2)}, u32[]{:S(2)}) collective-permute-start(bf16[2,128,256]{2,1,0:T(8,128)(2,1)S(1)} %get-tuple-element.103), channel_id=1, source_target_pairs={{0,10},{1,11},{2,26},{3,27},{4,14},{5,15},{6,30},{7,31},{8,2},{9,3... | collective-permute-start | bytes 393224 | tf_op jit(solution)/shard_map/ppermute | solution.py:693
  58.4 7.9 %collective-permute-start.14 = (bf16[2,128,256]{2,1,0:T(8,128)(2,1)S(1)}, bf16[2,128,256]{2,1,0:T(8,128)(2,1)S(1)}, u32[]{:S(2)}, u32[]{:S(2)}) collective-permute-start(bf16[2,128,256]{2,1,0:T(8,128)(2,1)S(1)} %get-tuple-element.104), channel_id=1, source_target_pairs={{0,2},{1,3},{2,18},{3,19},{4,6},{5,7},{6,22},{7,23},{8,10},{9,11},... | collective-permute-start | bytes 393224 | tf_op jit(solution)/shard_map/ppermute | solution.py:693
  60.0 9.6 %collective-permute-start.16 = (bf16[2,128,256]{2,1,0:T(8,128)(2,1)S(1)}, bf16[2,128,256]{2,1,0:T(8,128)(2,1)S(1)}, u32[]{:S(2)}, u32[]{:S(2)}) collective-permute-start(bf16[2,128,256]{2,1,0:T(8,128)(2,1)S(1)} %get-tuple-element.105), channel_id=1, source_target_pairs={{0,0},{1,1},{2,16},{3,17},{4,4},{5,5},{6,20},{7,21},{8,8},{9,9},{1... | collective-permute-start | bytes 393224 | tf_op jit(solution)/shard_map/ppermute | solution.py:693
  63.3 7.6 %collective-permute-start.15 = (bf16[2,128,256]{2,1,0:T(8,128)(2,1)S(1)}, bf16[2,128,256]{2,1,0:T(8,128)(2,1)S(1)}, u32[]{:S(2)}, u32[]{:S(2)}) collective-permute-start(bf16[2,128,256]{2,1,0:T(8,128)(2,1)S(1)} %get-tuple-element.106), channel_id=1, source_target_pairs={{0,8},{1,9},{2,24},{3,25},{4,12},{5,13},{6,28},{7,29},{8,0},{9,1},... | collective-permute-start | bytes 393224 | tf_op jit(solution)/shard_map/ppermute | solution.py:693

commit v3 on v2

--- a/solution.py
+++ b/solution.py
@@ -681,16 +681,15 @@
     part1 = keep1.astype(F32) + move(send1, 1).astype(F32)
     both = jnp.stack([part0, part1], axis=1).astype(BF16)
     total = 0.0
-    for kz in (1, 0):
-        for kx in (1, 0):
-            route = []
-            for s in range(4):
-                for b in range(8):
-                    sy, sx, bx, bc = s // 2, s % 2, b // 4, b % 2
-                    by = (b // 2) % 2
-                    target = (by * 2 + (sx ^ kx)) * 8 + bx * 4 + (sy ^ kz) * 2 + bc
-                    route.append((s * 8 + b, target))
-            total = total + lax.ppermute(both[kz * 2 + kx], ("shot", "slab"), route).astype(F32)
+    for kz, kx in ((0, 1), (1, 1), (0, 0), (1, 0)):
+        route = []
+        for s in range(4):
+            for b in range(8):
+                sy, sx, bx, bc = s // 2, s % 2, b // 4, b % 2
+                by = (b // 2) % 2
+                target = (by * 2 + (sx ^ kx)) * 8 + bx * 4 + (sy ^ kz) * 2 + bc
+                route.append((s * 8 + b, target))
+        total = total + lax.ppermute(both[kz * 2 + kx], ("shot", "slab"), route).astype(F32)
     return total
 
 

time: 71.9 us -> 70.1 us (0.975)
  waiting for transfers between devices: 16.9 us -> 15.1 us
    ppermute x4, waiting for transfers between devices: 6.07 us -> 4.31 us  [block_shards(): lax.ppermute(both[kz * 2 + kx], ('shot', 'slab'), route).astype(F32)]
  transfers between devices with their start and end apart: 17 -> 17, of which waited for: 10 -> 10; matrix products, arithmetic and copies ran while one was open for 1% -> 1% of each run, Pallas kernels for 28% -> 29%
where the time goes in v3:
time: 70.1 us; the launch traced here: 69.9 us
  Pallas kernels  30.2 us (43%)
  starting transfers between devices  19.8 us (28%)
  waiting for transfers between devices  15.1 us (22%)
  local copies, waits for them, and re-layouts  3.26 us (5%)
  other arithmetic  1.21 us (2%)
    pallas_call x10, Pallas kernels, call(): pl.pallas_call(body, in_specs=specs, out_specs=[vmem] * len(outs), out_sh...  23.6 us
    ppermute x13, starting transfers between devices, move(): return lax.ppermute(array, 'slab', [(i, i ^ k) for i in range(8)])  11.9 us
    ppermute x13, waiting for transfers between devices, move(): return lax.ppermute(array, 'slab', [(i, i ^ k) for i in range(8)])  10.8 us
    ppermute x4, starting transfers between devices, block_shards(): lax.ppermute(both[kz * 2 + kx], ('shot', 'slab'), route).astype(F32)  7.87 us
    ppermute x4, waiting for transfers between devices, block_shards(): lax.ppermute(both[kz * 2 + kx], ('shot', 'slab'), route).astype(F32)  4.31 us
    unnamed x16, local copies, waits for them, and re-layouts  3.13 us
    pallas_call x1, Pallas kernels, block_shards(): pl.pallas_call(source_kernel, in_specs=[smem] * 3 + [vmem] * 3, out_specs...  2.37 us
    pallas_call x1, Pallas kernels, block_shards(): pl.pallas_call(other_kernel, in_specs=[smem, smem, vmem, vmem], out_specs...  2.15 us
  transfers between devices with their start and end apart: 17, of which 10 were waited for; matrix products, arithmetic and copies ran while one was open for 1% of the time, Pallas kernels for 29%

profile of v3, /device:TPU:4, one launch (start us, length us, event | category | flops | bytes accessed | tf_op | source)
XLA Modules:
  0.0 69.9 jit_solution(12678996737780376530)
XLA Ops:
  0.0 0.1 stack.48.meta
  0.1 1.2 %copy-done.1 = f32[2,128,1024]{2,1,0:T(8,128)S(1)} copy-done((f32[2,128,1024]{2,1,0:T(8,128)S(1)}, f32[2,128,1024]{2,1,0:T(8,128)}, u32[]{:S(2)}) %copy-start.1) | copy-done | bytes 1048600
  1.3 1.2 %copy-done.3 = bf16[1,2,128,2,1024]{4,3,2,1,0:T(2,128)(2,1)S(1)} copy-done((bf16[1,2,128,2,1024]{4,3,2,1,0:T(2,128)(2,1)S(1)}, bf16[1,2,128,2,1024]{4,3,2,1,0:T(2,128)(2,1)}, u32[]{:S(2)}) %copy-start.3) | copy-done | bytes 1048600
  2.5 0.7 copy-done.7
  3.2 2.2 %other.1 = (bf16[256,1024]{1,0:T(8,128)(2,1)S(1)}, bf16[128,2,1024]{2,1,0:T(2,128)(2,1)S(1)}, f32[128,1024]{1,0:T(8,128)S(1)}, f32[2]{0:T(128)S(1)}) custom-call(s32[6]{0:T(128)S(1)} %stack.48.meta, f32[2]{0:T(128)S(1)} %copy-done.7, bf16[1,2,128,2,1024]{4,3,2,1,0:T(2,128)(2,1)S(1)} %copy-done.3, f32[2,128,1024]{2,1,0:T(8,128)S(1)} %copy-done.1), custom_call_target="tpu_custom_call" | custom-call | tf_op jit(solution)/shard_map/other/pallas_call | solution.py:517
  5.4 0.1 collective-permute-start
  5.4 0.0 copy-start
  5.5 2.1 %own.1 = (bf16[256,1024]{1,0:T(8,128)(2,1)S(1)}, bf16[2,2,512,512]{3,2,1,0:T(8,128)(2,1)S(1)}) custom-call(s32[6]{0:T(128)S(1)} %stack.48.meta, f32[2]{0:T(128)S(1)} %get-tuple-element.54.freq, bf16[128,2,1024]{2,1,0:T(2,128)(2,1)S(1)} %get-tuple-element.55.raw, f32[128,1024]{1,0:T(8,128)S(1)} %get-tuple-element.65.slow, bf16[2,2,2,512,512]{4,3,2,1,0:T(8,128)(2,1)} %inverse.1), custom_call_target="tpu_custom_call" | custom-call | tf_op jit(solution)/shard_map/own/pallas_call | solution.py:525
  7.6 0.0 copy-done.2
  7.6 0.0 copy-start.4
  7.7 0.0 collective-permute-done.core
  7.7 0.0 copy-done.5
  7.7 2.4 %slab.1 = (bf16[512,512]{1,0:T(8,128)(2,1)S(1)}, bf16[512,512]{1,0:T(8,128)(2,1)S(1)}, f32[4,512]{1,0:T(4,128)S(1)}, f32[6]{0:T(128)S(1)}) custom-call(s32[6]{0:T(128)S(1)} %stack.48.meta, f32[2]{0:T(128)S(1)} %get-tuple-element.54.freq, f32[2,2]{1,0:T(2,128)S(1)} %copy-done.5, bf16[256,1024]{1,0:T(8,128)(2,1)S(1)} %get-tuple-element.57.own, ...), custom_call_target="tpu_custom_call" | custom-call | tf_op jit(solution)/shard_map/slab/pallas_call | solution.py:536
  10.1 0.0 copy-done
  10.1 0.6 away.1
  10.7 0.5 collective-permute-start.1
  11.2 0.1 collective-permute-start.2
  11.3 1.6 %collective-permute-start.3 = (bf16[512,512]{1,0:T(8,128)(2,1)S(1)}, bf16[512,512]{1,0:T(8,128)(2,1)S(1)}, u32[]{:S(2)}, u32[]{:S(2)}) collective-permute-start(bf16[512,512]{1,0:T(8,128)(2,1)S(1)} %get-tuple-element.66.cross0), channel_id=1, source_target_pairs={{0,2},{1,3},{2,0},{3,1},{4,6},{5,7},{6,4},{7,5},{8,10},{9,11},{10,... | collective-permute-start | bytes 1572872 | tf_op jit(solution)/shard_map/ppermute | solution.py:513
  12.9 0.0 copy-start.6
  12.9 0.1 fusion.11
  13.0 0.5 collective-permute-start.4
  13.5 0.0 collective-permute-done.1.core_raw
  13.5 0.0 collective-permute-done.2.core_slow
  13.5 0.0 copy-done.4
  13.5 4.7 %receiver.1 = (bf16[512,512]{1,0:T(8,128)(2,1)S(1)}, bf16[512,512]{1,0:T(8,128)(2,1)S(1)}, f32[4,512]{1,0:T(4,128)S(1)}, f32[4,512]{1,0:T(4,128)S(1)}) custom-call(s32[6]{0:T(128)S(1)} %stack.48.meta, f32[6]{0:T(128)S(1)} %get-tuple-element.60.scalars, s32[1,1024]{1,0:T(1,128)S(1)} %copy-done.4, bf16[1,2,128,2,1024]{4,3,2,1,0:T(2,128)(2,1)S(1)} %copy-done, ...), custom_call_target="tpu_custom_call" | custom-call | tf_op jit(solution)/shard_map/receiver/pallas_call | solution.py:502
  18.3 2.7 %collective-permute-start.5 = (f32[4,512]{1,0:T(4,128)S(1)}, f32[4,512]{1,0:T(4,128)S(1)}, u32[]{:S(2)}, u32[]{:S(2)}) collective-permute-start(f32[4,512]{1,0:T(4,128)S(1)} %get-tuple-element.70), channel_id=1, source_target_pairs={{0,4},{1,5},{2,6},{3,7},{4,0},{5,1},{6,2},{7,3},{8,12},{9,13},{10,... | collective-permute-start | bytes 24584 | tf_op jit(solution)/shard_map/ppermute | solution.py:513
  20.9 1.4 %collective-permute-start.6 = (f32[4,512]{1,0:T(4,128)S(1)}, f32[4,512]{1,0:T(4,128)S(1)}, u32[]{:S(2)}, u32[]{:S(2)}) collective-permute-start(f32[4,512]{1,0:T(4,128)S(1)} %get-tuple-element.71), channel_id=1, source_target_pairs={{0,6},{1,7},{2,4},{3,5},{4,2},{5,3},{6,0},{7,1},{8,14},{9,15},{10,... | collective-permute-start | bytes 24584 | tf_op jit(solution)/shard_map/ppermute | solution.py:513
  22.3 3.9 %collective-permute-done.3.far = bf16[512,512]{1,0:T(8,128)(2,1)S(1)} collective-permute-done((bf16[512,512]{1,0:T(8,128)(2,1)S(1)}, bf16[512,512]{1,0:T(8,128)(2,1)S(1)}, u32[]{:S(2)}, u32[]{:S(2)}) %collective-permute-start.3) | collective-permute-done | bytes 524320 | tf_op jit(solution)/shard_map/ppermute | solution.py:513
  26.2 1.4 %collective-permute-start.8 = (bf16[512,512]{1,0:T(8,128)(2,1)S(1)}, bf16[512,512]{1,0:T(8,128)(2,1)S(1)}, u32[]{:S(2)}, u32[]{:S(2)}) collective-permute-start(bf16[512,512]{1,0:T(8,128)(2,1)S(1)} %get-tuple-element.82), channel_id=1, source_target_pairs={{0,2},{1,3},{2,0},{3,1},{4,6},{5,7},{6,4},{7,5},{8,10},{9,11},{10,... | collective-permute-start | bytes 1572872 | tf_op jit(solution)/shard_map/ppermute | solution.py:513
  27.6 1.4 %collective-permute-done.4 = f16[128,512]{1,0:T(8,128)(2,1)S(1)} collective-permute-done((f16[128,512]{1,0:T(8,128)(2,1)S(1)}, f16[128,512]{1,0:T(8,128)(2,1)S(1)}, u32[]{:S(2)}, u32[]{:S(2)}) %collective-permute-start.4) | collective-permute-done | bytes 131104 | tf_op jit(solution)/shard_map/ppermute | solution.py:513
  29.0 0.0 collective-permute-done.5
  29.0 2.2 %collective-permute-done.6 = f32[4,512]{1,0:T(4,128)S(1)} collective-permute-done((f32[4,512]{1,0:T(4,128)S(1)}, f32[4,512]{1,0:T(4,128)S(1)}, u32[]{:S(2)}, u32[]{:S(2)}) %collective-permute-start.6) | collective-permute-done | bytes 8224 | tf_op jit(solution)/shard_map/ppermute | solution.py:513
  31.2 0.1 pad_maximum_fusion
  31.3 0.1 collective-permute-start.7
  31.4 1.5 %collective-permute-done.7 = f16[2,128,512]{2,1,0:T(8,128)(2,1)S(1)} collective-permute-done((f16[2,128,512]{2,1,0:T(8,128)(2,1)S(1)}, f16[2,128,512]{2,1,0:T(8,128)(2,1)S(1)}, u32[]{:S(2)}, u32[]{:S(2)}) %collective-permute-start.7) | collective-permute-done | bytes 262176 | tf_op jit(solution)/shard_map/ppermute | solution.py:513
  32.9 0.1 fusion.9
  32.9 2.1 %phase.1 = (f32[512,512]{1,0:T(8,128)S(1)}, f32[512,512]{1,0:T(8,128)S(1)}, f32[512,512]{1,0:T(8,128)S(1)}) custom-call(s32[6]{0:T(128)S(1)} %stack.48.meta, f32[6]{0:T(128)S(1)} %get-tuple-element.60.scalars, s32[1,2]{1,0:T(1,128)S(1)} %copy-done.6, f32[128,512]{1,0:T(8,128)S(1)} %get-tuple-element.111.own, f32[128,512]{1,0:T(8,128)S(1)} %get-tuple-element.108.core, ...), custom_call_target="tpu_custom_call" | custom-call | tf_op jit(solution)/shard_map/phase/pallas_call | solution.py:502
  35.0 2.7 %column.2 = (bf16[1024,512]{1,0:T(8,128)(2,1)S(1)}, bf16[1024,512]{1,0:T(8,128)(2,1)S(1)}, f32[2,512]{1,0:T(2,128)S(1)}) custom-call(s32[6]{0:T(128)S(1)} %stack.48.meta, f32[6]{0:T(128)S(1)} %get-tuple-element.60.scalars, bf16[512,512]{1,0:T(8,128)(2,1)S(1)} %get-tuple-element.63.same0.near, bf16[512,512]{1,0:T(8,128)(2,1)S(1)} %collective-permute-done.3.far, ...), custom_call_target="tpu_custom_call" | custom-call | tf_op jit(solution)/shard_map/column/pallas_call | solution.py:502
  37.7 3.5 %both.2 = (bf16[1024,512]{1,0:T(8,128)(2,1)S(1)}, f32[2,512]{1,0:T(2,128)S(1)}) custom-call(s32[6]{0:T(128)S(1)} %stack.48.meta, bf16[1024,512]{1,0:T(8,128)(2,1)S(1)} %get-tuple-element.79.shifted, bf16[2,2,512,512]{3,2,1,0:T(8,128)(2,1)S(1)} %get-tuple-element.59.blocks), custom_call_target="tpu_custom_call" | custom-call | tf_op jit(solution)/shard_map/both/pallas_call | solution.py:502
  41.2 0.0 collective-permute-done.8.far
  41.2 2.7 %column.3 = (bf16[1024,512]{1,0:T(8,128)(2,1)S(1)}, bf16[1024,512]{1,0:T(8,128)(2,1)S(1)}, f32[2,512]{1,0:T(2,128)S(1)}) custom-call(s32[6]{0:T(128)S(1)} %stack.48.meta, f32[6]{0:T(128)S(1)} %get-tuple-element.60.scalars, bf16[512,512]{1,0:T(8,128)(2,1)S(1)} %get-tuple-element.81.near, bf16[512,512]{1,0:T(8,128)(2,1)S(1)} %collective-permute-done.8.far, ...), custom_call_target="tpu_custom_call" | custom-call | tf_op jit(solution)/shard_map/column/pallas_call | solution.py:502
  43.9 1.4 %collective-permute-start.9 = (f32[4,512]{1,0:T(4,128)S(1)}, f32[4,512]{1,0:T(4,128)S(1)}, u32[]{:S(2)}, u32[]{:S(2)}) collective-permute-start(f32[4,512]{1,0:T(4,128)S(1)} %pad_maximum_fusion.2.edge_x), channel_id=1, source_target_pairs={{0,4},{1,5},{2,6},{3,7},{4,0},{5,1},{6,2},{7,3},{8,12},{9,13},{10,... | collective-permute-start | bytes 24584 | tf_op jit(solution)/shard_map/ppermute | solution.py:513
  45.3 3.3 %both.3 = (bf16[1024,512]{1,0:T(8,128)(2,1)S(1)}, f32[2,512]{1,0:T(2,128)S(1)}) custom-call(s32[6]{0:T(128)S(1)} %stack.48.meta, bf16[1024,512]{1,0:T(8,128)(2,1)S(1)} %get-tuple-element.85.shifted, bf16[2,2,512,512]{3,2,1,0:T(8,128)(2,1)S(1)} %get-tuple-element.59.blocks), custom_call_target="tpu_custom_call" | custom-call | tf_op jit(solution)/shard_map/both/pallas_call | solution.py:502
  48.6 0.0 collective-permute-done.9.near_x
  48.6 0.7 %turn.1 = (f32[4,512]{1,0:T(4,128)S(1)}, f32[4,512]{1,0:T(4,128)S(1)}) custom-call(s32[6]{0:T(128)S(1)} %stack.48.meta, f32[6]{0:T(128)S(1)} %get-tuple-element.60.scalars, f32[4,512]{1,0:T(4,128)S(1)} %pad_maximum_fusion.2.edge_x, f32[4,512]{1,0:T(4,128)S(1)} %collective-permute-done.9.near_x, f32[2,512]{1,0:T(2,128)S(1)} %get-tuple-element.84.edge_y0, ...), custom_call_target="tpu_custom_call" | custom-call | tf_op jit(solution)/shard_map/turn/pallas_call | solution.py:502
  49.4 1.6 %collective-permute-start.10 = (f32[4,512]{1,0:T(4,128)S(1)}, f32[4,512]{1,0:T(4,128)S(1)}, u32[]{:S(2)}, u32[]{:S(2)}) collective-permute-start(f32[4,512]{1,0:T(4,128)S(1)} %get-tuple-element.93.edge), channel_id=1, source_target_pairs={{0,2},{1,3},{2,0},{3,1},{4,6},{5,7},{6,4},{7,5},{8,10},{9,11},{10,... | collective-permute-start | bytes 24584 | tf_op jit(solution)/shard_map/ppermute | solution.py:513
  51.0 1.6 %between.1 = (f32[4,512]{1,0:T(4,128)S(1)}, bf16[4,128,256]{2,1,0:T(8,128)(2,1)S(1)}, bf16[4,128,256]{2,1,0:T(8,128)(2,1)S(1)}) custom-call(s32[6]{0:T(128)S(1)} %stack.48.meta, f32[4,512]{1,0:T(4,128)S(1)} %get-tuple-element.88.whole, bf16[2,2,512,512]{3,2,1,0:T(8,128)(2,1)S(1)} %get-tuple-element.59.blocks, ...), custom_call_target="tpu_custom_call" | custom-call | tf_op jit(solution)/shard_map/between/pallas_call | solution.py:502
  52.6 0.5 collective-permute-done.10.near
  53.1 1.7 %second_image.1 = (bf16[4,128,256]{2,1,0:T(8,128)(2,1)S(1)}, bf16[4,128,256]{2,1,0:T(8,128)(2,1)S(1)}) custom-call(s32[6]{0:T(128)S(1)} %stack.48.meta, f32[6]{0:T(128)S(1)} %get-tuple-element.60.scalars, bf16[1024,512]{1,0:T(8,128)(2,1)S(1)} %get-tuple-element.97.source, bf16[1024,512]{1,0:T(8,128)(2,1)S(1)} %get-tuple-element.98.receiver, ...), custom_call_target="tpu_custom_call" | custom-call | tf_op jit(solution)/shard_map/second_image/pallas_call | solution.py:502
  54.8 0.1 collective-permute-start.12
  54.9 0.5 collective-permute-start.11
  55.4 1.0 %collective-permute-done.12 = bf16[4,128,256]{2,1,0:T(8,128)(2,1)S(1)} collective-permute-done((bf16[4,128,256]{2,1,0:T(8,128)(2,1)S(1)}, bf16[4,128,256]{2,1,0:T(8,128)(2,1)S(1)}, u32[]{:S(2)}, u32[]{:S(2)}) %collective-permute-start.12) | collective-permute-done | bytes 262176 | tf_op jit(solution)/shard_map/ppermute | solution.py:513
  56.4 0.1 fusion.1
  56.5 0.3 collective-permute-done.11
  56.8 0.1 fusion
  56.9 2.5 %collective-permute-start.13 = (bf16[2,128,256]{2,1,0:T(8,128)(2,1)S(1)}, bf16[2,128,256]{2,1,0:T(8,128)(2,1)S(1)}, u32[]{:S(2)}, u32[]{:S(2)}) collective-permute-start(bf16[2,128,256]{2,1,0:T(8,128)(2,1)S(1)} %get-tuple-element.103), channel_id=1, source_target_pairs={{0,8},{1,9},{2,24},{3,25},{4,12},{5,13},{6,28},{7,29},{8,0},{9,1},... | collective-permute-start | bytes 393224 | tf_op jit(solution)/shard_map/ppermute | solution.py:692
  59.4 0.0 collective-permute-start.14
  59.4 1.9 %collective-permute-start.16 = (bf16[2,128,256]{2,1,0:T(8,128)(2,1)S(1)}, bf16[2,128,256]{2,1,0:T(8,128)(2,1)S(1)}, u32[]{:S(2)}, u32[]{:S(2)}) collective-permute-start(bf16[2,128,256]{2,1,0:T(8,128)(2,1)S(1)} %get-tuple-element.105), channel_id=1, source_target_pairs={{0,2},{1,3},{2,18},{3,19},{4,6},{5,7},{6,22},{7,23},{8,10},{9,11},... | collective-permute-start | bytes 393224 | tf_op jit(solution)/shard_map/ppermute | solution.py:692
  61.4 3.4 %collective-permute-start.15 = (bf16[2,128,256]{2,1,0:T(8,128)(2,1)S(1)}, bf16[2,128,256]{2,1,0:T(8,128)(2,1)S(1)}, u32[]{:S(2)}, u32[]{:S(2)}) collective-permute-start(bf16[2,128,256]{2,1,0:T(8,128)(2,1)S(1)} %get-tuple-element.106), channel_id=1, source_target_pairs={{0,0},{1,1},{2,16},{3,17},{4,4},{5,5},{6,20},{7,21},{8,8},{9,9},{1... | collective-permute-start | bytes 393224 | tf_op jit(solution)/shard_map/ppermute | solution.py:692
  64.8 0.0 collective-permute-done.13
  64.8 1.9 %collective-permute-done.14 = bf16[2,128,256]{2,1,0:T(8,128)(2,1)S(1)} collective-permute-done((bf16[2,128,256]{2,1,0:T(8,128)(2,1)S(1)}, bf16[2,128,256]{2,1,0:T(8,128)(2,1)S(1)}, u32[]{:S(2)}, u32[]{:S(2)}) %collective-permute-start.14) | collective-permute-done | bytes 131104 | tf_op jit(solution)/shard_map/ppermute | solution.py:692
  66.7 0.8 %collective-permute-done.16 = bf16[2,128,256]{2,1,0:T(8,128)(2,1)S(1)} collective-permute-done((bf16[2,128,256]{2,1,0:T(8,128)(2,1)S(1)}, bf16[2,128,256]{2,1,0:T(8,128)(2,1)S(1)}, u32[]{:S(2)}, u32[]{:S(2)}) %collective-permute-start.16) | collective-permute-done | bytes 131104 | tf_op jit(solution)/shard_map/ppermute | solution.py:692
  67.5 1.6 %collective-permute-done.15 = bf16[2,128,256]{2,1,0:T(8,128)(2,1)S(1)} collective-permute-done((bf16[2,128,256]{2,1,0:T(8,128)(2,1)S(1)}, bf16[2,128,256]{2,1,0:T(8,128)(2,1)S(1)}, u32[]{:S(2)}, u32[]{:S(2)}) %collective-permute-start.15) | collective-permute-done | bytes 131104 | tf_op jit(solution)/shard_map/ppermute | solution.py:692
  69.1 0.8 %convert_add_fusion = f32[2,128,256]{2,1,0:T(8,128)} fusion(bf16[2,128,256]{2,1,0:T(8,128)(2,1)S(1)} %collective-permute-done.16, bf16[2,128,256]{2,1,0:T(8,128)(2,1)S(1)} %collective-permute-done.15, bf16[2,128,256]{2,1,0:T(8,128)(2,1)S(1)} %collective-permute-done.14, bf16[2,128,256]{2,1,0:T(8,128)(2,1)S(1)} %collective-permute-done.13), kind=kLoop, calls=%fused_computation.13 | loop fusion | flops 458752 | bytes 786432 | tf_op jit(solution)/shard_map/add | solution.py:692
  (12 shorter events, 0.2 us)
Async XLA Ops:
  0.1 1.2 %copy-start.1 = (f32[2,128,1024]{2,1,0:T(8,128)S(1)}, f32[2,128,1024]{2,1,0:T(8,128)}, u32[]{:S(2)}) copy-start(f32[2,128,1024]{2,1,0:T(8,128)} %slowness.1) | copy-start | bytes 3145732
  1.3 1.2 %copy-start.3 = (bf16[1,2,128,2,1024]{4,3,2,1,0:T(2,128)(2,1)S(1)}, bf16[1,2,128,2,1024]{4,3,2,1,0:T(2,128)(2,1)}, u32[]{:S(2)}) copy-start(bf16[1,2,128,2,1024]{4,3,2,1,0:T(2,128)(2,1)} %field.2) | copy-start | bytes 3145732
  2.5 0.7 copy-start.7
  3.2 4.4 %copy-start.2 = (f32[2,128,1024]{2,1,0:T(8,128)S(1)}, f32[2,128,1024]{2,1,0:T(8,128)}, u32[]{:S(2)}) copy-start(f32[2,128,1024]{2,1,0:T(8,128)} %slowness.1) | copy-start | bytes 3145732
  3.2 4.5 %copy-start.5 = (f32[2,2]{1,0:T(2,128)S(1)}, f32[2,2]{1,0:T(2,128)}, u32[]{:S(2)}) copy-start(f32[2,2]{1,0:T(2,128)} %coupling.1) | copy-start | bytes 52
  5.4 2.3 %collective-permute-start = (bf16[256,1024]{1,0:T(8,128)(2,1)S(1)}, bf16[256,1024]{1,0:T(8,128)(2,1)S(1)}, u32[]{:S(2)}, u32[]{:S(2)}) collective-permute-start(bf16[256,1024]{1,0:T(8,128)(2,1)S(1)} %get-tuple-element.58), channel_id=1, source_target_pairs={{0,1},{1,0},{2,3},{3,2},{4,5},{5,4},{6,7},{7,6},{8,9},{9,8},{10,11... | collective-permute-start | bytes 1572872 | tf_op jit(solution)/shard_map/ppermute | solution.py:513
  5.4 4.6 %copy-start = (bf16[1,2,128,2,1024]{4,3,2,1,0:T(2,128)(2,1)S(1)}, bf16[1,2,128,2,1024]{4,3,2,1,0:T(2,128)(2,1)}, u32[]{:S(2)}) copy-start(bf16[1,2,128,2,1024]{4,3,2,1,0:T(2,128)(2,1)} %field.3) | copy-start | bytes 3145732
  7.6 5.9 %copy-start.4 = (s32[1,1024]{1,0:T(1,128)S(1)}, s32[1,1024]{1,0:T(1,128)}, u32[]{:S(2)}) copy-start(s32[1,1024]{1,0:T(1,128)} %mask.1) | copy-start | bytes 12292
  10.7 2.9 %collective-permute-start.1 = (bf16[128,2,1024]{2,1,0:T(2,128)(2,1)S(1)}, bf16[128,2,1024]{2,1,0:T(2,128)(2,1)S(1)}, u32[]{:S(2)}, u32[]{:S(2)}) collective-permute-start(bf16[128,2,1024]{2,1,0:T(2,128)(2,1)S(1)} %away.1), channel_id=1, source_target_pairs={{0,1},{1,0},{2,3},{3,2},{4,5},{5,4},{6,7},{7,6},{8,9},{9,8},{10,11... | collective-permute-start | bytes 1572872 | tf_op jit(solution)/shard_map/ppermute | solution.py:513
  11.2 2.3 %collective-permute-start.2 = (f32[128,1024]{1,0:T(8,128)S(1)}, f32[128,1024]{1,0:T(8,128)S(1)}, u32[]{:S(2)}, u32[]{:S(2)}) collective-permute-start(f32[128,1024]{1,0:T(8,128)S(1)} %get-tuple-element.65.slow), channel_id=1, source_target_pairs={{0,1},{1,0},{2,3},{3,2},{4,5},{5,4},{6,7},{7,6},{8,9},{9,8},{10,11... | collective-permute-start | bytes 1572872 | tf_op jit(solution)/shard_map/ppermute | solution.py:513
  11.3 14.9 %collective-permute-start.3 = (bf16[512,512]{1,0:T(8,128)(2,1)S(1)}, bf16[512,512]{1,0:T(8,128)(2,1)S(1)}, u32[]{:S(2)}, u32[]{:S(2)}) collective-permute-start(bf16[512,512]{1,0:T(8,128)(2,1)S(1)} %get-tuple-element.66.cross0), channel_id=1, source_target_pairs={{0,2},{1,3},{2,0},{3,1},{4,6},{5,7},{6,4},{7,5},{8,10},{9,11},{10,... | collective-permute-start | bytes 1572872 | tf_op jit(solution)/shard_map/ppermute | solution.py:513
  12.9 20.0 %copy-start.6 = (s32[1,2]{1,0:T(1,128)S(1)}, s32[1,2]{1,0:T(1,128)}, u32[]{:S(2)}) copy-start(s32[1,2]{1,0:T(1,128)} %place.1) | copy-start | bytes 28
  13.0 16.0 %collective-permute-start.4 = (f16[128,512]{1,0:T(8,128)(2,1)S(1)}, f16[128,512]{1,0:T(8,128)(2,1)S(1)}, u32[]{:S(2)}, u32[]{:S(2)}) collective-permute-start(f16[128,512]{1,0:T(8,128)(2,1)S(1)} %get-tuple-element.110), channel_id=1, source_target_pairs={{0,2},{1,3},{2,0},{3,1},{4,6},{5,7},{6,4},{7,5},{8,10},{9,11},{10,... | collective-permute-start | bytes 393224 | tf_op jit(solution)/shard_map/ppermute | solution.py:513
  18.3 10.7 %collective-permute-start.5 = (f32[4,512]{1,0:T(4,128)S(1)}, f32[4,512]{1,0:T(4,128)S(1)}, u32[]{:S(2)}, u32[]{:S(2)}) collective-permute-start(f32[4,512]{1,0:T(4,128)S(1)} %get-tuple-element.70), channel_id=1, source_target_pairs={{0,4},{1,5},{2,6},{3,7},{4,0},{5,1},{6,2},{7,3},{8,12},{9,13},{10,... | collective-permute-start | bytes 24584 | tf_op jit(solution)/shard_map/ppermute | solution.py:513
  20.9 10.3 %collective-permute-start.6 = (f32[4,512]{1,0:T(4,128)S(1)}, f32[4,512]{1,0:T(4,128)S(1)}, u32[]{:S(2)}, u32[]{:S(2)}) collective-permute-start(f32[4,512]{1,0:T(4,128)S(1)} %get-tuple-element.71), channel_id=1, source_target_pairs={{0,6},{1,7},{2,4},{3,5},{4,2},{5,3},{6,0},{7,1},{8,14},{9,15},{10,... | collective-permute-start | bytes 24584 | tf_op jit(solution)/shard_map/ppermute | solution.py:513
  26.2 15.0 %collective-permute-start.8 = (bf16[512,512]{1,0:T(8,128)(2,1)S(1)}, bf16[512,512]{1,0:T(8,128)(2,1)S(1)}, u32[]{:S(2)}, u32[]{:S(2)}) collective-permute-start(bf16[512,512]{1,0:T(8,128)(2,1)S(1)} %get-tuple-element.82), channel_id=1, source_target_pairs={{0,2},{1,3},{2,0},{3,1},{4,6},{5,7},{6,4},{7,5},{8,10},{9,11},{10,... | collective-permute-start | bytes 1572872 | tf_op jit(solution)/shard_map/ppermute | solution.py:513
  31.3 1.6 %collective-permute-start.7 = (f16[2,128,512]{2,1,0:T(8,128)(2,1)S(1)}, f16[2,128,512]{2,1,0:T(8,128)(2,1)S(1)}, u32[]{:S(2)}, u32[]{:S(2)}) collective-permute-start(f16[2,128,512]{2,1,0:T(8,128)(2,1)S(1)} %pad_maximum_fusion), channel_id=1, source_target_pairs={{0,1},{1,0},{2,3},{3,2},{4,5},{5,4},{6,7},{7,6},{8,9},{9,8},{10,11... | collective-permute-start | bytes 786440 | tf_op jit(solution)/shard_map/ppermute | solution.py:513
  43.9 4.7 %collective-permute-start.9 = (f32[4,512]{1,0:T(4,128)S(1)}, f32[4,512]{1,0:T(4,128)S(1)}, u32[]{:S(2)}, u32[]{:S(2)}) collective-permute-start(f32[4,512]{1,0:T(4,128)S(1)} %pad_maximum_fusion.2.edge_x), channel_id=1, source_target_pairs={{0,4},{1,5},{2,6},{3,7},{4,0},{5,1},{6,2},{7,3},{8,12},{9,13},{10,... | collective-permute-start | bytes 24584 | tf_op jit(solution)/shard_map/ppermute | solution.py:513
  49.4 3.7 %collective-permute-start.10 = (f32[4,512]{1,0:T(4,128)S(1)}, f32[4,512]{1,0:T(4,128)S(1)}, u32[]{:S(2)}, u32[]{:S(2)}) collective-permute-start(f32[4,512]{1,0:T(4,128)S(1)} %get-tuple-element.93.edge), channel_id=1, source_target_pairs={{0,2},{1,3},{2,0},{3,1},{4,6},{5,7},{6,4},{7,5},{8,10},{9,11},{10,... | collective-permute-start | bytes 24584 | tf_op jit(solution)/shard_map/ppermute | solution.py:513
  54.8 1.6 %collective-permute-start.12 = (bf16[4,128,256]{2,1,0:T(8,128)(2,1)S(1)}, bf16[4,128,256]{2,1,0:T(8,128)(2,1)S(1)}, u32[]{:S(2)}, u32[]{:S(2)}) collective-permute-start(bf16[4,128,256]{2,1,0:T(8,128)(2,1)S(1)} %get-tuple-element.102), channel_id=1, source_target_pairs={{0,1},{1,0},{2,3},{3,2},{4,5},{5,4},{6,7},{7,6},{8,9},{9,8},{10,11... | collective-permute-start | bytes 786440 | tf_op jit(solution)/shard_map/ppermute | solution.py:513
  54.9 1.9 %collective-permute-start.11 = (bf16[4,128,256]{2,1,0:T(8,128)(2,1)S(1)}, bf16[4,128,256]{2,1,0:T(8,128)(2,1)S(1)}, u32[]{:S(2)}, u32[]{:S(2)}) collective-permute-start(bf16[4,128,256]{2,1,0:T(8,128)(2,1)S(1)} %get-tuple-element.96), channel_id=1, source_target_pairs={{0,1},{1,0},{2,3},{3,2},{4,5},{5,4},{6,7},{7,6},{8,9},{9,8},{10,11... | collective-permute-start | bytes 786440 | tf_op jit(solution)/shard_map/ppermute | solution.py:513
  56.9 7.9 %collective-permute-start.13 = (bf16[2,128,256]{2,1,0:T(8,128)(2,1)S(1)}, bf16[2,128,256]{2,1,0:T(8,128)(2,1)S(1)}, u32[]{:S(2)}, u32[]{:S(2)}) collective-permute-start(bf16[2,128,256]{2,1,0:T(8,128)(2,1)S(1)} %get-tuple-element.103), channel_id=1, source_target_pairs={{0,8},{1,9},{2,24},{3,25},{4,12},{5,13},{6,28},{7,29},{8,0},{9,1},... | collective-permute-start | bytes 393224 | tf_op jit(solution)/shard_map/ppermute | solution.py:692
  59.4 7.3 %collective-permute-start.14 = (bf16[2,128,256]{2,1,0:T(8,128)(2,1)S(1)}, bf16[2,128,256]{2,1,0:T(8,128)(2,1)S(1)}, u32[]{:S(2)}, u32[]{:S(2)}) collective-permute-start(bf16[2,128,256]{2,1,0:T(8,128)(2,1)S(1)} %get-tuple-element.104), channel_id=1, source_target_pairs={{0,10},{1,11},{2,26},{3,27},{4,14},{5,15},{6,30},{7,31},{8,2},{9,3... | collective-permute-start | bytes 393224 | tf_op jit(solution)/shard_map/ppermute | solution.py:692
  59.4 8.1 %collective-permute-start.16 = (bf16[2,128,256]{2,1,0:T(8,128)(2,1)S(1)}, bf16[2,128,256]{2,1,0:T(8,128)(2,1)S(1)}, u32[]{:S(2)}, u32[]{:S(2)}) collective-permute-start(bf16[2,128,256]{2,1,0:T(8,128)(2,1)S(1)} %get-tuple-element.105), channel_id=1, source_target_pairs={{0,2},{1,3},{2,18},{3,19},{4,6},{5,7},{6,22},{7,23},{8,10},{9,11},... | collective-permute-start | bytes 393224 | tf_op jit(solution)/shard_map/ppermute | solution.py:692
  61.4 7.7 %collective-permute-start.15 = (bf16[2,128,256]{2,1,0:T(8,128)(2,1)S(1)}, bf16[2,128,256]{2,1,0:T(8,128)(2,1)S(1)}, u32[]{:S(2)}, u32[]{:S(2)}) collective-permute-start(bf16[2,128,256]{2,1,0:T(8,128)(2,1)S(1)} %get-tuple-element.106), channel_id=1, source_target_pairs={{0,0},{1,1},{2,16},{3,17},{4,4},{5,5},{6,20},{7,21},{8,8},{9,9},{1... | collective-permute-start | bytes 393224 | tf_op jit(solution)/shard_map/ppermute | solution.py:692

commit v4 on v3

--- a/solution.py
+++ b/solution.py
@@ -325,11 +325,12 @@
 
 
 def column_kernel(
-    meta, scalars, near, far, blocks, edge_same, edge_cross, sine, cosine, solved, shifted, own_edge, real, imag
+    meta, scalars, near, far, blocks, edge_same, edge_cross, sine, cosine, solved, shifted, own_edge, lines
 ):
     rows = near.shape[0] // 4
     half = near.shape[1]
     xb = meta[2]
+    real, imag = lines.at[pl.ds(0, half)], lines.at[pl.ds(half, half)]
     for k, (piece, n) in enumerate(((near, 0), (near, 1), (far, 0), (far, 1))):
         start = pl.multiple_of((meta[3] ^ k) * rows, rows)
         real[pl.ds(start, rows)] = piece[2 * n * rows : (2 * n + 1) * rows]
@@ -350,13 +351,11 @@
         ref[half - 16 :] = (
             ref[half - 16 :].astype(F32) + jnp.where(high & jnp.logical_not(upper), add, 0.0)
         ).astype(BF16)
-    left = jnp.concatenate([blocks[0, xb], blocks[1, xb]], axis=0)
+    left = complex_block(blocks, xb)
     for n in range(0, half, 256):
         cols = slice(n, n + 256)
-        by_real = dot(left, real[:, cols])
-        by_imag = dot(left, imag[:, cols])
-        xr = (by_real[:half] - by_imag[half:]).astype(BF16)
-        xi = (by_imag[:half] + by_real[half:]).astype(BF16)
+        x = dot(left, lines[:, cols]).astype(BF16)
+        xr, xi = x[:half], x[half:]
         solved[:half, cols] = xr
         solved[half:, cols] = xi
         xr, xi = xr.astype(F32), xi.astype(F32)
@@ -368,23 +367,25 @@
     own_edge[1:2] = own_imag
 
 
+def complex_block(blocks, block):
+    real, imag = blocks[0, block], blocks[1, block]
+    return jnp.concatenate(
+        [jnp.concatenate([real, -imag], axis=1), jnp.concatenate([imag, real], axis=1)], axis=0
+    )
+
+
 def both_kernel(meta, shifted, blocks, solved, edge):
     half = shifted.shape[1]
     xb, zz = meta[2], meta[1]
-    left = jnp.concatenate([blocks[0, xb], blocks[1, xb]], axis=0)
-    by_real = dot(left, shifted[:half])
-    by_imag = dot(left, shifted[half:])
-    u = jnp.concatenate(
-        [(by_real[:half] - by_imag[half:]).astype(BF16), (by_imag[:half] + by_real[half:]).astype(BF16)], axis=0
-    )
+    u = dot(complex_block(blocks, xb), shifted[...]).astype(BF16)
     row = dot_t(edge_rows(meta, blocks, zz, slice(0, half)), u)
     edge_real, edge_imag = edge_product(zz, row[:, :half], row[:, half:])
     edge[0:1] = edge_real
     edge[1:2] = edge_imag
-    by_real = dot_t(u, blocks[0, zz])
-    by_imag = dot_t(u, blocks[1, zz])
-    solved[:half] = (by_real[:half] - by_imag[half:]).astype(BF16)
-    solved[half:] = (by_real[half:] + by_imag[:half]).astype(BF16)
+    wide = jnp.concatenate([u[:half], u[half:]], axis=1)
+    real, imag = blocks[0, zz], blocks[1, zz]
+    solved[:half] = dot_t(wide, jnp.concatenate([real, -imag], axis=1)).astype(BF16)
+    solved[half:] = dot_t(wide, jnp.concatenate([imag, real], axis=1)).astype(BF16)
 
 
 def image_pieces(meta, image, keep, send):
@@ -607,7 +608,7 @@
             "column",
             [smem, smem] + [vmem] * 7,
             [pair, pair, line],
-            [VMEM((half, half), BF16)] * 2,
+            [VMEM((2 * half, half), BF16)],
             16,
             meta,
             scalars,

time: 70.1 us -> 69.9 us (level)
  transfers between devices with their start and end apart: 17 -> 17, of which waited for: 10 -> 10; matrix products, arithmetic and copies ran while one was open for 1% -> 1% of each run, Pallas kernels for 29% -> 28%
where the time goes in v4:
time: 69.9 us; the launch traced here: 69.7 us
  Pallas kernels  29.9 us (43%)
  starting transfers between devices  20 us (29%)
  waiting for transfers between devices  15.1 us (22%)
  local copies, waits for them, and re-layouts  3.26 us (5%)
  other arithmetic  1.21 us (2%)
    pallas_call x10, Pallas kernels, call(): pl.pallas_call(body, in_specs=specs, out_specs=[vmem] * len(outs), out_sh...  23.2 us
    ppermute x13, starting transfers between devices, move(): return lax.ppermute(array, 'slab', [(i, i ^ k) for i in range(8)])  12.1 us
    ppermute x13, waiting for transfers between devices, move(): return lax.ppermute(array, 'slab', [(i, i ^ k) for i in range(8)])  10.8 us
    ppermute x4, starting transfers between devices, block_shards(): lax.ppermute(both[kz * 2 + kx], ('shot', 'slab'), route).astype(F32)  7.87 us
    ppermute x4, waiting for transfers between devices, block_shards(): lax.ppermute(both[kz * 2 + kx], ('shot', 'slab'), route).astype(F32)  4.31 us
    unnamed x16, local copies, waits for them, and re-layouts  3.13 us
    pallas_call x1, Pallas kernels, block_shards(): pl.pallas_call(source_kernel, in_specs=[smem] * 3 + [vmem] * 3, out_specs...  2.37 us
    pallas_call x1, Pallas kernels, block_shards(): pl.pallas_call(other_kernel, in_specs=[smem, smem, vmem, vmem], out_specs...  2.15 us
  transfers between devices with their start and end apart: 17, of which 10 were waited for; matrix products, arithmetic and copies ran while one was open for 1% of the time, Pallas kernels for 28%

profile of v4, /device:TPU:4, one launch (start us, length us, event | category | flops | bytes accessed | tf_op | source)
XLA Modules:
  0.0 69.7 jit_solution(17705925790584731220)
XLA Ops:
  0.0 0.1 stack.48.meta
  0.1 1.2 %copy-done.1 = f32[2,128,1024]{2,1,0:T(8,128)S(1)} copy-done((f32[2,128,1024]{2,1,0:T(8,128)S(1)}, f32[2,128,1024]{2,1,0:T(8,128)}, u32[]{:S(2)}) %copy-start.1) | copy-done | bytes 1048600
  1.3 1.2 %copy-done.3 = bf16[1,2,128,2,1024]{4,3,2,1,0:T(2,128)(2,1)S(1)} copy-done((bf16[1,2,128,2,1024]{4,3,2,1,0:T(2,128)(2,1)S(1)}, bf16[1,2,128,2,1024]{4,3,2,1,0:T(2,128)(2,1)}, u32[]{:S(2)}) %copy-start.3) | copy-done | bytes 1048600
  2.5 0.7 copy-done.7
  3.2 2.2 %other.1 = (bf16[256,1024]{1,0:T(8,128)(2,1)S(1)}, bf16[128,2,1024]{2,1,0:T(2,128)(2,1)S(1)}, f32[128,1024]{1,0:T(8,128)S(1)}, f32[2]{0:T(128)S(1)}) custom-call(s32[6]{0:T(128)S(1)} %stack.48.meta, f32[2]{0:T(128)S(1)} %copy-done.7, bf16[1,2,128,2,1024]{4,3,2,1,0:T(2,128)(2,1)S(1)} %copy-done.3, f32[2,128,1024]{2,1,0:T(8,128)S(1)} %copy-done.1), custom_call_target="tpu_custom_call" | custom-call | tf_op jit(solution)/shard_map/other/pallas_call | solution.py:518
  5.4 0.1 collective-permute-start
  5.4 0.0 copy-start
  5.5 2.1 %own.1 = (bf16[256,1024]{1,0:T(8,128)(2,1)S(1)}, bf16[2,2,512,512]{3,2,1,0:T(8,128)(2,1)S(1)}) custom-call(s32[6]{0:T(128)S(1)} %stack.48.meta, f32[2]{0:T(128)S(1)} %get-tuple-element.54.freq, bf16[128,2,1024]{2,1,0:T(2,128)(2,1)S(1)} %get-tuple-element.55.raw, f32[128,1024]{1,0:T(8,128)S(1)} %get-tuple-element.65.slow, bf16[2,2,2,512,512]{4,3,2,1,0:T(8,128)(2,1)} %inverse.1), custom_call_target="tpu_custom_call" | custom-call | tf_op jit(solution)/shard_map/own/pallas_call | solution.py:526
  7.6 0.0 copy-done.2
  7.6 0.0 copy-start.4
  7.7 0.0 collective-permute-done.core
  7.7 0.0 copy-done.5
  7.7 2.4 %slab.1 = (bf16[512,512]{1,0:T(8,128)(2,1)S(1)}, bf16[512,512]{1,0:T(8,128)(2,1)S(1)}, f32[4,512]{1,0:T(4,128)S(1)}, f32[6]{0:T(128)S(1)}) custom-call(s32[6]{0:T(128)S(1)} %stack.48.meta, f32[2]{0:T(128)S(1)} %get-tuple-element.54.freq, f32[2,2]{1,0:T(2,128)S(1)} %copy-done.5, bf16[256,1024]{1,0:T(8,128)(2,1)S(1)} %get-tuple-element.57.own, ...), custom_call_target="tpu_custom_call" | custom-call | tf_op jit(solution)/shard_map/slab/pallas_call | solution.py:537
  10.1 0.0 copy-done
  10.1 0.6 away.1
  10.7 0.5 collective-permute-start.1
  11.2 0.1 collective-permute-start.2
  11.3 1.6 %collective-permute-start.3 = (bf16[512,512]{1,0:T(8,128)(2,1)S(1)}, bf16[512,512]{1,0:T(8,128)(2,1)S(1)}, u32[]{:S(2)}, u32[]{:S(2)}) collective-permute-start(bf16[512,512]{1,0:T(8,128)(2,1)S(1)} %get-tuple-element.66.cross0), channel_id=1, source_target_pairs={{0,2},{1,3},{2,0},{3,1},{4,6},{5,7},{6,4},{7,5},{8,10},{9,11},{10,... | collective-permute-start | bytes 1572872 | tf_op jit(solution)/shard_map/ppermute | solution.py:514
  12.9 0.0 copy-start.6
  12.9 0.1 fusion.11
  13.0 0.5 collective-permute-start.4
  13.5 0.0 collective-permute-done.1.core_raw
  13.5 0.0 collective-permute-done.2.core_slow
  13.5 4.7 %receiver.1 = (bf16[512,512]{1,0:T(8,128)(2,1)S(1)}, bf16[512,512]{1,0:T(8,128)(2,1)S(1)}, f32[4,512]{1,0:T(4,128)S(1)}, f32[4,512]{1,0:T(4,128)S(1)}) custom-call(s32[6]{0:T(128)S(1)} %stack.48.meta, f32[6]{0:T(128)S(1)} %get-tuple-element.60.scalars, s32[1,1024]{1,0:T(1,128)S(1)} %copy-done.4, bf16[1,2,128,2,1024]{4,3,2,1,0:T(2,128)(2,1)S(1)} %copy-done, ...), custom_call_target="tpu_custom_call" | custom-call | tf_op jit(solution)/shard_map/receiver/pallas_call | solution.py:503
  18.3 2.7 %collective-permute-start.5 = (f32[4,512]{1,0:T(4,128)S(1)}, f32[4,512]{1,0:T(4,128)S(1)}, u32[]{:S(2)}, u32[]{:S(2)}) collective-permute-start(f32[4,512]{1,0:T(4,128)S(1)} %get-tuple-element.70), channel_id=1, source_target_pairs={{0,4},{1,5},{2,6},{3,7},{4,0},{5,1},{6,2},{7,3},{8,12},{9,13},{10,... | collective-permute-start | bytes 24584 | tf_op jit(solution)/shard_map/ppermute | solution.py:514
  20.9 1.4 %collective-permute-start.6 = (f32[4,512]{1,0:T(4,128)S(1)}, f32[4,512]{1,0:T(4,128)S(1)}, u32[]{:S(2)}, u32[]{:S(2)}) collective-permute-start(f32[4,512]{1,0:T(4,128)S(1)} %get-tuple-element.71), channel_id=1, source_target_pairs={{0,6},{1,7},{2,4},{3,5},{4,2},{5,3},{6,0},{7,1},{8,14},{9,15},{10,... | collective-permute-start | bytes 24584 | tf_op jit(solution)/shard_map/ppermute | solution.py:514
  22.3 3.9 %collective-permute-done.3.far = bf16[512,512]{1,0:T(8,128)(2,1)S(1)} collective-permute-done((bf16[512,512]{1,0:T(8,128)(2,1)S(1)}, bf16[512,512]{1,0:T(8,128)(2,1)S(1)}, u32[]{:S(2)}, u32[]{:S(2)}) %collective-permute-start.3) | collective-permute-done | bytes 524320 | tf_op jit(solution)/shard_map/ppermute | solution.py:514
  26.2 1.4 %collective-permute-start.8 = (bf16[512,512]{1,0:T(8,128)(2,1)S(1)}, bf16[512,512]{1,0:T(8,128)(2,1)S(1)}, u32[]{:S(2)}, u32[]{:S(2)}) collective-permute-start(bf16[512,512]{1,0:T(8,128)(2,1)S(1)} %get-tuple-element.82), channel_id=1, source_target_pairs={{0,2},{1,3},{2,0},{3,1},{4,6},{5,7},{6,4},{7,5},{8,10},{9,11},{10,... | collective-permute-start | bytes 1572872 | tf_op jit(solution)/shard_map/ppermute | solution.py:514
  27.6 1.4 %collective-permute-done.4 = f16[128,512]{1,0:T(8,128)(2,1)S(1)} collective-permute-done((f16[128,512]{1,0:T(8,128)(2,1)S(1)}, f16[128,512]{1,0:T(8,128)(2,1)S(1)}, u32[]{:S(2)}, u32[]{:S(2)}) %collective-permute-start.4) | collective-permute-done | bytes 131104 | tf_op jit(solution)/shard_map/ppermute | solution.py:514
  29.0 0.0 collective-permute-done.5
  29.0 2.2 %collective-permute-done.6 = f32[4,512]{1,0:T(4,128)S(1)} collective-permute-done((f32[4,512]{1,0:T(4,128)S(1)}, f32[4,512]{1,0:T(4,128)S(1)}, u32[]{:S(2)}, u32[]{:S(2)}) %collective-permute-start.6) | collective-permute-done | bytes 8224 | tf_op jit(solution)/shard_map/ppermute | solution.py:514
  31.2 0.1 pad_maximum_fusion
  31.3 0.1 collective-permute-start.7
  31.4 1.5 %collective-permute-done.7 = f16[2,128,512]{2,1,0:T(8,128)(2,1)S(1)} collective-permute-done((f16[2,128,512]{2,1,0:T(8,128)(2,1)S(1)}, f16[2,128,512]{2,1,0:T(8,128)(2,1)S(1)}, u32[]{:S(2)}, u32[]{:S(2)}) %collective-permute-start.7) | collective-permute-done | bytes 262176 | tf_op jit(solution)/shard_map/ppermute | solution.py:514
  32.9 0.1 fusion.9
  32.9 0.0 copy-done.6
  32.9 2.1 %phase.1 = (f32[512,512]{1,0:T(8,128)S(1)}, f32[512,512]{1,0:T(8,128)S(1)}, f32[512,512]{1,0:T(8,128)S(1)}) custom-call(s32[6]{0:T(128)S(1)} %stack.48.meta, f32[6]{0:T(128)S(1)} %get-tuple-element.60.scalars, s32[1,2]{1,0:T(1,128)S(1)} %copy-done.6, f32[128,512]{1,0:T(8,128)S(1)} %get-tuple-element.111.own, f32[128,512]{1,0:T(8,128)S(1)} %get-tuple-element.108.core, ...), custom_call_target="tpu_custom_call" | custom-call | tf_op jit(solution)/shard_map/phase/pallas_call | solution.py:503
  35.0 2.6 %column.2 = (bf16[1024,512]{1,0:T(8,128)(2,1)S(1)}, bf16[1024,512]{1,0:T(8,128)(2,1)S(1)}, f32[2,512]{1,0:T(2,128)S(1)}) custom-call(s32[6]{0:T(128)S(1)} %stack.48.meta, f32[6]{0:T(128)S(1)} %get-tuple-element.60.scalars, bf16[512,512]{1,0:T(8,128)(2,1)S(1)} %get-tuple-element.63.same0.near, bf16[512,512]{1,0:T(8,128)(2,1)S(1)} %collective-permute-done.3.far, ...), custom_call_target="tpu_custom_call" | custom-call | tf_op jit(solution)/shard_map/column/pallas_call | solution.py:503
  37.6 3.4 %both.2 = (bf16[1024,512]{1,0:T(8,128)(2,1)S(1)}, f32[2,512]{1,0:T(2,128)S(1)}) custom-call(s32[6]{0:T(128)S(1)} %stack.48.meta, bf16[1024,512]{1,0:T(8,128)(2,1)S(1)} %get-tuple-element.79.shifted, bf16[2,2,512,512]{3,2,1,0:T(8,128)(2,1)S(1)} %get-tuple-element.59.blocks), custom_call_target="tpu_custom_call" | custom-call | tf_op jit(solution)/shard_map/both/pallas_call | solution.py:503
  41.0 0.0 collective-permute-done.8.far
  41.0 2.6 %column.3 = (bf16[1024,512]{1,0:T(8,128)(2,1)S(1)}, bf16[1024,512]{1,0:T(8,128)(2,1)S(1)}, f32[2,512]{1,0:T(2,128)S(1)}) custom-call(s32[6]{0:T(128)S(1)} %stack.48.meta, f32[6]{0:T(128)S(1)} %get-tuple-element.60.scalars, bf16[512,512]{1,0:T(8,128)(2,1)S(1)} %get-tuple-element.81.near, bf16[512,512]{1,0:T(8,128)(2,1)S(1)} %collective-permute-done.8.far, ...), custom_call_target="tpu_custom_call" | custom-call | tf_op jit(solution)/shard_map/column/pallas_call | solution.py:503
  43.7 1.6 %collective-permute-start.9 = (f32[4,512]{1,0:T(4,128)S(1)}, f32[4,512]{1,0:T(4,128)S(1)}, u32[]{:S(2)}, u32[]{:S(2)}) collective-permute-start(f32[4,512]{1,0:T(4,128)S(1)} %pad_maximum_fusion.2.edge_x), channel_id=1, source_target_pairs={{0,4},{1,5},{2,6},{3,7},{4,0},{5,1},{6,2},{7,3},{8,12},{9,13},{10,... | collective-permute-start | bytes 24584 | tf_op jit(solution)/shard_map/ppermute | solution.py:514
  45.3 3.2 %both.3 = (bf16[1024,512]{1,0:T(8,128)(2,1)S(1)}, f32[2,512]{1,0:T(2,128)S(1)}) custom-call(s32[6]{0:T(128)S(1)} %stack.48.meta, bf16[1024,512]{1,0:T(8,128)(2,1)S(1)} %get-tuple-element.85.shifted, bf16[2,2,512,512]{3,2,1,0:T(8,128)(2,1)S(1)} %get-tuple-element.59.blocks), custom_call_target="tpu_custom_call" | custom-call | tf_op jit(solution)/shard_map/both/pallas_call | solution.py:503
  48.4 0.0 collective-permute-done.9.near_x
  48.5 0.7 %turn.1 = (f32[4,512]{1,0:T(4,128)S(1)}, f32[4,512]{1,0:T(4,128)S(1)}) custom-call(s32[6]{0:T(128)S(1)} %stack.48.meta, f32[6]{0:T(128)S(1)} %get-tuple-element.60.scalars, f32[4,512]{1,0:T(4,128)S(1)} %pad_maximum_fusion.2.edge_x, f32[4,512]{1,0:T(4,128)S(1)} %collective-permute-done.9.near_x, f32[2,512]{1,0:T(2,128)S(1)} %get-tuple-element.84.edge_y0, ...), custom_call_target="tpu_custom_call" | custom-call | tf_op jit(solution)/shard_map/turn/pallas_call | solution.py:503
  49.2 1.6 %collective-permute-start.10 = (f32[4,512]{1,0:T(4,128)S(1)}, f32[4,512]{1,0:T(4,128)S(1)}, u32[]{:S(2)}, u32[]{:S(2)}) collective-permute-start(f32[4,512]{1,0:T(4,128)S(1)} %get-tuple-element.93.edge), channel_id=1, source_target_pairs={{0,2},{1,3},{2,0},{3,1},{4,6},{5,7},{6,4},{7,5},{8,10},{9,11},{10,... | collective-permute-start | bytes 24584 | tf_op jit(solution)/shard_map/ppermute | solution.py:514
  50.8 1.6 %between.1 = (f32[4,512]{1,0:T(4,128)S(1)}, bf16[4,128,256]{2,1,0:T(8,128)(2,1)S(1)}, bf16[4,128,256]{2,1,0:T(8,128)(2,1)S(1)}) custom-call(s32[6]{0:T(128)S(1)} %stack.48.meta, f32[4,512]{1,0:T(4,128)S(1)} %get-tuple-element.88.whole, bf16[2,2,512,512]{3,2,1,0:T(8,128)(2,1)S(1)} %get-tuple-element.59.blocks, ...), custom_call_target="tpu_custom_call" | custom-call | tf_op jit(solution)/shard_map/between/pallas_call | solution.py:503
  52.4 0.5 collective-permute-done.10.near
  52.9 1.7 %second_image.1 = (bf16[4,128,256]{2,1,0:T(8,128)(2,1)S(1)}, bf16[4,128,256]{2,1,0:T(8,128)(2,1)S(1)}) custom-call(s32[6]{0:T(128)S(1)} %stack.48.meta, f32[6]{0:T(128)S(1)} %get-tuple-element.60.scalars, bf16[1024,512]{1,0:T(8,128)(2,1)S(1)} %get-tuple-element.97.source, bf16[1024,512]{1,0:T(8,128)(2,1)S(1)} %get-tuple-element.98.receiver, ...), custom_call_target="tpu_custom_call" | custom-call | tf_op jit(solution)/shard_map/second_image/pallas_call | solution.py:503
  54.6 0.1 collective-permute-start.12
  54.7 0.5 collective-permute-start.11
  55.2 1.0 %collective-permute-done.12 = bf16[4,128,256]{2,1,0:T(8,128)(2,1)S(1)} collective-permute-done((bf16[4,128,256]{2,1,0:T(8,128)(2,1)S(1)}, bf16[4,128,256]{2,1,0:T(8,128)(2,1)S(1)}, u32[]{:S(2)}, u32[]{:S(2)}) %collective-permute-start.12) | collective-permute-done | bytes 262176 | tf_op jit(solution)/shard_map/ppermute | solution.py:514
  56.2 0.1 fusion.1
  56.3 0.3 collective-permute-done.11
  56.6 0.1 fusion
  56.7 2.5 %collective-permute-start.13 = (bf16[2,128,256]{2,1,0:T(8,128)(2,1)S(1)}, bf16[2,128,256]{2,1,0:T(8,128)(2,1)S(1)}, u32[]{:S(2)}, u32[]{:S(2)}) collective-permute-start(bf16[2,128,256]{2,1,0:T(8,128)(2,1)S(1)} %get-tuple-element.103), channel_id=1, source_target_pairs={{0,8},{1,9},{2,24},{3,25},{4,12},{5,13},{6,28},{7,29},{8,0},{9,1},... | collective-permute-start | bytes 393224 | tf_op jit(solution)/shard_map/ppermute | solution.py:693
  59.3 0.0 collective-permute-start.14
  59.3 1.9 %collective-permute-start.16 = (bf16[2,128,256]{2,1,0:T(8,128)(2,1)S(1)}, bf16[2,128,256]{2,1,0:T(8,128)(2,1)S(1)}, u32[]{:S(2)}, u32[]{:S(2)}) collective-permute-start(bf16[2,128,256]{2,1,0:T(8,128)(2,1)S(1)} %get-tuple-element.105), channel_id=1, source_target_pairs={{0,2},{1,3},{2,18},{3,19},{4,6},{5,7},{6,22},{7,23},{8,10},{9,11},... | collective-permute-start | bytes 393224 | tf_op jit(solution)/shard_map/ppermute | solution.py:693
  61.2 3.4 %collective-permute-start.15 = (bf16[2,128,256]{2,1,0:T(8,128)(2,1)S(1)}, bf16[2,128,256]{2,1,0:T(8,128)(2,1)S(1)}, u32[]{:S(2)}, u32[]{:S(2)}) collective-permute-start(bf16[2,128,256]{2,1,0:T(8,128)(2,1)S(1)} %get-tuple-element.106), channel_id=1, source_target_pairs={{0,0},{1,1},{2,16},{3,17},{4,4},{5,5},{6,20},{7,21},{8,8},{9,9},{1... | collective-permute-start | bytes 393224 | tf_op jit(solution)/shard_map/ppermute | solution.py:693
  64.6 0.0 collective-permute-done.13
  64.6 1.9 %collective-permute-done.14 = bf16[2,128,256]{2,1,0:T(8,128)(2,1)S(1)} collective-permute-done((bf16[2,128,256]{2,1,0:T(8,128)(2,1)S(1)}, bf16[2,128,256]{2,1,0:T(8,128)(2,1)S(1)}, u32[]{:S(2)}, u32[]{:S(2)}) %collective-permute-start.14) | collective-permute-done | bytes 131104 | tf_op jit(solution)/shard_map/ppermute | solution.py:693
  66.5 0.8 %collective-permute-done.16 = bf16[2,128,256]{2,1,0:T(8,128)(2,1)S(1)} collective-permute-done((bf16[2,128,256]{2,1,0:T(8,128)(2,1)S(1)}, bf16[2,128,256]{2,1,0:T(8,128)(2,1)S(1)}, u32[]{:S(2)}, u32[]{:S(2)}) %collective-permute-start.16) | collective-permute-done | bytes 131104 | tf_op jit(solution)/shard_map/ppermute | solution.py:693
  67.3 1.6 %collective-permute-done.15 = bf16[2,128,256]{2,1,0:T(8,128)(2,1)S(1)} collective-permute-done((bf16[2,128,256]{2,1,0:T(8,128)(2,1)S(1)}, bf16[2,128,256]{2,1,0:T(8,128)(2,1)S(1)}, u32[]{:S(2)}, u32[]{:S(2)}) %collective-permute-start.15) | collective-permute-done | bytes 131104 | tf_op jit(solution)/shard_map/ppermute | solution.py:693
  68.9 0.8 %convert_add_fusion = f32[2,128,256]{2,1,0:T(8,128)} fusion(bf16[2,128,256]{2,1,0:T(8,128)(2,1)S(1)} %collective-permute-done.16, bf16[2,128,256]{2,1,0:T(8,128)(2,1)S(1)} %collective-permute-done.15, bf16[2,128,256]{2,1,0:T(8,128)(2,1)S(1)} %collective-permute-done.14, bf16[2,128,256]{2,1,0:T(8,128)(2,1)S(1)} %collective-permute-done.13), kind=kLoop, calls=%fused_computation.13 | loop fusion | flops 458752 | bytes 786432 | tf_op jit(solution)/shard_map/add | solution.py:693
  (12 shorter events, 0.2 us)
Async XLA Ops:
  0.1 1.2 %copy-start.1 = (f32[2,128,1024]{2,1,0:T(8,128)S(1)}, f32[2,128,1024]{2,1,0:T(8,128)}, u32[]{:S(2)}) copy-start(f32[2,128,1024]{2,1,0:T(8,128)} %slowness.1) | copy-start | bytes 3145732
  1.3 1.2 %copy-start.3 = (bf16[1,2,128,2,1024]{4,3,2,1,0:T(2,128)(2,1)S(1)}, bf16[1,2,128,2,1024]{4,3,2,1,0:T(2,128)(2,1)}, u32[]{:S(2)}) copy-start(bf16[1,2,128,2,1024]{4,3,2,1,0:T(2,128)(2,1)} %field.2) | copy-start | bytes 3145732
  2.5 0.7 copy-start.7
  3.2 4.4 %copy-start.2 = (f32[2,128,1024]{2,1,0:T(8,128)S(1)}, f32[2,128,1024]{2,1,0:T(8,128)}, u32[]{:S(2)}) copy-start(f32[2,128,1024]{2,1,0:T(8,128)} %slowness.1) | copy-start | bytes 3145732
  3.2 4.5 %copy-start.5 = (f32[2,2]{1,0:T(2,128)S(1)}, f32[2,2]{1,0:T(2,128)}, u32[]{:S(2)}) copy-start(f32[2,2]{1,0:T(2,128)} %coupling.1) | copy-start | bytes 52
  5.4 2.3 %collective-permute-start = (bf16[256,1024]{1,0:T(8,128)(2,1)S(1)}, bf16[256,1024]{1,0:T(8,128)(2,1)S(1)}, u32[]{:S(2)}, u32[]{:S(2)}) collective-permute-start(bf16[256,1024]{1,0:T(8,128)(2,1)S(1)} %get-tuple-element.58), channel_id=1, source_target_pairs={{0,1},{1,0},{2,3},{3,2},{4,5},{5,4},{6,7},{7,6},{8,9},{9,8},{10,11... | collective-permute-start | bytes 1572872 | tf_op jit(solution)/shard_map/ppermute | solution.py:514
  5.4 4.6 %copy-start = (bf16[1,2,128,2,1024]{4,3,2,1,0:T(2,128)(2,1)S(1)}, bf16[1,2,128,2,1024]{4,3,2,1,0:T(2,128)(2,1)}, u32[]{:S(2)}) copy-start(bf16[1,2,128,2,1024]{4,3,2,1,0:T(2,128)(2,1)} %field.3) | copy-start | bytes 3145732
  7.6 5.9 %copy-start.4 = (s32[1,1024]{1,0:T(1,128)S(1)}, s32[1,1024]{1,0:T(1,128)}, u32[]{:S(2)}) copy-start(s32[1,1024]{1,0:T(1,128)} %mask.1) | copy-start | bytes 12292
  10.7 2.9 %collective-permute-start.1 = (bf16[128,2,1024]{2,1,0:T(2,128)(2,1)S(1)}, bf16[128,2,1024]{2,1,0:T(2,128)(2,1)S(1)}, u32[]{:S(2)}, u32[]{:S(2)}) collective-permute-start(bf16[128,2,1024]{2,1,0:T(2,128)(2,1)S(1)} %away.1), channel_id=1, source_target_pairs={{0,1},{1,0},{2,3},{3,2},{4,5},{5,4},{6,7},{7,6},{8,9},{9,8},{10,11... | collective-permute-start | bytes 1572872 | tf_op jit(solution)/shard_map/ppermute | solution.py:514
  11.2 2.3 %collective-permute-start.2 = (f32[128,1024]{1,0:T(8,128)S(1)}, f32[128,1024]{1,0:T(8,128)S(1)}, u32[]{:S(2)}, u32[]{:S(2)}) collective-permute-start(f32[128,1024]{1,0:T(8,128)S(1)} %get-tuple-element.65.slow), channel_id=1, source_target_pairs={{0,1},{1,0},{2,3},{3,2},{4,5},{5,4},{6,7},{7,6},{8,9},{9,8},{10,11... | collective-permute-start | bytes 1572872 | tf_op jit(solution)/shard_map/ppermute | solution.py:514
  11.3 14.9 %collective-permute-start.3 = (bf16[512,512]{1,0:T(8,128)(2,1)S(1)}, bf16[512,512]{1,0:T(8,128)(2,1)S(1)}, u32[]{:S(2)}, u32[]{:S(2)}) collective-permute-start(bf16[512,512]{1,0:T(8,128)(2,1)S(1)} %get-tuple-element.66.cross0), channel_id=1, source_target_pairs={{0,2},{1,3},{2,0},{3,1},{4,6},{5,7},{6,4},{7,5},{8,10},{9,11},{10,... | collective-permute-start | bytes 1572872 | tf_op jit(solution)/shard_map/ppermute | solution.py:514
  12.9 20.0 %copy-start.6 = (s32[1,2]{1,0:T(1,128)S(1)}, s32[1,2]{1,0:T(1,128)}, u32[]{:S(2)}) copy-start(s32[1,2]{1,0:T(1,128)} %place.1) | copy-start | bytes 28
  13.0 16.0 %collective-permute-start.4 = (f16[128,512]{1,0:T(8,128)(2,1)S(1)}, f16[128,512]{1,0:T(8,128)(2,1)S(1)}, u32[]{:S(2)}, u32[]{:S(2)}) collective-permute-start(f16[128,512]{1,0:T(8,128)(2,1)S(1)} %get-tuple-element.110), channel_id=1, source_target_pairs={{0,2},{1,3},{2,0},{3,1},{4,6},{5,7},{6,4},{7,5},{8,10},{9,11},{10,... | collective-permute-start | bytes 393224 | tf_op jit(solution)/shard_map/ppermute | solution.py:514
  18.3 10.7 %collective-permute-start.5 = (f32[4,512]{1,0:T(4,128)S(1)}, f32[4,512]{1,0:T(4,128)S(1)}, u32[]{:S(2)}, u32[]{:S(2)}) collective-permute-start(f32[4,512]{1,0:T(4,128)S(1)} %get-tuple-element.70), channel_id=1, source_target_pairs={{0,4},{1,5},{2,6},{3,7},{4,0},{5,1},{6,2},{7,3},{8,12},{9,13},{10,... | collective-permute-start | bytes 24584 | tf_op jit(solution)/shard_map/ppermute | solution.py:514
  20.9 10.3 %collective-permute-start.6 = (f32[4,512]{1,0:T(4,128)S(1)}, f32[4,512]{1,0:T(4,128)S(1)}, u32[]{:S(2)}, u32[]{:S(2)}) collective-permute-start(f32[4,512]{1,0:T(4,128)S(1)} %get-tuple-element.71), channel_id=1, source_target_pairs={{0,6},{1,7},{2,4},{3,5},{4,2},{5,3},{6,0},{7,1},{8,14},{9,15},{10,... | collective-permute-start | bytes 24584 | tf_op jit(solution)/shard_map/ppermute | solution.py:514
  26.2 14.8 %collective-permute-start.8 = (bf16[512,512]{1,0:T(8,128)(2,1)S(1)}, bf16[512,512]{1,0:T(8,128)(2,1)S(1)}, u32[]{:S(2)}, u32[]{:S(2)}) collective-permute-start(bf16[512,512]{1,0:T(8,128)(2,1)S(1)} %get-tuple-element.82), channel_id=1, source_target_pairs={{0,2},{1,3},{2,0},{3,1},{4,6},{5,7},{6,4},{7,5},{8,10},{9,11},{10,... | collective-permute-start | bytes 1572872 | tf_op jit(solution)/shard_map/ppermute | solution.py:514
  31.3 1.6 %collective-permute-start.7 = (f16[2,128,512]{2,1,0:T(8,128)(2,1)S(1)}, f16[2,128,512]{2,1,0:T(8,128)(2,1)S(1)}, u32[]{:S(2)}, u32[]{:S(2)}) collective-permute-start(f16[2,128,512]{2,1,0:T(8,128)(2,1)S(1)} %pad_maximum_fusion), channel_id=1, source_target_pairs={{0,1},{1,0},{2,3},{3,2},{4,5},{5,4},{6,7},{7,6},{8,9},{9,8},{10,11... | collective-permute-start | bytes 786440 | tf_op jit(solution)/shard_map/ppermute | solution.py:514
  43.7 4.8 %collective-permute-start.9 = (f32[4,512]{1,0:T(4,128)S(1)}, f32[4,512]{1,0:T(4,128)S(1)}, u32[]{:S(2)}, u32[]{:S(2)}) collective-permute-start(f32[4,512]{1,0:T(4,128)S(1)} %pad_maximum_fusion.2.edge_x), channel_id=1, source_target_pairs={{0,4},{1,5},{2,6},{3,7},{4,0},{5,1},{6,2},{7,3},{8,12},{9,13},{10,... | collective-permute-start | bytes 24584 | tf_op jit(solution)/shard_map/ppermute | solution.py:514
  49.2 3.7 %collective-permute-start.10 = (f32[4,512]{1,0:T(4,128)S(1)}, f32[4,512]{1,0:T(4,128)S(1)}, u32[]{:S(2)}, u32[]{:S(2)}) collective-permute-start(f32[4,512]{1,0:T(4,128)S(1)} %get-tuple-element.93.edge), channel_id=1, source_target_pairs={{0,2},{1,3},{2,0},{3,1},{4,6},{5,7},{6,4},{7,5},{8,10},{9,11},{10,... | collective-permute-start | bytes 24584 | tf_op jit(solution)/shard_map/ppermute | solution.py:514
  54.6 1.6 %collective-permute-start.12 = (bf16[4,128,256]{2,1,0:T(8,128)(2,1)S(1)}, bf16[4,128,256]{2,1,0:T(8,128)(2,1)S(1)}, u32[]{:S(2)}, u32[]{:S(2)}) collective-permute-start(bf16[4,128,256]{2,1,0:T(8,128)(2,1)S(1)} %get-tuple-element.102), channel_id=1, source_target_pairs={{0,1},{1,0},{2,3},{3,2},{4,5},{5,4},{6,7},{7,6},{8,9},{9,8},{10,11... | collective-permute-start | bytes 786440 | tf_op jit(solution)/shard_map/ppermute | solution.py:514
  54.7 1.9 %collective-permute-start.11 = (bf16[4,128,256]{2,1,0:T(8,128)(2,1)S(1)}, bf16[4,128,256]{2,1,0:T(8,128)(2,1)S(1)}, u32[]{:S(2)}, u32[]{:S(2)}) collective-permute-start(bf16[4,128,256]{2,1,0:T(8,128)(2,1)S(1)} %get-tuple-element.96), channel_id=1, source_target_pairs={{0,1},{1,0},{2,3},{3,2},{4,5},{5,4},{6,7},{7,6},{8,9},{9,8},{10,11... | collective-permute-start | bytes 786440 | tf_op jit(solution)/shard_map/ppermute | solution.py:514
  56.7 7.9 %collective-permute-start.13 = (bf16[2,128,256]{2,1,0:T(8,128)(2,1)S(1)}, bf16[2,128,256]{2,1,0:T(8,128)(2,1)S(1)}, u32[]{:S(2)}, u32[]{:S(2)}) collective-permute-start(bf16[2,128,256]{2,1,0:T(8,128)(2,1)S(1)} %get-tuple-element.103), channel_id=1, source_target_pairs={{0,8},{1,9},{2,24},{3,25},{4,12},{5,13},{6,28},{7,29},{8,0},{9,1},... | collective-permute-start | bytes 393224 | tf_op jit(solution)/shard_map/ppermute | solution.py:693
  59.3 7.3 %collective-permute-start.14 = (bf16[2,128,256]{2,1,0:T(8,128)(2,1)S(1)}, bf16[2,128,256]{2,1,0:T(8,128)(2,1)S(1)}, u32[]{:S(2)}, u32[]{:S(2)}) collective-permute-start(bf16[2,128,256]{2,1,0:T(8,128)(2,1)S(1)} %get-tuple-element.104), channel_id=1, source_target_pairs={{0,10},{1,11},{2,26},{3,27},{4,14},{5,15},{6,30},{7,31},{8,2},{9,3... | collective-permute-start | bytes 393224 | tf_op jit(solution)/shard_map/ppermute | solution.py:693
  59.3 8.1 %collective-permute-start.16 = (bf16[2,128,256]{2,1,0:T(8,128)(2,1)S(1)}, bf16[2,128,256]{2,1,0:T(8,128)(2,1)S(1)}, u32[]{:S(2)}, u32[]{:S(2)}) collective-permute-start(bf16[2,128,256]{2,1,0:T(8,128)(2,1)S(1)} %get-tuple-element.105), channel_id=1, source_target_pairs={{0,2},{1,3},{2,18},{3,19},{4,6},{5,7},{6,22},{7,23},{8,10},{9,11},... | collective-permute-start | bytes 393224 | tf_op jit(solution)/shard_map/ppermute | solution.py:693
  61.2 7.7 %collective-permute-start.15 = (bf16[2,128,256]{2,1,0:T(8,128)(2,1)S(1)}, bf16[2,128,256]{2,1,0:T(8,128)(2,1)S(1)}, u32[]{:S(2)}, u32[]{:S(2)}) collective-permute-start(bf16[2,128,256]{2,1,0:T(8,128)(2,1)S(1)} %get-tuple-element.106), channel_id=1, source_target_pairs={{0,0},{1,1},{2,16},{3,17},{4,4},{5,5},{6,20},{7,21},{8,8},{9,9},{1... | collective-permute-start | bytes 393224 | tf_op jit(solution)/shard_map/ppermute | solution.py:693

commit v5 on v4

--- a/solution.py
+++ b/solution.py
@@ -581,7 +581,7 @@
     pair = shape(BF16, 2 * half, half)
     line = shape(F32, 2, half)
     four = shape(F32, 4, half)
-    far_slow, edge_same, edge_cross = lax.optimization_barrier((far_slow, edge_same, edge_cross))
+    far_slow, edge_same = lax.optimization_barrier((far_slow, edge_same))
     core_slow = move(jnp.stack([own_slow, far_slow]), 1)
     block = shape(F32, half, half)
     sine, cosine, weight = call(

time: 69.9 us -> 69.9 us (level)
  starting transfers between devices: 20 us -> 21 us
  waiting for transfers between devices: 15.1 us -> 14.1 us
    ppermute x13, starting transfers between devices: 12.1 us -> 13.1 us  [move(): return lax.ppermute(array, 'slab', [(i, i ^ k) for i in range(8)])]
    ppermute x13, waiting for transfers between devices: 10.8 us -> 9.74 us  [move(): return lax.ppermute(array, 'slab', [(i, i ^ k) for i in range(8)])]
where the time goes in v5:
time: 69.9 us; the launch traced here: 69.7 us
  Pallas kernels  29.9 us (43%)
  starting transfers between devices  21 us (30%)
  waiting for transfers between devices  14.1 us (20%)
  local copies, waits for them, and re-layouts  3.26 us (5%)
  other arithmetic  1.21 us (2%)
    pallas_call x10, Pallas kernels, call(): pl.pallas_call(body, in_specs=specs, out_specs=[vmem] * len(outs), out_sh...  23.2 us
    ppermute x13, starting transfers between devices, move(): return lax.ppermute(array, 'slab', [(i, i ^ k) for i in range(8)])  13.1 us
    ppermute x13, waiting for transfers between devices, move(): return lax.ppermute(array, 'slab', [(i, i ^ k) for i in range(8)])  9.74 us
    ppermute x4, starting transfers between devices, block_shards(): lax.ppermute(both[kz * 2 + kx], ('shot', 'slab'), route).astype(F32)  7.87 us
    ppermute x4, waiting for transfers between devices, block_shards(): lax.ppermute(both[kz * 2 + kx], ('shot', 'slab'), route).astype(F32)  4.31 us
    unnamed x16, local copies, waits for them, and re-layouts  3.13 us
    pallas_call x1, Pallas kernels, block_shards(): pl.pallas_call(source_kernel, in_specs=[smem] * 3 + [vmem] * 3, out_specs...  2.37 us
    pallas_call x1, Pallas kernels, block_shards(): pl.pallas_call(other_kernel, in_specs=[smem, smem, vmem, vmem], out_specs...  2.15 us
  transfers between devices with their start and end apart: 17, of which 10 were waited for; matrix products, arithmetic and copies ran while one was open for 1% of the time, Pallas kernels for 28%

profile of v5, /device:TPU:4, one launch (start us, length us, event | category | flops | bytes accessed | tf_op | source)
XLA Modules:
  0.0 69.7 jit_solution(6604050533842365820)
XLA Ops:
  0.0 0.1 stack.48.meta
  0.1 1.2 %copy-done.1 = f32[2,128,1024]{2,1,0:T(8,128)S(1)} copy-done((f32[2,128,1024]{2,1,0:T(8,128)S(1)}, f32[2,128,1024]{2,1,0:T(8,128)}, u32[]{:S(2)}) %copy-start.1) | copy-done | bytes 1048600
  1.3 1.2 %copy-done.3 = bf16[1,2,128,2,1024]{4,3,2,1,0:T(2,128)(2,1)S(1)} copy-done((bf16[1,2,128,2,1024]{4,3,2,1,0:T(2,128)(2,1)S(1)}, bf16[1,2,128,2,1024]{4,3,2,1,0:T(2,128)(2,1)}, u32[]{:S(2)}) %copy-start.3) | copy-done | bytes 1048600
  2.5 0.7 copy-done.7
  3.2 2.2 %other.1 = (bf16[256,1024]{1,0:T(8,128)(2,1)S(1)}, bf16[128,2,1024]{2,1,0:T(2,128)(2,1)S(1)}, f32[128,1024]{1,0:T(8,128)S(1)}, f32[2]{0:T(128)S(1)}) custom-call(s32[6]{0:T(128)S(1)} %stack.48.meta, f32[2]{0:T(128)S(1)} %copy-done.7, bf16[1,2,128,2,1024]{4,3,2,1,0:T(2,128)(2,1)S(1)} %copy-done.3, f32[2,128,1024]{2,1,0:T(8,128)S(1)} %copy-done.1), custom_call_target="tpu_custom_call" | custom-call | tf_op jit(solution)/shard_map/other/pallas_call | solution.py:518
  5.4 0.1 collective-permute-start
  5.4 0.0 copy-start
  5.5 2.1 %own.1 = (bf16[256,1024]{1,0:T(8,128)(2,1)S(1)}, bf16[2,2,512,512]{3,2,1,0:T(8,128)(2,1)S(1)}) custom-call(s32[6]{0:T(128)S(1)} %stack.48.meta, f32[2]{0:T(128)S(1)} %get-tuple-element.53.freq, bf16[128,2,1024]{2,1,0:T(2,128)(2,1)S(1)} %get-tuple-element.54.raw, f32[128,1024]{1,0:T(8,128)S(1)} %get-tuple-element.64.slow, bf16[2,2,2,512,512]{4,3,2,1,0:T(8,128)(2,1)} %inverse.1), custom_call_target="tpu_custom_call" | custom-call | tf_op jit(solution)/shard_map/own/pallas_call | solution.py:526
  7.6 0.0 copy-done.2
  7.6 0.0 copy-start.4
  7.7 0.0 collective-permute-done.core
  7.7 0.0 copy-done.5
  7.7 2.4 %slab.1 = (bf16[512,512]{1,0:T(8,128)(2,1)S(1)}, bf16[512,512]{1,0:T(8,128)(2,1)S(1)}, f32[4,512]{1,0:T(4,128)S(1)}, f32[6]{0:T(128)S(1)}) custom-call(s32[6]{0:T(128)S(1)} %stack.48.meta, f32[2]{0:T(128)S(1)} %get-tuple-element.53.freq, f32[2,2]{1,0:T(2,128)S(1)} %copy-done.5, bf16[256,1024]{1,0:T(8,128)(2,1)S(1)} %get-tuple-element.56.own, ...), custom_call_target="tpu_custom_call" | custom-call | tf_op jit(solution)/shard_map/slab/pallas_call | solution.py:537
  10.1 0.0 copy-done
  10.1 0.6 away.1
  10.7 0.5 collective-permute-start.1
  11.2 0.1 collective-permute-start.2
  11.3 1.6 %collective-permute-start.3 = (bf16[512,512]{1,0:T(8,128)(2,1)S(1)}, bf16[512,512]{1,0:T(8,128)(2,1)S(1)}, u32[]{:S(2)}, u32[]{:S(2)}) collective-permute-start(bf16[512,512]{1,0:T(8,128)(2,1)S(1)} %get-tuple-element.65.cross0), channel_id=1, source_target_pairs={{0,2},{1,3},{2,0},{3,1},{4,6},{5,7},{6,4},{7,5},{8,10},{9,11},{10,... | collective-permute-start | bytes 1572872 | tf_op jit(solution)/shard_map/ppermute | solution.py:514
  12.9 0.0 copy-start.6
  12.9 0.1 fusion.11
  13.0 0.5 collective-permute-start.4
  13.5 0.0 collective-permute-done.1.core_raw
  13.5 0.0 collective-permute-done.2.core_slow
  13.5 0.0 copy-done.4
  13.5 4.7 %receiver.1 = (bf16[512,512]{1,0:T(8,128)(2,1)S(1)}, bf16[512,512]{1,0:T(8,128)(2,1)S(1)}, f32[4,512]{1,0:T(4,128)S(1)}, f32[4,512]{1,0:T(4,128)S(1)}) custom-call(s32[6]{0:T(128)S(1)} %stack.48.meta, f32[6]{0:T(128)S(1)} %get-tuple-element.59.scalars, s32[1,1024]{1,0:T(1,128)S(1)} %copy-done.4, bf16[1,2,128,2,1024]{4,3,2,1,0:T(2,128)(2,1)S(1)} %copy-done, ...), custom_call_target="tpu_custom_call" | custom-call | tf_op jit(solution)/shard_map/receiver/pallas_call | solution.py:503
  18.3 2.7 %collective-permute-start.5 = (f32[4,512]{1,0:T(4,128)S(1)}, f32[4,512]{1,0:T(4,128)S(1)}, u32[]{:S(2)}, u32[]{:S(2)}) collective-permute-start(f32[4,512]{1,0:T(4,128)S(1)} %get-tuple-element.69), channel_id=1, source_target_pairs={{0,4},{1,5},{2,6},{3,7},{4,0},{5,1},{6,2},{7,3},{8,12},{9,13},{10,... | collective-permute-start | bytes 24584 | tf_op jit(solution)/shard_map/ppermute | solution.py:514
  20.9 1.4 %collective-permute-start.6 = (f32[4,512]{1,0:T(4,128)S(1)}, f32[4,512]{1,0:T(4,128)S(1)}, u32[]{:S(2)}, u32[]{:S(2)}) collective-permute-start(f32[4,512]{1,0:T(4,128)S(1)} %get-tuple-element.71), channel_id=1, source_target_pairs={{0,6},{1,7},{2,4},{3,5},{4,2},{5,3},{6,0},{7,1},{8,14},{9,15},{10,... | collective-permute-start | bytes 24584 | tf_op jit(solution)/shard_map/ppermute | solution.py:514
  22.3 3.9 %collective-permute-done.3.far = bf16[512,512]{1,0:T(8,128)(2,1)S(1)} collective-permute-done((bf16[512,512]{1,0:T(8,128)(2,1)S(1)}, bf16[512,512]{1,0:T(8,128)(2,1)S(1)}, u32[]{:S(2)}, u32[]{:S(2)}) %collective-permute-start.3) | collective-permute-done | bytes 524320 | tf_op jit(solution)/shard_map/ppermute | solution.py:514
  26.2 1.4 %collective-permute-start.8 = (bf16[512,512]{1,0:T(8,128)(2,1)S(1)}, bf16[512,512]{1,0:T(8,128)(2,1)S(1)}, u32[]{:S(2)}, u32[]{:S(2)}) collective-permute-start(bf16[512,512]{1,0:T(8,128)(2,1)S(1)} %get-tuple-element.80), channel_id=1, source_target_pairs={{0,2},{1,3},{2,0},{3,1},{4,6},{5,7},{6,4},{7,5},{8,10},{9,11},{10,... | collective-permute-start | bytes 1572872 | tf_op jit(solution)/shard_map/ppermute | solution.py:514
  27.6 1.4 %collective-permute-done.4 = f16[128,512]{1,0:T(8,128)(2,1)S(1)} collective-permute-done((f16[128,512]{1,0:T(8,128)(2,1)S(1)}, f16[128,512]{1,0:T(8,128)(2,1)S(1)}, u32[]{:S(2)}, u32[]{:S(2)}) %collective-permute-start.4) | collective-permute-done | bytes 131104 | tf_op jit(solution)/shard_map/ppermute | solution.py:514
  29.0 0.0 collective-permute-done.5
  29.0 0.1 pad_maximum_fusion
  29.1 0.1 collective-permute-start.7
  29.2 2.0 %collective-permute-done.6 = f32[4,512]{1,0:T(4,128)S(1)} collective-permute-done((f32[4,512]{1,0:T(4,128)S(1)}, f32[4,512]{1,0:T(4,128)S(1)}, u32[]{:S(2)}, u32[]{:S(2)}) %collective-permute-start.6) | collective-permute-done | bytes 8224 | tf_op jit(solution)/shard_map/ppermute | solution.py:514
  31.2 0.0 collective-permute-done.7
  31.2 0.1 fusion.9
  31.3 2.1 %phase.1 = (f32[512,512]{1,0:T(8,128)S(1)}, f32[512,512]{1,0:T(8,128)S(1)}, f32[512,512]{1,0:T(8,128)S(1)}) custom-call(s32[6]{0:T(128)S(1)} %stack.48.meta, f32[6]{0:T(128)S(1)} %get-tuple-element.59.scalars, s32[1,2]{1,0:T(1,128)S(1)} %copy-done.6, f32[128,512]{1,0:T(8,128)S(1)} %get-tuple-element.109.own, f32[128,512]{1,0:T(8,128)S(1)} %get-tuple-element.106.core, ...), custom_call_target="tpu_custom_call" | custom-call | tf_op jit(solution)/shard_map/phase/pallas_call | solution.py:503
  33.4 2.6 %column.2 = (bf16[1024,512]{1,0:T(8,128)(2,1)S(1)}, bf16[1024,512]{1,0:T(8,128)(2,1)S(1)}, f32[2,512]{1,0:T(2,128)S(1)}) custom-call(s32[6]{0:T(128)S(1)} %stack.48.meta, f32[6]{0:T(128)S(1)} %get-tuple-element.59.scalars, bf16[512,512]{1,0:T(8,128)(2,1)S(1)} %get-tuple-element.62.same0.near, bf16[512,512]{1,0:T(8,128)(2,1)S(1)} %collective-permute-done.3.far, ...), custom_call_target="tpu_custom_call" | custom-call | tf_op jit(solution)/shard_map/column/pallas_call | solution.py:503
  36.0 3.4 %both.2 = (bf16[1024,512]{1,0:T(8,128)(2,1)S(1)}, f32[2,512]{1,0:T(2,128)S(1)}) custom-call(s32[6]{0:T(128)S(1)} %stack.48.meta, bf16[1024,512]{1,0:T(8,128)(2,1)S(1)} %get-tuple-element.77.shifted, bf16[2,2,512,512]{3,2,1,0:T(8,128)(2,1)S(1)} %get-tuple-element.58.blocks), custom_call_target="tpu_custom_call" | custom-call | tf_op jit(solution)/shard_map/both/pallas_call | solution.py:503
  39.4 0.6 collective-permute-done.8.far
  40.0 2.6 %column.3 = (bf16[1024,512]{1,0:T(8,128)(2,1)S(1)}, bf16[1024,512]{1,0:T(8,128)(2,1)S(1)}, f32[2,512]{1,0:T(2,128)S(1)}) custom-call(s32[6]{0:T(128)S(1)} %stack.48.meta, f32[6]{0:T(128)S(1)} %get-tuple-element.59.scalars, bf16[512,512]{1,0:T(8,128)(2,1)S(1)} %get-tuple-element.79.near, bf16[512,512]{1,0:T(8,128)(2,1)S(1)} %collective-permute-done.8.far, ...), custom_call_target="tpu_custom_call" | custom-call | tf_op jit(solution)/shard_map/column/pallas_call | solution.py:503
  42.6 2.7 %collective-permute-start.9 = (f32[4,512]{1,0:T(4,128)S(1)}, f32[4,512]{1,0:T(4,128)S(1)}, u32[]{:S(2)}, u32[]{:S(2)}) collective-permute-start(f32[4,512]{1,0:T(4,128)S(1)} %pad_maximum_fusion.2.edge_x), channel_id=1, source_target_pairs={{0,4},{1,5},{2,6},{3,7},{4,0},{5,1},{6,2},{7,3},{8,12},{9,13},{10,... | collective-permute-start | bytes 24584 | tf_op jit(solution)/shard_map/ppermute | solution.py:514
  45.3 3.2 %both.3 = (bf16[1024,512]{1,0:T(8,128)(2,1)S(1)}, f32[2,512]{1,0:T(2,128)S(1)}) custom-call(s32[6]{0:T(128)S(1)} %stack.48.meta, bf16[1024,512]{1,0:T(8,128)(2,1)S(1)} %get-tuple-element.83.shifted, bf16[2,2,512,512]{3,2,1,0:T(8,128)(2,1)S(1)} %get-tuple-element.58.blocks), custom_call_target="tpu_custom_call" | custom-call | tf_op jit(solution)/shard_map/both/pallas_call | solution.py:503
  48.4 0.0 collective-permute-done.9.near_x
  48.5 0.7 %turn.1 = (f32[4,512]{1,0:T(4,128)S(1)}, f32[4,512]{1,0:T(4,128)S(1)}) custom-call(s32[6]{0:T(128)S(1)} %stack.48.meta, f32[6]{0:T(128)S(1)} %get-tuple-element.59.scalars, f32[4,512]{1,0:T(4,128)S(1)} %pad_maximum_fusion.2.edge_x, f32[4,512]{1,0:T(4,128)S(1)} %collective-permute-done.9.near_x, f32[2,512]{1,0:T(2,128)S(1)} %get-tuple-element.82.edge_y0, ...), custom_call_target="tpu_custom_call" | custom-call | tf_op jit(solution)/shard_map/turn/pallas_call | solution.py:503
  49.2 1.6 %collective-permute-start.10 = (f32[4,512]{1,0:T(4,128)S(1)}, f32[4,512]{1,0:T(4,128)S(1)}, u32[]{:S(2)}, u32[]{:S(2)}) collective-permute-start(f32[4,512]{1,0:T(4,128)S(1)} %get-tuple-element.91.edge), channel_id=1, source_target_pairs={{0,2},{1,3},{2,0},{3,1},{4,6},{5,7},{6,4},{7,5},{8,10},{9,11},{10,... | collective-permute-start | bytes 24584 | tf_op jit(solution)/shard_map/ppermute | solution.py:514
  50.8 1.6 %between.1 = (f32[4,512]{1,0:T(4,128)S(1)}, bf16[4,128,256]{2,1,0:T(8,128)(2,1)S(1)}, bf16[4,128,256]{2,1,0:T(8,128)(2,1)S(1)}) custom-call(s32[6]{0:T(128)S(1)} %stack.48.meta, f32[4,512]{1,0:T(4,128)S(1)} %get-tuple-element.86.whole, bf16[2,2,512,512]{3,2,1,0:T(8,128)(2,1)S(1)} %get-tuple-element.58.blocks, ...), custom_call_target="tpu_custom_call" | custom-call | tf_op jit(solution)/shard_map/between/pallas_call | solution.py:503
  52.4 0.5 collective-permute-done.10.near
  52.9 1.7 %second_image.1 = (bf16[4,128,256]{2,1,0:T(8,128)(2,1)S(1)}, bf16[4,128,256]{2,1,0:T(8,128)(2,1)S(1)}) custom-call(s32[6]{0:T(128)S(1)} %stack.48.meta, f32[6]{0:T(128)S(1)} %get-tuple-element.59.scalars, bf16[1024,512]{1,0:T(8,128)(2,1)S(1)} %get-tuple-element.95.source, bf16[1024,512]{1,0:T(8,128)(2,1)S(1)} %get-tuple-element.96.receiver, ...), custom_call_target="tpu_custom_call" | custom-call | tf_op jit(solution)/shard_map/second_image/pallas_call | solution.py:503
  54.6 0.1 collective-permute-start.12
  54.7 0.5 collective-permute-start.11
  55.2 1.0 %collective-permute-done.12 = bf16[4,128,256]{2,1,0:T(8,128)(2,1)S(1)} collective-permute-done((bf16[4,128,256]{2,1,0:T(8,128)(2,1)S(1)}, bf16[4,128,256]{2,1,0:T(8,128)(2,1)S(1)}, u32[]{:S(2)}, u32[]{:S(2)}) %collective-permute-start.12) | collective-permute-done | bytes 262176 | tf_op jit(solution)/shard_map/ppermute | solution.py:514
  56.2 0.1 fusion.1
  56.3 0.3 collective-permute-done.11
  56.6 0.1 fusion
  56.7 2.5 %collective-permute-start.13 = (bf16[2,128,256]{2,1,0:T(8,128)(2,1)S(1)}, bf16[2,128,256]{2,1,0:T(8,128)(2,1)S(1)}, u32[]{:S(2)}, u32[]{:S(2)}) collective-permute-start(bf16[2,128,256]{2,1,0:T(8,128)(2,1)S(1)} %get-tuple-element.101), channel_id=1, source_target_pairs={{0,8},{1,9},{2,24},{3,25},{4,12},{5,13},{6,28},{7,29},{8,0},{9,1},... | collective-permute-start | bytes 393224 | tf_op jit(solution)/shard_map/ppermute | solution.py:693
  59.3 0.0 collective-permute-start.14
  59.3 1.9 %collective-permute-start.16 = (bf16[2,128,256]{2,1,0:T(8,128)(2,1)S(1)}, bf16[2,128,256]{2,1,0:T(8,128)(2,1)S(1)}, u32[]{:S(2)}, u32[]{:S(2)}) collective-permute-start(bf16[2,128,256]{2,1,0:T(8,128)(2,1)S(1)} %get-tuple-element.103), channel_id=1, source_target_pairs={{0,2},{1,3},{2,18},{3,19},{4,6},{5,7},{6,22},{7,23},{8,10},{9,11},... | collective-permute-start | bytes 393224 | tf_op jit(solution)/shard_map/ppermute | solution.py:693
  61.2 3.4 %collective-permute-start.15 = (bf16[2,128,256]{2,1,0:T(8,128)(2,1)S(1)}, bf16[2,128,256]{2,1,0:T(8,128)(2,1)S(1)}, u32[]{:S(2)}, u32[]{:S(2)}) collective-permute-start(bf16[2,128,256]{2,1,0:T(8,128)(2,1)S(1)} %get-tuple-element.104), channel_id=1, source_target_pairs={{0,0},{1,1},{2,16},{3,17},{4,4},{5,5},{6,20},{7,21},{8,8},{9,9},{1... | collective-permute-start | bytes 393224 | tf_op jit(solution)/shard_map/ppermute | solution.py:693
  64.6 0.0 collective-permute-done.13
  64.6 1.9 %collective-permute-done.14 = bf16[2,128,256]{2,1,0:T(8,128)(2,1)S(1)} collective-permute-done((bf16[2,128,256]{2,1,0:T(8,128)(2,1)S(1)}, bf16[2,128,256]{2,1,0:T(8,128)(2,1)S(1)}, u32[]{:S(2)}, u32[]{:S(2)}) %collective-permute-start.14) | collective-permute-done | bytes 131104 | tf_op jit(solution)/shard_map/ppermute | solution.py:693
  66.5 0.8 %collective-permute-done.16 = bf16[2,128,256]{2,1,0:T(8,128)(2,1)S(1)} collective-permute-done((bf16[2,128,256]{2,1,0:T(8,128)(2,1)S(1)}, bf16[2,128,256]{2,1,0:T(8,128)(2,1)S(1)}, u32[]{:S(2)}, u32[]{:S(2)}) %collective-permute-start.16) | collective-permute-done | bytes 131104 | tf_op jit(solution)/shard_map/ppermute | solution.py:693
  67.3 1.6 %collective-permute-done.15 = bf16[2,128,256]{2,1,0:T(8,128)(2,1)S(1)} collective-permute-done((bf16[2,128,256]{2,1,0:T(8,128)(2,1)S(1)}, bf16[2,128,256]{2,1,0:T(8,128)(2,1)S(1)}, u32[]{:S(2)}, u32[]{:S(2)}) %collective-permute-start.15) | collective-permute-done | bytes 131104 | tf_op jit(solution)/shard_map/ppermute | solution.py:693
  68.9 0.8 %convert_add_fusion = f32[2,128,256]{2,1,0:T(8,128)} fusion(bf16[2,128,256]{2,1,0:T(8,128)(2,1)S(1)} %collective-permute-done.16, bf16[2,128,256]{2,1,0:T(8,128)(2,1)S(1)} %collective-permute-done.15, bf16[2,128,256]{2,1,0:T(8,128)(2,1)S(1)} %collective-permute-done.14, bf16[2,128,256]{2,1,0:T(8,128)(2,1)S(1)} %collective-permute-done.13), kind=kLoop, calls=%fused_computation.13 | loop fusion | flops 458752 | bytes 786432 | tf_op jit(solution)/shard_map/add | solution.py:693
  (13 shorter events, 0.2 us)
Async XLA Ops:
  0.1 1.2 %copy-start.1 = (f32[2,128,1024]{2,1,0:T(8,128)S(1)}, f32[2,128,1024]{2,1,0:T(8,128)}, u32[]{:S(2)}) copy-start(f32[2,128,1024]{2,1,0:T(8,128)} %slowness.1) | copy-start | bytes 3145732
  1.3 1.2 %copy-start.3 = (bf16[1,2,128,2,1024]{4,3,2,1,0:T(2,128)(2,1)S(1)}, bf16[1,2,128,2,1024]{4,3,2,1,0:T(2,128)(2,1)}, u32[]{:S(2)}) copy-start(bf16[1,2,128,2,1024]{4,3,2,1,0:T(2,128)(2,1)} %field.2) | copy-start | bytes 3145732
  2.5 0.7 copy-start.7
  3.2 4.4 %copy-start.2 = (f32[2,128,1024]{2,1,0:T(8,128)S(1)}, f32[2,128,1024]{2,1,0:T(8,128)}, u32[]{:S(2)}) copy-start(f32[2,128,1024]{2,1,0:T(8,128)} %slowness.1) | copy-start | bytes 3145732
  3.2 4.5 %copy-start.5 = (f32[2,2]{1,0:T(2,128)S(1)}, f32[2,2]{1,0:T(2,128)}, u32[]{:S(2)}) copy-start(f32[2,2]{1,0:T(2,128)} %coupling.1) | copy-start | bytes 52
  5.4 2.3 %collective-permute-start = (bf16[256,1024]{1,0:T(8,128)(2,1)S(1)}, bf16[256,1024]{1,0:T(8,128)(2,1)S(1)}, u32[]{:S(2)}, u32[]{:S(2)}) collective-permute-start(bf16[256,1024]{1,0:T(8,128)(2,1)S(1)} %get-tuple-element.57), channel_id=1, source_target_pairs={{0,1},{1,0},{2,3},{3,2},{4,5},{5,4},{6,7},{7,6},{8,9},{9,8},{10,11... | collective-permute-start | bytes 1572872 | tf_op jit(solution)/shard_map/ppermute | solution.py:514
  5.4 4.6 %copy-start = (bf16[1,2,128,2,1024]{4,3,2,1,0:T(2,128)(2,1)S(1)}, bf16[1,2,128,2,1024]{4,3,2,1,0:T(2,128)(2,1)}, u32[]{:S(2)}) copy-start(bf16[1,2,128,2,1024]{4,3,2,1,0:T(2,128)(2,1)} %field.3) | copy-start | bytes 3145732
  7.6 5.9 %copy-start.4 = (s32[1,1024]{1,0:T(1,128)S(1)}, s32[1,1024]{1,0:T(1,128)}, u32[]{:S(2)}) copy-start(s32[1,1024]{1,0:T(1,128)} %mask.1) | copy-start | bytes 12292
  10.7 2.9 %collective-permute-start.1 = (bf16[128,2,1024]{2,1,0:T(2,128)(2,1)S(1)}, bf16[128,2,1024]{2,1,0:T(2,128)(2,1)S(1)}, u32[]{:S(2)}, u32[]{:S(2)}) collective-permute-start(bf16[128,2,1024]{2,1,0:T(2,128)(2,1)S(1)} %away.1), channel_id=1, source_target_pairs={{0,1},{1,0},{2,3},{3,2},{4,5},{5,4},{6,7},{7,6},{8,9},{9,8},{10,11... | collective-permute-start | bytes 1572872 | tf_op jit(solution)/shard_map/ppermute | solution.py:514
  11.2 2.3 %collective-permute-start.2 = (f32[128,1024]{1,0:T(8,128)S(1)}, f32[128,1024]{1,0:T(8,128)S(1)}, u32[]{:S(2)}, u32[]{:S(2)}) collective-permute-start(f32[128,1024]{1,0:T(8,128)S(1)} %get-tuple-element.64.slow), channel_id=1, source_target_pairs={{0,1},{1,0},{2,3},{3,2},{4,5},{5,4},{6,7},{7,6},{8,9},{9,8},{10,11... | collective-permute-start | bytes 1572872 | tf_op jit(solution)/shard_map/ppermute | solution.py:514
  11.3 14.9 %collective-permute-start.3 = (bf16[512,512]{1,0:T(8,128)(2,1)S(1)}, bf16[512,512]{1,0:T(8,128)(2,1)S(1)}, u32[]{:S(2)}, u32[]{:S(2)}) collective-permute-start(bf16[512,512]{1,0:T(8,128)(2,1)S(1)} %get-tuple-element.65.cross0), channel_id=1, source_target_pairs={{0,2},{1,3},{2,0},{3,1},{4,6},{5,7},{6,4},{7,5},{8,10},{9,11},{10,... | collective-permute-start | bytes 1572872 | tf_op jit(solution)/shard_map/ppermute | solution.py:514
  12.9 18.4 %copy-start.6 = (s32[1,2]{1,0:T(1,128)S(1)}, s32[1,2]{1,0:T(1,128)}, u32[]{:S(2)}) copy-start(s32[1,2]{1,0:T(1,128)} %place.1) | copy-start | bytes 28
  13.0 16.0 %collective-permute-start.4 = (f16[128,512]{1,0:T(8,128)(2,1)S(1)}, f16[128,512]{1,0:T(8,128)(2,1)S(1)}, u32[]{:S(2)}, u32[]{:S(2)}) collective-permute-start(f16[128,512]{1,0:T(8,128)(2,1)S(1)} %get-tuple-element.108), channel_id=1, source_target_pairs={{0,2},{1,3},{2,0},{3,1},{4,6},{5,7},{6,4},{7,5},{8,10},{9,11},{10,... | collective-permute-start | bytes 393224 | tf_op jit(solution)/shard_map/ppermute | solution.py:514
  18.3 10.7 %collective-permute-start.5 = (f32[4,512]{1,0:T(4,128)S(1)}, f32[4,512]{1,0:T(4,128)S(1)}, u32[]{:S(2)}, u32[]{:S(2)}) collective-permute-start(f32[4,512]{1,0:T(4,128)S(1)} %get-tuple-element.69), channel_id=1, source_target_pairs={{0,4},{1,5},{2,6},{3,7},{4,0},{5,1},{6,2},{7,3},{8,12},{9,13},{10,... | collective-permute-start | bytes 24584 | tf_op jit(solution)/shard_map/ppermute | solution.py:514
  20.9 10.3 %collective-permute-start.6 = (f32[4,512]{1,0:T(4,128)S(1)}, f32[4,512]{1,0:T(4,128)S(1)}, u32[]{:S(2)}, u32[]{:S(2)}) collective-permute-start(f32[4,512]{1,0:T(4,128)S(1)} %get-tuple-element.71), channel_id=1, source_target_pairs={{0,6},{1,7},{2,4},{3,5},{4,2},{5,3},{6,0},{7,1},{8,14},{9,15},{10,... | collective-permute-start | bytes 24584 | tf_op jit(solution)/shard_map/ppermute | solution.py:514
  26.2 13.8 %collective-permute-start.8 = (bf16[512,512]{1,0:T(8,128)(2,1)S(1)}, bf16[512,512]{1,0:T(8,128)(2,1)S(1)}, u32[]{:S(2)}, u32[]{:S(2)}) collective-permute-start(bf16[512,512]{1,0:T(8,128)(2,1)S(1)} %get-tuple-element.80), channel_id=1, source_target_pairs={{0,2},{1,3},{2,0},{3,1},{4,6},{5,7},{6,4},{7,5},{8,10},{9,11},{10,... | collective-permute-start | bytes 1572872 | tf_op jit(solution)/shard_map/ppermute | solution.py:514
  29.1 2.1 %collective-permute-start.7 = (f16[2,128,512]{2,1,0:T(8,128)(2,1)S(1)}, f16[2,128,512]{2,1,0:T(8,128)(2,1)S(1)}, u32[]{:S(2)}, u32[]{:S(2)}) collective-permute-start(f16[2,128,512]{2,1,0:T(8,128)(2,1)S(1)} %pad_maximum_fusion), channel_id=1, source_target_pairs={{0,1},{1,0},{2,3},{3,2},{4,5},{5,4},{6,7},{7,6},{8,9},{9,8},{10,11... | collective-permute-start | bytes 786440 | tf_op jit(solution)/shard_map/ppermute | solution.py:514
  42.6 5.8 %collective-permute-start.9 = (f32[4,512]{1,0:T(4,128)S(1)}, f32[4,512]{1,0:T(4,128)S(1)}, u32[]{:S(2)}, u32[]{:S(2)}) collective-permute-start(f32[4,512]{1,0:T(4,128)S(1)} %pad_maximum_fusion.2.edge_x), channel_id=1, source_target_pairs={{0,4},{1,5},{2,6},{3,7},{4,0},{5,1},{6,2},{7,3},{8,12},{9,13},{10,... | collective-permute-start | bytes 24584 | tf_op jit(solution)/shard_map/ppermute | solution.py:514
  49.2 3.7 %collective-permute-start.10 = (f32[4,512]{1,0:T(4,128)S(1)}, f32[4,512]{1,0:T(4,128)S(1)}, u32[]{:S(2)}, u32[]{:S(2)}) collective-permute-start(f32[4,512]{1,0:T(4,128)S(1)} %get-tuple-element.91.edge), channel_id=1, source_target_pairs={{0,2},{1,3},{2,0},{3,1},{4,6},{5,7},{6,4},{7,5},{8,10},{9,11},{10,... | collective-permute-start | bytes 24584 | tf_op jit(solution)/shard_map/ppermute | solution.py:514
  54.6 1.6 %collective-permute-start.12 = (bf16[4,128,256]{2,1,0:T(8,128)(2,1)S(1)}, bf16[4,128,256]{2,1,0:T(8,128)(2,1)S(1)}, u32[]{:S(2)}, u32[]{:S(2)}) collective-permute-start(bf16[4,128,256]{2,1,0:T(8,128)(2,1)S(1)} %get-tuple-element.100), channel_id=1, source_target_pairs={{0,1},{1,0},{2,3},{3,2},{4,5},{5,4},{6,7},{7,6},{8,9},{9,8},{10,11... | collective-permute-start | bytes 786440 | tf_op jit(solution)/shard_map/ppermute | solution.py:514
  54.7 1.9 %collective-permute-start.11 = (bf16[4,128,256]{2,1,0:T(8,128)(2,1)S(1)}, bf16[4,128,256]{2,1,0:T(8,128)(2,1)S(1)}, u32[]{:S(2)}, u32[]{:S(2)}) collective-permute-start(bf16[4,128,256]{2,1,0:T(8,128)(2,1)S(1)} %get-tuple-element.94), channel_id=1, source_target_pairs={{0,1},{1,0},{2,3},{3,2},{4,5},{5,4},{6,7},{7,6},{8,9},{9,8},{10,11... | collective-permute-start | bytes 786440 | tf_op jit(solution)/shard_map/ppermute | solution.py:514
  56.7 7.9 %collective-permute-start.13 = (bf16[2,128,256]{2,1,0:T(8,128)(2,1)S(1)}, bf16[2,128,256]{2,1,0:T(8,128)(2,1)S(1)}, u32[]{:S(2)}, u32[]{:S(2)}) collective-permute-start(bf16[2,128,256]{2,1,0:T(8,128)(2,1)S(1)} %get-tuple-element.101), channel_id=1, source_target_pairs={{0,8},{1,9},{2,24},{3,25},{4,12},{5,13},{6,28},{7,29},{8,0},{9,1},... | collective-permute-start | bytes 393224 | tf_op jit(solution)/shard_map/ppermute | solution.py:693
  59.3 7.3 %collective-permute-start.14 = (bf16[2,128,256]{2,1,0:T(8,128)(2,1)S(1)}, bf16[2,128,256]{2,1,0:T(8,128)(2,1)S(1)}, u32[]{:S(2)}, u32[]{:S(2)}) collective-permute-start(bf16[2,128,256]{2,1,0:T(8,128)(2,1)S(1)} %get-tuple-element.102), channel_id=1, source_target_pairs={{0,10},{1,11},{2,26},{3,27},{4,14},{5,15},{6,30},{7,31},{8,2},{9,3... | collective-permute-start | bytes 393224 | tf_op jit(solution)/shard_map/ppermute | solution.py:693
  59.3 8.1 %collective-permute-start.16 = (bf16[2,128,256]{2,1,0:T(8,128)(2,1)S(1)}, bf16[2,128,256]{2,1,0:T(8,128)(2,1)S(1)}, u32[]{:S(2)}, u32[]{:S(2)}) collective-permute-start(bf16[2,128,256]{2,1,0:T(8,128)(2,1)S(1)} %get-tuple-element.103), channel_id=1, source_target_pairs={{0,2},{1,3},{2,18},{3,19},{4,6},{5,7},{6,22},{7,23},{8,10},{9,11},... | collective-permute-start | bytes 393224 | tf_op jit(solution)/shard_map/ppermute | solution.py:693
  61.2 7.7 %collective-permute-start.15 = (bf16[2,128,256]{2,1,0:T(8,128)(2,1)S(1)}, bf16[2,128,256]{2,1,0:T(8,128)(2,1)S(1)}, u32[]{:S(2)}, u32[]{:S(2)}) collective-permute-start(bf16[2,128,256]{2,1,0:T(8,128)(2,1)S(1)} %get-tuple-element.104), channel_id=1, source_target_pairs={{0,0},{1,1},{2,16},{3,17},{4,4},{5,5},{6,20},{7,21},{8,8},{9,9},{1... | collective-permute-start | bytes 393224 | tf_op jit(solution)/shard_map/ppermute | solution.py:693

commit v6 on v4

--- a/solution.py
+++ b/solution.py
@@ -395,7 +395,7 @@
             col = pl.multiple_of((meta[5] ^ kx) * cols, cols)
             for other, ref in ((0, keep), (1, send)):
                 row = pl.multiple_of(((meta[4] ^ kz) * 2 + (meta[0] ^ other)) * rows, rows)
-                ref[kz * 2 + kx] = image[pl.ds(row, rows), pl.ds(col, cols)].astype(BF16)
+                ref[kz * 2 + kx] = image[pl.ds(row, rows), pl.ds(col, cols)]
 
 
 def pick_end(ends, block):
@@ -440,7 +440,7 @@
     half = source.shape[1]
     sr, si = source[:half].astype(F32), source[half:].astype(F32)
     rr, ri = receiver[:half].astype(F32), receiver[half:].astype(F32)
-    image[...] = (sr * ri + si * rr) * weight[...]
+    image[...] = ((sr * ri + si * rr) * weight[...]).astype(BF16)
     image_pieces(meta, image, keep, send)
 
 
@@ -478,7 +478,7 @@
             )
         )
     (sr, si), (rr, ri) = fields
-    image[...] = (sr * ri + si * rr) * weight[...]
+    image[...] = ((sr * ri + si * rr) * weight[...]).astype(BF16)
     image_pieces(meta, image, keep, send)
 
 
@@ -644,7 +644,7 @@
     )
     near_y = move(edge, 2)
     cut = shape(BF16, 4, rows, half // 2)
-    scratch = [VMEM((half, half), F32)]
+    scratch = [VMEM((half, half), BF16)]
     rows_y, keep0, send0 = call(
         between_kernel,
         "between",

time: 69.9 us -> 69.9 us (level)
  no operation moved by 1% of the time
where the time goes in v6:
time: 69.9 us; the launch traced here: 69.7 us
  Pallas kernels  29.9 us (43%)
  starting transfers between devices  20 us (29%)
  waiting for transfers between devices  15.1 us (22%)
  local copies, waits for them, and re-layouts  3.26 us (5%)
  other arithmetic  1.21 us (2%)
    pallas_call x10, Pallas kernels, call(): pl.pallas_call(body, in_specs=specs, out_specs=[vmem] * len(outs), out_sh...  23.2 us
    ppermute x13, starting transfers between devices, move(): return lax.ppermute(array, 'slab', [(i, i ^ k) for i in range(8)])  12.1 us
    ppermute x13, waiting for transfers between devices, move(): return lax.ppermute(array, 'slab', [(i, i ^ k) for i in range(8)])  10.8 us
    ppermute x4, starting transfers between devices, block_shards(): lax.ppermute(both[kz * 2 + kx], ('shot', 'slab'), route).astype(F32)  7.87 us
    ppermute x4, waiting for transfers between devices, block_shards(): lax.ppermute(both[kz * 2 + kx], ('shot', 'slab'), route).astype(F32)  4.31 us
    unnamed x16, local copies, waits for them, and re-layouts  3.13 us
    pallas_call x1, Pallas kernels, block_shards(): pl.pallas_call(source_kernel, in_specs=[smem] * 3 + [vmem] * 3, out_specs...  2.37 us
    pallas_call x1, Pallas kernels, block_shards(): pl.pallas_call(other_kernel, in_specs=[smem, smem, vmem, vmem], out_specs...  2.15 us
  transfers between devices with their start and end apart: 17, of which 10 were waited for; matrix products, arithmetic and copies ran while one was open for 1% of the time, Pallas kernels for 28%

profile of v6, /device:TPU:4, one launch (start us, length us, event | category | flops | bytes accessed | tf_op | source)
XLA Modules:
  0.0 69.7 jit_solution(5540340437885216050)
XLA Ops:
  0.0 0.1 stack.48.meta
  0.1 1.2 %copy-done.1 = f32[2,128,1024]{2,1,0:T(8,128)S(1)} copy-done((f32[2,128,1024]{2,1,0:T(8,128)S(1)}, f32[2,128,1024]{2,1,0:T(8,128)}, u32[]{:S(2)}) %copy-start.1) | copy-done | bytes 1048600
  1.3 1.2 %copy-done.3 = bf16[1,2,128,2,1024]{4,3,2,1,0:T(2,128)(2,1)S(1)} copy-done((bf16[1,2,128,2,1024]{4,3,2,1,0:T(2,128)(2,1)S(1)}, bf16[1,2,128,2,1024]{4,3,2,1,0:T(2,128)(2,1)}, u32[]{:S(2)}) %copy-start.3) | copy-done | bytes 1048600
  2.5 0.7 copy-done.7
  3.2 2.2 %other.1 = (bf16[256,1024]{1,0:T(8,128)(2,1)S(1)}, bf16[128,2,1024]{2,1,0:T(2,128)(2,1)S(1)}, f32[128,1024]{1,0:T(8,128)S(1)}, f32[2]{0:T(128)S(1)}) custom-call(s32[6]{0:T(128)S(1)} %stack.48.meta, f32[2]{0:T(128)S(1)} %copy-done.7, bf16[1,2,128,2,1024]{4,3,2,1,0:T(2,128)(2,1)S(1)} %copy-done.3, f32[2,128,1024]{2,1,0:T(8,128)S(1)} %copy-done.1), custom_call_target="tpu_custom_call" | custom-call | tf_op jit(solution)/shard_map/other/pallas_call | solution.py:518
  5.4 0.1 collective-permute-start
  5.4 0.0 copy-start
  5.5 2.1 %own.1 = (bf16[256,1024]{1,0:T(8,128)(2,1)S(1)}, bf16[2,2,512,512]{3,2,1,0:T(8,128)(2,1)S(1)}) custom-call(s32[6]{0:T(128)S(1)} %stack.48.meta, f32[2]{0:T(128)S(1)} %get-tuple-element.54.freq, bf16[128,2,1024]{2,1,0:T(2,128)(2,1)S(1)} %get-tuple-element.55.raw, f32[128,1024]{1,0:T(8,128)S(1)} %get-tuple-element.65.slow, bf16[2,2,2,512,512]{4,3,2,1,0:T(8,128)(2,1)} %inverse.1), custom_call_target="tpu_custom_call" | custom-call | tf_op jit(solution)/shard_map/own/pallas_call | solution.py:526
  7.6 0.0 copy-done.2
  7.6 0.0 copy-start.4
  7.7 0.0 collective-permute-done.core
  7.7 0.0 copy-done.5
  7.7 2.4 %slab.1 = (bf16[512,512]{1,0:T(8,128)(2,1)S(1)}, bf16[512,512]{1,0:T(8,128)(2,1)S(1)}, f32[4,512]{1,0:T(4,128)S(1)}, f32[6]{0:T(128)S(1)}) custom-call(s32[6]{0:T(128)S(1)} %stack.48.meta, f32[2]{0:T(128)S(1)} %get-tuple-element.54.freq, f32[2,2]{1,0:T(2,128)S(1)} %copy-done.5, bf16[256,1024]{1,0:T(8,128)(2,1)S(1)} %get-tuple-element.57.own, ...), custom_call_target="tpu_custom_call" | custom-call | tf_op jit(solution)/shard_map/slab/pallas_call | solution.py:537
  10.1 0.0 copy-done
  10.1 0.6 away.1
  10.7 0.5 collective-permute-start.1
  11.2 0.1 collective-permute-start.2
  11.3 1.6 %collective-permute-start.3 = (bf16[512,512]{1,0:T(8,128)(2,1)S(1)}, bf16[512,512]{1,0:T(8,128)(2,1)S(1)}, u32[]{:S(2)}, u32[]{:S(2)}) collective-permute-start(bf16[512,512]{1,0:T(8,128)(2,1)S(1)} %get-tuple-element.66.cross0), channel_id=1, source_target_pairs={{0,2},{1,3},{2,0},{3,1},{4,6},{5,7},{6,4},{7,5},{8,10},{9,11},{10,... | collective-permute-start | bytes 1572872 | tf_op jit(solution)/shard_map/ppermute | solution.py:514
  12.9 0.0 copy-start.6
  12.9 0.1 fusion.11
  13.0 0.5 collective-permute-start.4
  13.5 0.0 collective-permute-done.1.core_raw
  13.5 0.0 collective-permute-done.2.core_slow
  13.5 4.7 %receiver.1 = (bf16[512,512]{1,0:T(8,128)(2,1)S(1)}, bf16[512,512]{1,0:T(8,128)(2,1)S(1)}, f32[4,512]{1,0:T(4,128)S(1)}, f32[4,512]{1,0:T(4,128)S(1)}) custom-call(s32[6]{0:T(128)S(1)} %stack.48.meta, f32[6]{0:T(128)S(1)} %get-tuple-element.60.scalars, s32[1,1024]{1,0:T(1,128)S(1)} %copy-done.4, bf16[1,2,128,2,1024]{4,3,2,1,0:T(2,128)(2,1)S(1)} %copy-done, ...), custom_call_target="tpu_custom_call" | custom-call | tf_op jit(solution)/shard_map/receiver/pallas_call | solution.py:503
  18.3 2.7 %collective-permute-start.5 = (f32[4,512]{1,0:T(4,128)S(1)}, f32[4,512]{1,0:T(4,128)S(1)}, u32[]{:S(2)}, u32[]{:S(2)}) collective-permute-start(f32[4,512]{1,0:T(4,128)S(1)} %get-tuple-element.70), channel_id=1, source_target_pairs={{0,4},{1,5},{2,6},{3,7},{4,0},{5,1},{6,2},{7,3},{8,12},{9,13},{10,... | collective-permute-start | bytes 24584 | tf_op jit(solution)/shard_map/ppermute | solution.py:514
  20.9 1.4 %collective-permute-start.6 = (f32[4,512]{1,0:T(4,128)S(1)}, f32[4,512]{1,0:T(4,128)S(1)}, u32[]{:S(2)}, u32[]{:S(2)}) collective-permute-start(f32[4,512]{1,0:T(4,128)S(1)} %get-tuple-element.71), channel_id=1, source_target_pairs={{0,6},{1,7},{2,4},{3,5},{4,2},{5,3},{6,0},{7,1},{8,14},{9,15},{10,... | collective-permute-start | bytes 24584 | tf_op jit(solution)/shard_map/ppermute | solution.py:514
  22.3 3.9 %collective-permute-done.3.far = bf16[512,512]{1,0:T(8,128)(2,1)S(1)} collective-permute-done((bf16[512,512]{1,0:T(8,128)(2,1)S(1)}, bf16[512,512]{1,0:T(8,128)(2,1)S(1)}, u32[]{:S(2)}, u32[]{:S(2)}) %collective-permute-start.3) | collective-permute-done | bytes 524320 | tf_op jit(solution)/shard_map/ppermute | solution.py:514
  26.2 1.4 %collective-permute-start.8 = (bf16[512,512]{1,0:T(8,128)(2,1)S(1)}, bf16[512,512]{1,0:T(8,128)(2,1)S(1)}, u32[]{:S(2)}, u32[]{:S(2)}) collective-permute-start(bf16[512,512]{1,0:T(8,128)(2,1)S(1)} %get-tuple-element.82), channel_id=1, source_target_pairs={{0,2},{1,3},{2,0},{3,1},{4,6},{5,7},{6,4},{7,5},{8,10},{9,11},{10,... | collective-permute-start | bytes 1572872 | tf_op jit(solution)/shard_map/ppermute | solution.py:514
  27.6 1.4 %collective-permute-done.4 = f16[128,512]{1,0:T(8,128)(2,1)S(1)} collective-permute-done((f16[128,512]{1,0:T(8,128)(2,1)S(1)}, f16[128,512]{1,0:T(8,128)(2,1)S(1)}, u32[]{:S(2)}, u32[]{:S(2)}) %collective-permute-start.4) | collective-permute-done | bytes 131104 | tf_op jit(solution)/shard_map/ppermute | solution.py:514
  29.0 0.0 collective-permute-done.5
  29.0 2.2 %collective-permute-done.6 = f32[4,512]{1,0:T(4,128)S(1)} collective-permute-done((f32[4,512]{1,0:T(4,128)S(1)}, f32[4,512]{1,0:T(4,128)S(1)}, u32[]{:S(2)}, u32[]{:S(2)}) %collective-permute-start.6) | collective-permute-done | bytes 8224 | tf_op jit(solution)/shard_map/ppermute | solution.py:514
  31.2 0.1 pad_maximum_fusion
  31.3 0.1 collective-permute-start.7
  31.4 1.5 %collective-permute-done.7 = f16[2,128,512]{2,1,0:T(8,128)(2,1)S(1)} collective-permute-done((f16[2,128,512]{2,1,0:T(8,128)(2,1)S(1)}, f16[2,128,512]{2,1,0:T(8,128)(2,1)S(1)}, u32[]{:S(2)}, u32[]{:S(2)}) %collective-permute-start.7) | collective-permute-done | bytes 262176 | tf_op jit(solution)/shard_map/ppermute | solution.py:514
  32.9 0.1 fusion.9
  32.9 0.0 copy-done.6
  32.9 2.1 %phase.1 = (f32[512,512]{1,0:T(8,128)S(1)}, f32[512,512]{1,0:T(8,128)S(1)}, f32[512,512]{1,0:T(8,128)S(1)}) custom-call(s32[6]{0:T(128)S(1)} %stack.48.meta, f32[6]{0:T(128)S(1)} %get-tuple-element.60.scalars, s32[1,2]{1,0:T(1,128)S(1)} %copy-done.6, f32[128,512]{1,0:T(8,128)S(1)} %get-tuple-element.111.own, f32[128,512]{1,0:T(8,128)S(1)} %get-tuple-element.108.core, ...), custom_call_target="tpu_custom_call" | custom-call | tf_op jit(solution)/shard_map/phase/pallas_call | solution.py:503
  35.0 2.6 %column.2 = (bf16[1024,512]{1,0:T(8,128)(2,1)S(1)}, bf16[1024,512]{1,0:T(8,128)(2,1)S(1)}, f32[2,512]{1,0:T(2,128)S(1)}) custom-call(s32[6]{0:T(128)S(1)} %stack.48.meta, f32[6]{0:T(128)S(1)} %get-tuple-element.60.scalars, bf16[512,512]{1,0:T(8,128)(2,1)S(1)} %get-tuple-element.63.same0.near, bf16[512,512]{1,0:T(8,128)(2,1)S(1)} %collective-permute-done.3.far, ...), custom_call_target="tpu_custom_call" | custom-call | tf_op jit(solution)/shard_map/column/pallas_call | solution.py:503
  37.6 3.4 %both.2 = (bf16[1024,512]{1,0:T(8,128)(2,1)S(1)}, f32[2,512]{1,0:T(2,128)S(1)}) custom-call(s32[6]{0:T(128)S(1)} %stack.48.meta, bf16[1024,512]{1,0:T(8,128)(2,1)S(1)} %get-tuple-element.79.shifted, bf16[2,2,512,512]{3,2,1,0:T(8,128)(2,1)S(1)} %get-tuple-element.59.blocks), custom_call_target="tpu_custom_call" | custom-call | tf_op jit(solution)/shard_map/both/pallas_call | solution.py:503
  41.0 0.0 collective-permute-done.8.far
  41.0 2.6 %column.3 = (bf16[1024,512]{1,0:T(8,128)(2,1)S(1)}, bf16[1024,512]{1,0:T(8,128)(2,1)S(1)}, f32[2,512]{1,0:T(2,128)S(1)}) custom-call(s32[6]{0:T(128)S(1)} %stack.48.meta, f32[6]{0:T(128)S(1)} %get-tuple-element.60.scalars, bf16[512,512]{1,0:T(8,128)(2,1)S(1)} %get-tuple-element.81.near, bf16[512,512]{1,0:T(8,128)(2,1)S(1)} %collective-permute-done.8.far, ...), custom_call_target="tpu_custom_call" | custom-call | tf_op jit(solution)/shard_map/column/pallas_call | solution.py:503
  43.7 1.6 %collective-permute-start.9 = (f32[4,512]{1,0:T(4,128)S(1)}, f32[4,512]{1,0:T(4,128)S(1)}, u32[]{:S(2)}, u32[]{:S(2)}) collective-permute-start(f32[4,512]{1,0:T(4,128)S(1)} %pad_maximum_fusion.2.edge_x), channel_id=1, source_target_pairs={{0,4},{1,5},{2,6},{3,7},{4,0},{5,1},{6,2},{7,3},{8,12},{9,13},{10,... | collective-permute-start | bytes 24584 | tf_op jit(solution)/shard_map/ppermute | solution.py:514
  45.3 3.2 %both.3 = (bf16[1024,512]{1,0:T(8,128)(2,1)S(1)}, f32[2,512]{1,0:T(2,128)S(1)}) custom-call(s32[6]{0:T(128)S(1)} %stack.48.meta, bf16[1024,512]{1,0:T(8,128)(2,1)S(1)} %get-tuple-element.85.shifted, bf16[2,2,512,512]{3,2,1,0:T(8,128)(2,1)S(1)} %get-tuple-element.59.blocks), custom_call_target="tpu_custom_call" | custom-call | tf_op jit(solution)/shard_map/both/pallas_call | solution.py:503
  48.4 0.0 collective-permute-done.9.near_x
  48.5 0.7 %turn.1 = (f32[4,512]{1,0:T(4,128)S(1)}, f32[4,512]{1,0:T(4,128)S(1)}) custom-call(s32[6]{0:T(128)S(1)} %stack.48.meta, f32[6]{0:T(128)S(1)} %get-tuple-element.60.scalars, f32[4,512]{1,0:T(4,128)S(1)} %pad_maximum_fusion.2.edge_x, f32[4,512]{1,0:T(4,128)S(1)} %collective-permute-done.9.near_x, f32[2,512]{1,0:T(2,128)S(1)} %get-tuple-element.84.edge_y0, ...), custom_call_target="tpu_custom_call" | custom-call | tf_op jit(solution)/shard_map/turn/pallas_call | solution.py:503
  49.2 1.6 %collective-permute-start.10 = (f32[4,512]{1,0:T(4,128)S(1)}, f32[4,512]{1,0:T(4,128)S(1)}, u32[]{:S(2)}, u32[]{:S(2)}) collective-permute-start(f32[4,512]{1,0:T(4,128)S(1)} %get-tuple-element.93.edge), channel_id=1, source_target_pairs={{0,2},{1,3},{2,0},{3,1},{4,6},{5,7},{6,4},{7,5},{8,10},{9,11},{10,... | collective-permute-start | bytes 24584 | tf_op jit(solution)/shard_map/ppermute | solution.py:514
  50.8 1.6 %between.1 = (f32[4,512]{1,0:T(4,128)S(1)}, bf16[4,128,256]{2,1,0:T(8,128)(2,1)S(1)}, bf16[4,128,256]{2,1,0:T(8,128)(2,1)S(1)}) custom-call(s32[6]{0:T(128)S(1)} %stack.48.meta, f32[4,512]{1,0:T(4,128)S(1)} %get-tuple-element.88.whole, bf16[2,2,512,512]{3,2,1,0:T(8,128)(2,1)S(1)} %get-tuple-element.59.blocks, ...), custom_call_target="tpu_custom_call" | custom-call | tf_op jit(solution)/shard_map/between/pallas_call | solution.py:503
  52.4 0.5 collective-permute-done.10.near
  52.9 1.7 %second_image.1 = (bf16[4,128,256]{2,1,0:T(8,128)(2,1)S(1)}, bf16[4,128,256]{2,1,0:T(8,128)(2,1)S(1)}) custom-call(s32[6]{0:T(128)S(1)} %stack.48.meta, f32[6]{0:T(128)S(1)} %get-tuple-element.60.scalars, bf16[1024,512]{1,0:T(8,128)(2,1)S(1)} %get-tuple-element.97.source, bf16[1024,512]{1,0:T(8,128)(2,1)S(1)} %get-tuple-element.98.receiver, ...), custom_call_target="tpu_custom_call" | custom-call | tf_op jit(solution)/shard_map/second_image/pallas_call | solution.py:503
  54.6 0.1 collective-permute-start.12
  54.7 0.5 collective-permute-start.11
  55.2 1.0 %collective-permute-done.12 = bf16[4,128,256]{2,1,0:T(8,128)(2,1)S(1)} collective-permute-done((bf16[4,128,256]{2,1,0:T(8,128)(2,1)S(1)}, bf16[4,128,256]{2,1,0:T(8,128)(2,1)S(1)}, u32[]{:S(2)}, u32[]{:S(2)}) %collective-permute-start.12) | collective-permute-done | bytes 262176 | tf_op jit(solution)/shard_map/ppermute | solution.py:514
  56.2 0.1 fusion.1
  56.3 0.3 collective-permute-done.11
  56.6 0.1 fusion
  56.7 2.5 %collective-permute-start.13 = (bf16[2,128,256]{2,1,0:T(8,128)(2,1)S(1)}, bf16[2,128,256]{2,1,0:T(8,128)(2,1)S(1)}, u32[]{:S(2)}, u32[]{:S(2)}) collective-permute-start(bf16[2,128,256]{2,1,0:T(8,128)(2,1)S(1)} %get-tuple-element.103), channel_id=1, source_target_pairs={{0,8},{1,9},{2,24},{3,25},{4,12},{5,13},{6,28},{7,29},{8,0},{9,1},... | collective-permute-start | bytes 393224 | tf_op jit(solution)/shard_map/ppermute | solution.py:693
  59.2 0.0 collective-permute-start.14
  59.2 1.9 %collective-permute-start.16 = (bf16[2,128,256]{2,1,0:T(8,128)(2,1)S(1)}, bf16[2,128,256]{2,1,0:T(8,128)(2,1)S(1)}, u32[]{:S(2)}, u32[]{:S(2)}) collective-permute-start(bf16[2,128,256]{2,1,0:T(8,128)(2,1)S(1)} %get-tuple-element.105), channel_id=1, source_target_pairs={{0,2},{1,3},{2,18},{3,19},{4,6},{5,7},{6,22},{7,23},{8,10},{9,11},... | collective-permute-start | bytes 393224 | tf_op jit(solution)/shard_map/ppermute | solution.py:693
  61.2 3.4 %collective-permute-start.15 = (bf16[2,128,256]{2,1,0:T(8,128)(2,1)S(1)}, bf16[2,128,256]{2,1,0:T(8,128)(2,1)S(1)}, u32[]{:S(2)}, u32[]{:S(2)}) collective-permute-start(bf16[2,128,256]{2,1,0:T(8,128)(2,1)S(1)} %get-tuple-element.106), channel_id=1, source_target_pairs={{0,0},{1,1},{2,16},{3,17},{4,4},{5,5},{6,20},{7,21},{8,8},{9,9},{1... | collective-permute-start | bytes 393224 | tf_op jit(solution)/shard_map/ppermute | solution.py:693
  64.6 0.0 collective-permute-done.13
  64.6 1.9 %collective-permute-done.14 = bf16[2,128,256]{2,1,0:T(8,128)(2,1)S(1)} collective-permute-done((bf16[2,128,256]{2,1,0:T(8,128)(2,1)S(1)}, bf16[2,128,256]{2,1,0:T(8,128)(2,1)S(1)}, u32[]{:S(2)}, u32[]{:S(2)}) %collective-permute-start.14) | collective-permute-done | bytes 131104 | tf_op jit(solution)/shard_map/ppermute | solution.py:693
  66.5 0.8 %collective-permute-done.16 = bf16[2,128,256]{2,1,0:T(8,128)(2,1)S(1)} collective-permute-done((bf16[2,128,256]{2,1,0:T(8,128)(2,1)S(1)}, bf16[2,128,256]{2,1,0:T(8,128)(2,1)S(1)}, u32[]{:S(2)}, u32[]{:S(2)}) %collective-permute-start.16) | collective-permute-done | bytes 131104 | tf_op jit(solution)/shard_map/ppermute | solution.py:693
  67.3 1.6 %collective-permute-done.15 = bf16[2,128,256]{2,1,0:T(8,128)(2,1)S(1)} collective-permute-done((bf16[2,128,256]{2,1,0:T(8,128)(2,1)S(1)}, bf16[2,128,256]{2,1,0:T(8,128)(2,1)S(1)}, u32[]{:S(2)}, u32[]{:S(2)}) %collective-permute-start.15) | collective-permute-done | bytes 131104 | tf_op jit(solution)/shard_map/ppermute | solution.py:693
  68.9 0.8 %convert_add_fusion = f32[2,128,256]{2,1,0:T(8,128)} fusion(bf16[2,128,256]{2,1,0:T(8,128)(2,1)S(1)} %collective-permute-done.16, bf16[2,128,256]{2,1,0:T(8,128)(2,1)S(1)} %collective-permute-done.15, bf16[2,128,256]{2,1,0:T(8,128)(2,1)S(1)} %collective-permute-done.14, bf16[2,128,256]{2,1,0:T(8,128)(2,1)S(1)} %collective-permute-done.13), kind=kLoop, calls=%fused_computation.13 | loop fusion | flops 458752 | bytes 786432 | tf_op jit(solution)/shard_map/add | solution.py:693
  (12 shorter events, 0.2 us)
Async XLA Ops:
  0.1 1.2 %copy-start.1 = (f32[2,128,1024]{2,1,0:T(8,128)S(1)}, f32[2,128,1024]{2,1,0:T(8,128)}, u32[]{:S(2)}) copy-start(f32[2,128,1024]{2,1,0:T(8,128)} %slowness.1) | copy-start | bytes 3145732
  1.3 1.2 %copy-start.3 = (bf16[1,2,128,2,1024]{4,3,2,1,0:T(2,128)(2,1)S(1)}, bf16[1,2,128,2,1024]{4,3,2,1,0:T(2,128)(2,1)}, u32[]{:S(2)}) copy-start(bf16[1,2,128,2,1024]{4,3,2,1,0:T(2,128)(2,1)} %field.2) | copy-start | bytes 3145732
  2.5 0.7 copy-start.7
  3.2 4.4 %copy-start.2 = (f32[2,128,1024]{2,1,0:T(8,128)S(1)}, f32[2,128,1024]{2,1,0:T(8,128)}, u32[]{:S(2)}) copy-start(f32[2,128,1024]{2,1,0:T(8,128)} %slowness.1) | copy-start | bytes 3145732
  3.2 4.5 %copy-start.5 = (f32[2,2]{1,0:T(2,128)S(1)}, f32[2,2]{1,0:T(2,128)}, u32[]{:S(2)}) copy-start(f32[2,2]{1,0:T(2,128)} %coupling.1) | copy-start | bytes 52
  5.4 2.3 %collective-permute-start = (bf16[256,1024]{1,0:T(8,128)(2,1)S(1)}, bf16[256,1024]{1,0:T(8,128)(2,1)S(1)}, u32[]{:S(2)}, u32[]{:S(2)}) collective-permute-start(bf16[256,1024]{1,0:T(8,128)(2,1)S(1)} %get-tuple-element.58), channel_id=1, source_target_pairs={{0,1},{1,0},{2,3},{3,2},{4,5},{5,4},{6,7},{7,6},{8,9},{9,8},{10,11... | collective-permute-start | bytes 1572872 | tf_op jit(solution)/shard_map/ppermute | solution.py:514
  5.4 4.6 %copy-start = (bf16[1,2,128,2,1024]{4,3,2,1,0:T(2,128)(2,1)S(1)}, bf16[1,2,128,2,1024]{4,3,2,1,0:T(2,128)(2,1)}, u32[]{:S(2)}) copy-start(bf16[1,2,128,2,1024]{4,3,2,1,0:T(2,128)(2,1)} %field.3) | copy-start | bytes 3145732
  7.6 5.9 %copy-start.4 = (s32[1,1024]{1,0:T(1,128)S(1)}, s32[1,1024]{1,0:T(1,128)}, u32[]{:S(2)}) copy-start(s32[1,1024]{1,0:T(1,128)} %mask.1) | copy-start | bytes 12292
  10.7 2.9 %collective-permute-start.1 = (bf16[128,2,1024]{2,1,0:T(2,128)(2,1)S(1)}, bf16[128,2,1024]{2,1,0:T(2,128)(2,1)S(1)}, u32[]{:S(2)}, u32[]{:S(2)}) collective-permute-start(bf16[128,2,1024]{2,1,0:T(2,128)(2,1)S(1)} %away.1), channel_id=1, source_target_pairs={{0,1},{1,0},{2,3},{3,2},{4,5},{5,4},{6,7},{7,6},{8,9},{9,8},{10,11... | collective-permute-start | bytes 1572872 | tf_op jit(solution)/shard_map/ppermute | solution.py:514
  11.2 2.3 %collective-permute-start.2 = (f32[128,1024]{1,0:T(8,128)S(1)}, f32[128,1024]{1,0:T(8,128)S(1)}, u32[]{:S(2)}, u32[]{:S(2)}) collective-permute-start(f32[128,1024]{1,0:T(8,128)S(1)} %get-tuple-element.65.slow), channel_id=1, source_target_pairs={{0,1},{1,0},{2,3},{3,2},{4,5},{5,4},{6,7},{7,6},{8,9},{9,8},{10,11... | collective-permute-start | bytes 1572872 | tf_op jit(solution)/shard_map/ppermute | solution.py:514
  11.3 14.9 %collective-permute-start.3 = (bf16[512,512]{1,0:T(8,128)(2,1)S(1)}, bf16[512,512]{1,0:T(8,128)(2,1)S(1)}, u32[]{:S(2)}, u32[]{:S(2)}) collective-permute-start(bf16[512,512]{1,0:T(8,128)(2,1)S(1)} %get-tuple-element.66.cross0), channel_id=1, source_target_pairs={{0,2},{1,3},{2,0},{3,1},{4,6},{5,7},{6,4},{7,5},{8,10},{9,11},{10,... | collective-permute-start | bytes 1572872 | tf_op jit(solution)/shard_map/ppermute | solution.py:514
  12.9 20.0 %copy-start.6 = (s32[1,2]{1,0:T(1,128)S(1)}, s32[1,2]{1,0:T(1,128)}, u32[]{:S(2)}) copy-start(s32[1,2]{1,0:T(1,128)} %place.1) | copy-start | bytes 28
  13.0 16.0 %collective-permute-start.4 = (f16[128,512]{1,0:T(8,128)(2,1)S(1)}, f16[128,512]{1,0:T(8,128)(2,1)S(1)}, u32[]{:S(2)}, u32[]{:S(2)}) collective-permute-start(f16[128,512]{1,0:T(8,128)(2,1)S(1)} %get-tuple-element.110), channel_id=1, source_target_pairs={{0,2},{1,3},{2,0},{3,1},{4,6},{5,7},{6,4},{7,5},{8,10},{9,11},{10,... | collective-permute-start | bytes 393224 | tf_op jit(solution)/shard_map/ppermute | solution.py:514
  18.3 10.7 %collective-permute-start.5 = (f32[4,512]{1,0:T(4,128)S(1)}, f32[4,512]{1,0:T(4,128)S(1)}, u32[]{:S(2)}, u32[]{:S(2)}) collective-permute-start(f32[4,512]{1,0:T(4,128)S(1)} %get-tuple-element.70), channel_id=1, source_target_pairs={{0,4},{1,5},{2,6},{3,7},{4,0},{5,1},{6,2},{7,3},{8,12},{9,13},{10,... | collective-permute-start | bytes 24584 | tf_op jit(solution)/shard_map/ppermute | solution.py:514
  20.9 10.3 %collective-permute-start.6 = (f32[4,512]{1,0:T(4,128)S(1)}, f32[4,512]{1,0:T(4,128)S(1)}, u32[]{:S(2)}, u32[]{:S(2)}) collective-permute-start(f32[4,512]{1,0:T(4,128)S(1)} %get-tuple-element.71), channel_id=1, source_target_pairs={{0,6},{1,7},{2,4},{3,5},{4,2},{5,3},{6,0},{7,1},{8,14},{9,15},{10,... | collective-permute-start | bytes 24584 | tf_op jit(solution)/shard_map/ppermute | solution.py:514
  26.2 14.8 %collective-permute-start.8 = (bf16[512,512]{1,0:T(8,128)(2,1)S(1)}, bf16[512,512]{1,0:T(8,128)(2,1)S(1)}, u32[]{:S(2)}, u32[]{:S(2)}) collective-permute-start(bf16[512,512]{1,0:T(8,128)(2,1)S(1)} %get-tuple-element.82), channel_id=1, source_target_pairs={{0,2},{1,3},{2,0},{3,1},{4,6},{5,7},{6,4},{7,5},{8,10},{9,11},{10,... | collective-permute-start | bytes 1572872 | tf_op jit(solution)/shard_map/ppermute | solution.py:514
  31.3 1.6 %collective-permute-start.7 = (f16[2,128,512]{2,1,0:T(8,128)(2,1)S(1)}, f16[2,128,512]{2,1,0:T(8,128)(2,1)S(1)}, u32[]{:S(2)}, u32[]{:S(2)}) collective-permute-start(f16[2,128,512]{2,1,0:T(8,128)(2,1)S(1)} %pad_maximum_fusion), channel_id=1, source_target_pairs={{0,1},{1,0},{2,3},{3,2},{4,5},{5,4},{6,7},{7,6},{8,9},{9,8},{10,11... | collective-permute-start | bytes 786440 | tf_op jit(solution)/shard_map/ppermute | solution.py:514
  43.7 4.8 %collective-permute-start.9 = (f32[4,512]{1,0:T(4,128)S(1)}, f32[4,512]{1,0:T(4,128)S(1)}, u32[]{:S(2)}, u32[]{:S(2)}) collective-permute-start(f32[4,512]{1,0:T(4,128)S(1)} %pad_maximum_fusion.2.edge_x), channel_id=1, source_target_pairs={{0,4},{1,5},{2,6},{3,7},{4,0},{5,1},{6,2},{7,3},{8,12},{9,13},{10,... | collective-permute-start | bytes 24584 | tf_op jit(solution)/shard_map/ppermute | solution.py:514
  49.2 3.7 %collective-permute-start.10 = (f32[4,512]{1,0:T(4,128)S(1)}, f32[4,512]{1,0:T(4,128)S(1)}, u32[]{:S(2)}, u32[]{:S(2)}) collective-permute-start(f32[4,512]{1,0:T(4,128)S(1)} %get-tuple-element.93.edge), channel_id=1, source_target_pairs={{0,2},{1,3},{2,0},{3,1},{4,6},{5,7},{6,4},{7,5},{8,10},{9,11},{10,... | collective-permute-start | bytes 24584 | tf_op jit(solution)/shard_map/ppermute | solution.py:514
  54.6 1.6 %collective-permute-start.12 = (bf16[4,128,256]{2,1,0:T(8,128)(2,1)S(1)}, bf16[4,128,256]{2,1,0:T(8,128)(2,1)S(1)}, u32[]{:S(2)}, u32[]{:S(2)}) collective-permute-start(bf16[4,128,256]{2,1,0:T(8,128)(2,1)S(1)} %get-tuple-element.102), channel_id=1, source_target_pairs={{0,1},{1,0},{2,3},{3,2},{4,5},{5,4},{6,7},{7,6},{8,9},{9,8},{10,11... | collective-permute-start | bytes 786440 | tf_op jit(solution)/shard_map/ppermute | solution.py:514
  54.7 1.9 %collective-permute-start.11 = (bf16[4,128,256]{2,1,0:T(8,128)(2,1)S(1)}, bf16[4,128,256]{2,1,0:T(8,128)(2,1)S(1)}, u32[]{:S(2)}, u32[]{:S(2)}) collective-permute-start(bf16[4,128,256]{2,1,0:T(8,128)(2,1)S(1)} %get-tuple-element.96), channel_id=1, source_target_pairs={{0,1},{1,0},{2,3},{3,2},{4,5},{5,4},{6,7},{7,6},{8,9},{9,8},{10,11... | collective-permute-start | bytes 786440 | tf_op jit(solution)/shard_map/ppermute | solution.py:514
  56.7 7.9 %collective-permute-start.13 = (bf16[2,128,256]{2,1,0:T(8,128)(2,1)S(1)}, bf16[2,128,256]{2,1,0:T(8,128)(2,1)S(1)}, u32[]{:S(2)}, u32[]{:S(2)}) collective-permute-start(bf16[2,128,256]{2,1,0:T(8,128)(2,1)S(1)} %get-tuple-element.103), channel_id=1, source_target_pairs={{0,8},{1,9},{2,24},{3,25},{4,12},{5,13},{6,28},{7,29},{8,0},{9,1},... | collective-permute-start | bytes 393224 | tf_op jit(solution)/shard_map/ppermute | solution.py:693
  59.2 7.3 %collective-permute-start.14 = (bf16[2,128,256]{2,1,0:T(8,128)(2,1)S(1)}, bf16[2,128,256]{2,1,0:T(8,128)(2,1)S(1)}, u32[]{:S(2)}, u32[]{:S(2)}) collective-permute-start(bf16[2,128,256]{2,1,0:T(8,128)(2,1)S(1)} %get-tuple-element.104), channel_id=1, source_target_pairs={{0,10},{1,11},{2,26},{3,27},{4,14},{5,15},{6,30},{7,31},{8,2},{9,3... | collective-permute-start | bytes 393224 | tf_op jit(solution)/shard_map/ppermute | solution.py:693
  59.2 8.1 %collective-permute-start.16 = (bf16[2,128,256]{2,1,0:T(8,128)(2,1)S(1)}, bf16[2,128,256]{2,1,0:T(8,128)(2,1)S(1)}, u32[]{:S(2)}, u32[]{:S(2)}) collective-permute-start(bf16[2,128,256]{2,1,0:T(8,128)(2,1)S(1)} %get-tuple-element.105), channel_id=1, source_target_pairs={{0,2},{1,3},{2,18},{3,19},{4,6},{5,7},{6,22},{7,23},{8,10},{9,11},... | collective-permute-start | bytes 393224 | tf_op jit(solution)/shard_map/ppermute | solution.py:693
  61.2 7.7 %collective-permute-start.15 = (bf16[2,128,256]{2,1,0:T(8,128)(2,1)S(1)}, bf16[2,128,256]{2,1,0:T(8,128)(2,1)S(1)}, u32[]{:S(2)}, u32[]{:S(2)}) collective-permute-start(bf16[2,128,256]{2,1,0:T(8,128)(2,1)S(1)} %get-tuple-element.106), channel_id=1, source_target_pairs={{0,0},{1,1},{2,16},{3,17},{4,4},{5,5},{6,20},{7,21},{8,8},{9,9},{1... | collective-permute-start | bytes 393224 | tf_op jit(solution)/shard_map/ppermute | solution.py:693
